TPU v7x, 128 devices: a whole 4x4x4 slice. The times are simulated.
128 devices in a mesh: parts: 128 (over z, y, x, core).
Axes of the slice: x: 4, y: 4, z: 4, core: 2. Of those that a mesh axis runs over, the one named last changes fastest.
Arguments:
- start_vectors: float32 [2097152, 16], P('parts'), may hold values from -120 to 120
- tile_index: int32 [32768, 2], P('parts'), may hold values from 0 to 255, as said below
- tile_values: bfloat16 [32768, 128, 128], P('parts'), may hold values from 0 to 1
- tile_count: int32 [128], P('parts'), may hold values from 128 to 256, as said below
- ghost_send: int32 [128, 2, 64], P('parts'), may hold values from 0 to 127, as said below
Outputs:
- basis_out: float32 [2097152, 80], P('parts')
- gram_matrix: float32 [80, 80], replicated
Inputs may be any that keep to these rules, and one draw needn't show every extreme that they name: `tile_index`: column 0 is a row block of the part, column 1 a block of its extended region; among a part's first 128 slots every one of the 128 ghost blocks is named exactly once and the other slots name own blocks. `tile_count`: slots at or beyond a part's count are dead; some part uses all 256 slots. `ghost_send`: each list holds distinct own block indices.
All inputs are finite; a program needn't handle non-finite values.
Results may differ from a plain program's by a relative error of at most 0.0058.
Values may be sent and summed in bfloat16 or wider, within the bound.
No kernel may reach another device: no remote copies, remote signals or barrier semaphores. Data moves between devices by JAX's collectives and lax.ppermute only.
A program may use at most 128 MiB of HBM per device.

v0:
```python
import functools

import jax
import jax.numpy as jnp
from jax import lax
from jax.experimental import pallas as pl
from jax.experimental.pallas import tpu as pltpu
from jax.sharding import PartitionSpec as P

STEPS = 4
AXIS = "parts"
VMEM = pltpu.VMEM
SMEM = pltpu.SMEM
F32 = jnp.float32
BF16 = jnp.bfloat16

SLOT, GROW, OCOL, OROW, SEND = range(5)


def spec(space):
    return pl.BlockSpec(memory_space=space)


def tile_product(block, tile):
    return lax.dot_general(block, tile, (((1,), (1,)), ((), ())), preferred_element_type=F32)


def pack(plan_ref, scaled_ref, send_a_ref, send_b_ref):
    half = send_a_ref.shape[0]

    def step(base, _):
        for u in range(8):
            g = base * 8 + u
            send_b_ref[g] = scaled_ref[plan_ref[SEND, half + g]]
        for u in range(8):
            g = base * 8 + u
            send_a_ref[g] = scaled_ref[plan_ref[SEND, g]]
        return 0

    lax.fori_loop(0, half // 8, step, 0)


def setup_kernel(index_ref, count_ref, ghost_ref, values_ref, start_ref,
                 tiles_ref, plan_ref, scale_ref, scaled_ref, send_a_ref, send_b_ref,
                 acc_ref, sems):
    total, side = values_ref.shape[0], values_ref.shape[1]
    blocks = scaled_ref.shape[0]
    half = send_a_ref.shape[0]
    ghosts = 2 * half
    chunks = sems.shape[0]
    per = total // chunks

    def copy(k):
        return pltpu.make_async_copy(
            values_ref.at[pl.ds(k * per, per)], tiles_ref.at[pl.ds(k * per, per)], sems.at[k]
        )

    for k in range(chunks):
        copy(k).start()

    odd = lax.rem(lax.axis_index(AXIS), 2)
    flip = (1 - odd) * half
    count = count_ref[0]
    acc_ref[...] = jnp.zeros_like(acc_ref)

    def ghost_plan(base, _):
        for u in range(4):
            t = base * 4 + u
            place = jnp.bitwise_xor(index_ref[1, t] - blocks, flip)
            plan_ref[SLOT, place] = t
            plan_ref[GROW, place] = index_ref[0, t]
            plan_ref[OCOL, t] = index_ref[1, ghosts + t]
            plan_ref[OROW, t] = jnp.where(ghosts + t < count, index_ref[0, ghosts + t], blocks)
        return 0

    lax.fori_loop(0, ghosts // 4, ghost_plan, 0)

    def send_plan(g, _):
        plan_ref[SEND, g] = ghost_ref[odd, g]
        plan_ref[SEND, half + g] = ghost_ref[1 - odd, g]
        return 0

    lax.fori_loop(0, half, send_plan, 0)

    ones = jnp.ones((16, side), BF16)
    for k in range(chunks):
        copy(k).wait()

        def degree_step(base, _):
            for u in range(8):
                t = k * per + base * 8 + u
                row = jnp.where(t < count, index_ref[0, t], blocks)
                acc_ref[row] += tile_product(ones, tiles_ref[t])
            return 0

        lax.fori_loop(0, per // 8, degree_step, 0)

    def scale_step(base, _):
        for u in range(8):
            b = base * 8 + u
            factor = 1.0 / jnp.sqrt(1.0 + acc_ref[b])
            scale_ref[b] = factor
            at = pl.ds(pl.multiple_of(b * side, side), side)
            scaled_ref[b] = (factor * start_ref[:, at]).astype(BF16)
        return 0

    lax.fori_loop(0, blocks // 8, scale_step, 0)
    pack(plan_ref, scaled_ref, send_a_ref, send_b_ref)


def split(value):
    high = value.astype(BF16)
    return high, (value - high.astype(F32)).astype(BF16)


def gram_rows(parts, gram_ref, level):
    rows = parts[0].shape[1]
    chunk = 1024
    width = 16 * (level + 1)
    acc = jnp.zeros((32, 2 * width), F32)
    for k in range(rows // chunk):
        at = slice(k * chunk, (k + 1) * chunk)
        right = jnp.concatenate([p[:16, at] for p in parts] + [p[16:, at] for p in parts], 0)
        acc += lax.dot_general(parts[-1][:, at], right, (((1,), (1,)), ((), ())), preferred_element_type=F32)
    both = acc[:16] + acc[16:]
    gram_ref[16 * level:16 * (level + 1), :width] = both[:, :width] + both[:, width:]


def own_kernel(level, *refs):
    plan_ref, tiles_ref, scaled_ref, got_ref, vec_ref = refs[:5]
    older = refs[5:5 + level]
    at = 5 + level
    gram_in = None
    if level:
        gram_in = refs[at]
        at += 1
    acc_ref, part_ref, gram_ref = refs[at:at + 3]
    half = got_ref.shape[0]
    acc_ref[...] = jnp.zeros_like(acc_ref)
    ghosts = 2 * half

    def own_step(base, _):
        for u in range(8):
            t = base * 8 + u
            acc_ref[plan_ref[OROW, t]] += tile_product(
                scaled_ref[plan_ref[OCOL, t]], tiles_ref[ghosts + t])
        return 0

    lax.fori_loop(0, ghosts // 8, own_step, 0)

    def near_step(base, _):
        for u in range(8):
            g = base * 8 + u
            acc_ref[plan_ref[GROW, g]] += tile_product(got_ref[g], tiles_ref[plan_ref[SLOT, g]])
        return 0

    lax.fori_loop(0, half // 8, near_step, 0)

    high, low = split(vec_ref[...])
    part_ref[:16] = high
    part_ref[16:] = low
    gram_ref[...] = gram_in[...] if level else jnp.zeros_like(gram_ref)
    gram_rows(tuple(older) + (part_ref,), gram_ref, level)


def far_kernel(level, last, *refs):
    plan_ref, tiles_ref, got_ref, acc_in, scale_ref = refs[:5]
    at = 5
    prev_ref = None
    if level > 1:
        prev_ref = refs[at]
        at += 1
    if last:
        older = refs[at:at + level]
        gram_in = refs[at + level]
        at += level + 1
        part_ref, gram_ref, acc_ref = refs[at:at + 3]
    else:
        vec_ref, scaled_ref, send_a_ref, send_b_ref, acc_ref = refs[at:at + 5]
    half = got_ref.shape[0]
    side = tiles_ref.shape[1]
    blocks = scale_ref.shape[0]
    acc_ref[...] = acc_in[...]

    def far_step(base, _):
        for u in range(8):
            g = base * 8 + u
            acc_ref[plan_ref[GROW, half + g]] += tile_product(
                got_ref[g], tiles_ref[plan_ref[SLOT, half + g]])
        return 0

    lax.fori_loop(0, half // 8, far_step, 0)

    def close_step(base, _):
        for u in range(8):
            b = base * 8 + u
            where = pl.ds(pl.multiple_of(b * side, side), side)
            factor = scale_ref[b]
            value = factor * acc_ref[b]
            if level > 1:
                value = 2.0 * value - prev_ref[:, where]
            if last:
                high, low = split(value)
                part_ref[:16, where] = high
                part_ref[16:, where] = low
            else:
                vec_ref[:, where] = value
                scaled_ref[b] = (factor * value).astype(BF16)
        return 0

    lax.fori_loop(0, blocks // 8, close_step, 0)
    if last:
        gram_ref[...] = gram_in[...]
        gram_rows(tuple(older) + (part_ref,), gram_ref, level)
    else:
        pack(plan_ref, scaled_ref, send_a_ref, send_b_ref)


def inverse_factor(gram):
    size = gram.shape[0]
    row = lax.broadcasted_iota(jnp.int32, gram.shape, 0)
    lane = lax.broadcasted_iota(jnp.int32, gram.shape, 1)
    left, right = gram, jnp.where(row == lane, 1.0, 0.0)
    row8 = lax.broadcasted_iota(jnp.int32, (8, 128), 0)
    done = []
    for base in range(0, size, 8):
        a, b = left[:8], right[:8]
        for j in range(8):
            at = base + j
            scale = lax.rsqrt(a[j:j + 1, at:at + 1])
            line_a, line_b = a[j:j + 1] * scale, b[j:j + 1] * scale
            column = jnp.where(row8 > j, a[:, at:at + 1] * scale, 0.0)
            a = jnp.where(row8 == j, line_a, a - column * line_a)
            b = jnp.where(row8 == j, line_b, b - column * line_b)
        done.append(b)
        if base + 8 < size:
            both = jnp.concatenate([a, b], 1)
            change = lax.dot_general(
                a.T[base + 8:size], both, (((1,), (0,)), ((), ())),
                precision=lax.Precision.HIGHEST, preferred_element_type=F32)
            left = left[8:] - change[:, :128]
            right = right[8:] - change[:, 128:]
    return jnp.concatenate(done, 0)


def final_kernel(row_total, gram_in, *refs):
    parts = refs[:STEPS + 1]
    basis_ref, gram_ref, mix_ref = refs[STEPS + 1:]
    width = gram_ref.shape[0]
    chunk = basis_ref.shape[1]

    @pl.when(pl.program_id(0) == 0)
    def _():
        lower = gram_in[...] * (1.0 / row_total)
        row = lax.broadcasted_iota(jnp.int32, lower.shape, 0)
        lane = lax.broadcasted_iota(jnp.int32, lower.shape, 1)
        lower = jnp.where(row >= lane, lower, 0.0)
        strict = jnp.where(row > lane, lower, 0.0)
        square = jnp.concatenate([strict, jnp.zeros((128 - width, 128), F32)], 0)
        full = lower + square.T[:width]
        gram_ref[...] = full[:, :width]
        inverse = inverse_factor(full)
        high, low = split(inverse[:, :width])
        mix_ref[...] = jnp.concatenate([high, low, high], 1)

    at = pl.ds(pl.multiple_of(pl.program_id(0) * chunk, chunk), chunk)
    tops = [p[:16, at] for p in parts]
    lows = [p[16:, at] for p in parts]
    stack = jnp.concatenate(tops + tops + lows, 0)
    basis_ref[...] = jnp.dot(mix_ref[...], stack, preferred_element_type=F32)


def params(mib, **kw):
    return pltpu.CompilerParams(vmem_limit_bytes=mib * 2**20, **kw)


def body(start_vectors, tile_index, tile_values, tile_count, ghost_send):
    rows, width = start_vectors.shape
    total, side, _ = tile_values.shape
    blocks = rows // side
    half = ghost_send.shape[2]
    n = lax.axis_size(AXIS)
    basis = width * (STEPS + 1)
    shape = jax.ShapeDtypeStruct

    scaled_t = shape((blocks, width, side), BF16)
    send_t = shape((half, width, side), BF16)
    vec_t = shape((width, rows), F32)
    part_t = shape((2 * width, rows), BF16)
    acc_t = shape((blocks + 1, width, side), F32)
    gram_t = shape((basis, 128), F32)

    near = [(i, i ^ 1) for i in range(n)]
    far = [(i, (i + 1) % n if i % 2 else (i - 1) % n) for i in range(n)]

    start = start_vectors.T
    tiles, plan, scale, scaled, send_a, send_b = pl.pallas_call(
        setup_kernel,
        out_shape=(shape((total, side, side), BF16), shape((8, 128), jnp.int32),
                   shape((blocks, width, side), F32), scaled_t, send_t, send_t),
        in_specs=[spec(SMEM), spec(SMEM), spec(SMEM), spec(pltpu.HBM), spec(VMEM)],
        out_specs=(spec(VMEM), spec(SMEM), spec(VMEM), spec(VMEM), spec(VMEM), spec(VMEM)),
        scratch_shapes=[VMEM(acc_t.shape, F32), pltpu.SemaphoreType.DMA((16,))],
        compiler_params=params(20),
        name="setup",
    )(tile_index.T, tile_count, ghost_send[0], tile_values, start)

    vectors = [start]
    parts = []
    gram = None
    for level in range(1, STEPS + 1):
        last = level == STEPS
        got_b = lax.ppermute(send_b, AXIS, far)
        got_a = lax.ppermute(send_a, AXIS, near)
        args = [plan, tiles, scaled, got_a, vectors[-1]] + parts + ([gram] if gram is not None else [])
        acc, part, gram = pl.pallas_call(
            functools.partial(own_kernel, level - 1),
            out_shape=(acc_t, part_t, gram_t),
            in_specs=[spec(SMEM)] + [spec(VMEM)] * (len(args) - 1),
            out_specs=(spec(VMEM),) * 3,
            compiler_params=params(20),
            cost_estimate=pl.CostEstimate(flops=10**9, bytes_accessed=10**7, transcendentals=0),
            name="own",
        )(*args)
        parts.append(part)
        args = [plan, tiles, got_b, acc, scale]
        if level > 1:
            args.append(vectors[-2])
        if last:
            args += parts + [gram]
            outs = (part_t, gram_t)
        else:
            outs = (vec_t, scaled_t, send_t, send_t)
        got = pl.pallas_call(
            functools.partial(far_kernel, level, last),
            out_shape=outs,
            in_specs=[spec(SMEM)] + [spec(VMEM)] * (len(args) - 1),
            out_specs=(spec(VMEM),) * len(outs),
            scratch_shapes=[VMEM(acc_t.shape, F32)],
            compiler_params=params(20),
            name="far",
        )(*args)
        if last:
            part, gram = got
            parts.append(part)
        else:
            vec, scaled, send_a, send_b = got
            vectors.append(vec)

    def phase(value, shift, count):
        mask = (count - 1) << shift
        moved = value
        for d in range(1, count):
            perm = [(i, (i & ~mask) | ((((i >> shift) + d) & (count - 1)) << shift)) for i in range(n)]
            moved = moved + lax.ppermute(value, AXIS, perm)
        return moved

    for shift, count in ((0, 2), (1, 4), (3, 4), (5, 4)):
        gram = phase(gram, shift, count)

    chunk = 1024
    basis_out, gram_matrix = pl.pallas_call(
        functools.partial(final_kernel, rows * n),
        grid=(rows // chunk,),
        out_shape=(shape((basis, rows), F32), shape((basis, basis), F32)),
        in_specs=[spec(VMEM)] * (STEPS + 2),
        out_specs=(pl.BlockSpec((basis, chunk), lambda i: (0, i)),
                   pl.BlockSpec((basis, basis), lambda i: (0, 0))),
        scratch_shapes=[VMEM((basis, 3 * basis), BF16)],
        compiler_params=params(20),
        name="final",
    )(gram, *parts)
    return basis_out.T, gram_matrix


def solution(mesh):
    placed = (
        P("parts", None),
        P("parts", None),
        P("parts", None, None),
        P("parts"),
        P("parts", None, None),
    )
    return jax.shard_map(
        body, mesh=mesh, in_specs=placed, out_specs=(P("parts", None), P()), check_vma=False
    )
```

profile of v0, /device:TPU:0, one launch (start us, length us, event | category | flops | bytes accessed | tf_op | source)
XLA Modules:
  0.0 127.0 jit_solution(18172682087320953718)
XLA Ops:
  1.3 0.0 copy-start
  1.3 1.2 copy-done
  2.5 0.0 copy-start.2
  2.5 3.4 %copy-done.2 = bf16[256,128,128]{2,1,0:T(8,128)(2,1)S(1)} copy-done((bf16[256,128,128]{2,1,0:T(8,128)(2,1)S(1)}, bf16[256,128,128]{2,1,0:T(8,128)(2,1)}, u32[]{:S(2)}) %copy-start.2) | copy-done | bytes 8388632
  5.9 0.0 copy-start.3
  5.9 0.7 copy-done.3
  6.6 0.0 copy-start.4
  6.6 0.7 copy-done.4
  7.2 0.0 copy-start.1
  7.2 13.3 %setup.1 = (bf16[256,128,128]{2,1,0:T(8,128)(2,1)S(1)}, s32[8,128]{1,0:T(8,128)S(1)}, f32[128,16,128]{2,1,0:T(8,128)S(1)}, bf16[128,16,128]{2,1,0:T(8,128)(2,1)S...) custom-call(s32[2,256]{1,0:T(2,128)S(1)} %bitcast.7, s32[1]{0:T(128)S(6)} %copy.7.count_ref, ...), custom_call_target="tpu_custom_call" | custom-call | tf_op jit(solution)/shard_map/setup/pallas_call | solution.py:297
  20.5 0.1 collective-permute-start.1
  20.6 8.8 %collective-permute-start = (bf16[64,16,128]{2,1,0:T(8,128)(2,1)S(1)}, bf16[64,16,128]{2,1,0:T(8,128)(2,1)S(1)}, u32[]{:S(2)}, u32[]{:S(2)}) collective-permute-start(bf16[64,16,128]{2,1,0:T(8,128)(2,1)S(1)} %get-tuple-element.38), channel_id=1, source_target_pairs={{0,127},{1,2},{2,1},{3,4},{4,3},{5,6},{6,5},{7,8},{8,7},{9,10},{10... | collective-permute-start | bytes 786440 | tf_op jit(solution)/shard_map/ppermute | solution.py:313
  29.5 0.0 collective-permute-done.1.refs_3_
  29.5 0.0 copy-done.1
  29.5 7.5 %own.4 = (f32[129,16,128]{2,1,0:T(8,128)S(1)}, bf16[32,16384]{1,0:T(8,128)(2,1)S(1)}, f32[80,128]{1,0:T(8,128)S(1)}) custom-call(s32[8,128]{1,0:T(8,128)S(1)} %get-tuple-element.36.refs_0_, bf16[256,128,128]{2,1,0:T(8,128)(2,1)S(1)} %get-tuple-element.37.refs_1_, bf16[128,16,128]{2,1,0:T(8,128)(2,1)S(1)} %get-tuple-element.39.refs_2_, ...), custom_call_target="tpu_custom_call" | custom-call | flops 1000000000 | bytes 10000000 | tf_op jit(solution)/shard_map/own/pallas_call | solution.py:316
  37.0 0.0 collective-permute-done.refs_2_
  37.0 3.3 %far.4 = (f32[16,16384]{1,0:T(8,128)S(1)}, bf16[128,16,128]{2,1,0:T(8,128)(2,1)S(1)}, bf16[64,16,128]{2,1,0:T(8,128)(2,1)S(1)}, bf16[64,16,128]{2,1,0:T(8,128)(2,1)S(1)}) custom-call(s32[8,128]{1,0:T(8,128)S(1)} %get-tuple-element.36.refs_0_, bf16[256,128,128]{2,1,0:T(8,128)(2,1)S(1)} %get-tuple-element.37.refs_1_, ...), custom_call_target="tpu_custom_call" | custom-call | tf_op jit(solution)/shard_map/far/pallas_call | solution.py:334
  40.3 0.1 collective-permute-start.3
  40.4 3.8 %collective-permute-start.2 = (bf16[64,16,128]{2,1,0:T(8,128)(2,1)S(1)}, bf16[64,16,128]{2,1,0:T(8,128)(2,1)S(1)}, u32[]{:S(2)}, u32[]{:S(2)}) collective-permute-start(bf16[64,16,128]{2,1,0:T(8,128)(2,1)S(1)} %get-tuple-element.43), channel_id=1, source_target_pairs={{0,127},{1,2},{2,1},{3,4},{4,3},{5,6},{6,5},{7,8},{8,7},{9,10},{10... | collective-permute-start | bytes 786440 | tf_op jit(solution)/shard_map/ppermute | solution.py:313
  44.2 0.0 collective-permute-done.3.refs_3_
  44.2 7.6 %own.5 = (f32[129,16,128]{2,1,0:T(8,128)S(1)}, bf16[32,16384]{1,0:T(8,128)(2,1)S(1)}, f32[80,128]{1,0:T(8,128)S(1)}) custom-call(s32[8,128]{1,0:T(8,128)S(1)} %get-tuple-element.36.refs_0_, bf16[256,128,128]{2,1,0:T(8,128)(2,1)S(1)} %get-tuple-element.37.refs_1_, bf16[128,16,128]{2,1,0:T(8,128)(2,1)S(1)} %get-tuple-element.44.refs_2_, ...), custom_call_target="tpu_custom_call" | custom-call | flops 1000000000 | bytes 10000000 | tf_op jit(solution)/shard_map/own/pallas_call | solution.py:316
  51.7 0.0 collective-permute-done.2.refs_2_
  51.7 3.4 %far.5 = (f32[16,16384]{1,0:T(8,128)S(1)}, bf16[128,16,128]{2,1,0:T(8,128)(2,1)S(1)}, bf16[64,16,128]{2,1,0:T(8,128)(2,1)S(1)}, bf16[64,16,128]{2,1,0:T(8,128)(2,1)S(1)}) custom-call(s32[8,128]{1,0:T(8,128)S(1)} %get-tuple-element.36.refs_0_, bf16[256,128,128]{2,1,0:T(8,128)(2,1)S(1)} %get-tuple-element.37.refs_1_, ...), custom_call_target="tpu_custom_call" | custom-call | tf_op jit(solution)/shard_map/far/pallas_call | solution.py:334
  55.1 0.1 collective-permute-start.5
  55.2 3.7 %collective-permute-start.4 = (bf16[64,16,128]{2,1,0:T(8,128)(2,1)S(1)}, bf16[64,16,128]{2,1,0:T(8,128)(2,1)S(1)}, u32[]{:S(2)}, u32[]{:S(2)}) collective-permute-start(bf16[64,16,128]{2,1,0:T(8,128)(2,1)S(1)} %get-tuple-element.50), channel_id=1, source_target_pairs={{0,127},{1,2},{2,1},{3,4},{4,3},{5,6},{6,5},{7,8},{8,7},{9,10},{10... | collective-permute-start | bytes 786440 | tf_op jit(solution)/shard_map/ppermute | solution.py:313
  58.9 0.0 collective-permute-done.5.refs_3_
  58.9 8.1 %own.6 = (f32[129,16,128]{2,1,0:T(8,128)S(1)}, bf16[32,16384]{1,0:T(8,128)(2,1)S(1)}, f32[80,128]{1,0:T(8,128)S(1)}) custom-call(s32[8,128]{1,0:T(8,128)S(1)} %get-tuple-element.36.refs_0_, bf16[256,128,128]{2,1,0:T(8,128)(2,1)S(1)} %get-tuple-element.37.refs_1_, bf16[128,16,128]{2,1,0:T(8,128)(2,1)S(1)} %get-tuple-element.51.refs_2_, ...), custom_call_target="tpu_custom_call" | custom-call | flops 1000000000 | bytes 10000000 | tf_op jit(solution)/shard_map/own/pallas_call | solution.py:316
  67.0 0.0 collective-permute-done.4.refs_2_
  67.0 3.4 %far.6 = (f32[16,16384]{1,0:T(8,128)S(1)}, bf16[128,16,128]{2,1,0:T(8,128)(2,1)S(1)}, bf16[64,16,128]{2,1,0:T(8,128)(2,1)S(1)}, bf16[64,16,128]{2,1,0:T(8,128)(2,1)S(1)}) custom-call(s32[8,128]{1,0:T(8,128)S(1)} %get-tuple-element.36.refs_0_, bf16[256,128,128]{2,1,0:T(8,128)(2,1)S(1)} %get-tuple-element.37.refs_1_, ...), custom_call_target="tpu_custom_call" | custom-call | tf_op jit(solution)/shard_map/far/pallas_call | solution.py:334
  70.4 0.1 collective-permute-start.7
  70.5 3.6 %collective-permute-start.6 = (bf16[64,16,128]{2,1,0:T(8,128)(2,1)S(1)}, bf16[64,16,128]{2,1,0:T(8,128)(2,1)S(1)}, u32[]{:S(2)}, u32[]{:S(2)}) collective-permute-start(bf16[64,16,128]{2,1,0:T(8,128)(2,1)S(1)} %get-tuple-element.57), channel_id=1, source_target_pairs={{0,127},{1,2},{2,1},{3,4},{4,3},{5,6},{6,5},{7,8},{8,7},{9,10},{10... | collective-permute-start | bytes 786440 | tf_op jit(solution)/shard_map/ppermute | solution.py:313
  74.1 0.0 collective-permute-done.7.refs_3_
  74.1 8.3 %own.7 = (f32[129,16,128]{2,1,0:T(8,128)S(1)}, bf16[32,16384]{1,0:T(8,128)(2,1)S(1)}, f32[80,128]{1,0:T(8,128)S(1)}) custom-call(s32[8,128]{1,0:T(8,128)S(1)} %get-tuple-element.36.refs_0_, bf16[256,128,128]{2,1,0:T(8,128)(2,1)S(1)} %get-tuple-element.37.refs_1_, bf16[128,16,128]{2,1,0:T(8,128)(2,1)S(1)} %get-tuple-element.58.refs_2_, ...), custom_call_target="tpu_custom_call" | custom-call | flops 1000000000 | bytes 10000000 | tf_op jit(solution)/shard_map/own/pallas_call | solution.py:316
  82.4 0.0 collective-permute-done.6.refs_2_
  82.4 4.9 %far.7 = (bf16[32,16384]{1,0:T(8,128)(2,1)S(1)}, f32[80,128]{1,0:T(8,128)S(1)}) custom-call(s32[8,128]{1,0:T(8,128)S(1)} %get-tuple-element.36.refs_0_, bf16[256,128,128]{2,1,0:T(8,128)(2,1)S(1)} %get-tuple-element.37.refs_1_, bf16[64,16,128]{2,1,0:T(8,128)(2,1)S(1)} %collective-permute-done.6.refs_2_, f32[129,16,128]{2,1,0:T(8,128)S(1)} %get-tuple-element.63.refs_3_, ...), custom_call_target="tpu_custom_call" | custom-call | tf_op jit(solution)/shard_map/far/pallas_call | solution.py:334
  87.3 0.0 collective-permute-start.8
  87.4 1.2 collective-permute-done.8
  88.6 0.0 collective-permute-start.11
  88.6 0.6 collective-permute-start.10
  89.2 1.5 %collective-permute-start.9 = (f32[80,128]{1,0:T(8,128)S(1)}, f32[80,128]{1,0:T(8,128)S(1)}, u32[]{:S(2)}, u32[]{:S(2)}) collective-permute-start(f32[80,128]{1,0:T(8,128)S(1)} %add.30), channel_id=1, source_target_pairs={{0,2},{1,3},{2,4},{3,5},{4,6},{5,7},{6,0},{7,1},{8,10},{9,11},{10,... | collective-permute-start | bytes 122888 | tf_op jit(solution)/shard_map/ppermute | solution.py:355
  90.6 2.0 %collective-permute-done.11 = f32[80,128]{1,0:T(8,128)S(1)} collective-permute-done((f32[80,128]{1,0:T(8,128)S(1)}, f32[80,128]{1,0:T(8,128)S(1)}, u32[]{:S(2)}, u32[]{:S(2)}) %collective-permute-start.11) | collective-permute-done | bytes 40992 | tf_op jit(solution)/shard_map/ppermute | solution.py:355
  92.7 1.6 %collective-permute-done.10 = f32[80,128]{1,0:T(8,128)S(1)} collective-permute-done((f32[80,128]{1,0:T(8,128)S(1)}, f32[80,128]{1,0:T(8,128)S(1)}, u32[]{:S(2)}, u32[]{:S(2)}) %collective-permute-start.10) | collective-permute-done | bytes 40992 | tf_op jit(solution)/shard_map/ppermute | solution.py:355
  94.3 1.0 collective-permute-done.9
  95.3 0.1 collective-permute-start.14
  95.4 0.1 collective-permute-start.13
  95.5 1.9 %collective-permute-start.12 = (f32[80,128]{1,0:T(8,128)S(1)}, f32[80,128]{1,0:T(8,128)S(1)}, u32[]{:S(2)}, u32[]{:S(2)}) collective-permute-start(f32[80,128]{1,0:T(8,128)S(1)} %add_add_fusion.2), channel_id=1, source_target_pairs={{0,8},{1,9},{2,10},{3,11},{4,12},{5,13},{6,14},{7,15},{8,16},{9,17... | collective-permute-start | bytes 122888 | tf_op jit(solution)/shard_map/ppermute | solution.py:355
  97.4 2.0 %collective-permute-done.14 = f32[80,128]{1,0:T(8,128)S(1)} collective-permute-done((f32[80,128]{1,0:T(8,128)S(1)}, f32[80,128]{1,0:T(8,128)S(1)}, u32[]{:S(2)}, u32[]{:S(2)}) %collective-permute-start.14) | collective-permute-done | bytes 40992 | tf_op jit(solution)/shard_map/ppermute | solution.py:355
  99.4 1.9 %collective-permute-done.13 = f32[80,128]{1,0:T(8,128)S(1)} collective-permute-done((f32[80,128]{1,0:T(8,128)S(1)}, f32[80,128]{1,0:T(8,128)S(1)}, u32[]{:S(2)}, u32[]{:S(2)}) %collective-permute-start.13) | collective-permute-done | bytes 40992 | tf_op jit(solution)/shard_map/ppermute | solution.py:355
  101.2 0.8 collective-permute-done.12
  102.1 2.8 %collective-permute-start.17 = (f32[80,128]{1,0:T(8,128)S(1)}, f32[80,128]{1,0:T(8,128)S(1)}, u32[]{:S(2)}, u32[]{:S(2)}) collective-permute-start(f32[80,128]{1,0:T(8,128)S(1)} %add_add_fusion.1), channel_id=1, source_target_pairs={{0,96},{1,97},{2,98},{3,99},{4,100},{5,101},{6,102},{7,103},{8,104... | collective-permute-start | bytes 122888 | tf_op jit(solution)/shard_map/ppermute | solution.py:355
  104.9 0.0 collective-permute-start.16
  104.9 0.9 collective-permute-start.15
  105.9 0.7 collective-permute-done.17
  106.6 3.9 %collective-permute-done.16 = f32[80,128]{1,0:T(8,128)S(1)} collective-permute-done((f32[80,128]{1,0:T(8,128)S(1)}, f32[80,128]{1,0:T(8,128)S(1)}, u32[]{:S(2)}, u32[]{:S(2)}) %collective-permute-start.16) | collective-permute-done | bytes 40992 | tf_op jit(solution)/shard_map/ppermute | solution.py:355
  110.5 0.0 collective-permute-done.15
  110.6 16.4 %final.1 = (f32[80,16384]{1,0:T(8,128)}, f32[80,80]{1,0:T(8,128)}) custom-call(f32[80,128]{1,0:T(8,128)S(1)} %add_add_fusion.gram_in, bf16[32,16384]{1,0:T(8,128)(2,1)S(1)} %get-tuple-element.47.refs_5_.refs_6_.refs_0_, bf16[32,16384]{1,0:T(8,128)(2,1)S(1)} %get-tuple-element.54.refs_6_.refs_7_.refs_1_, ...), custom_call_target="tpu_custom_call" | custom-call | tf_op jit(solution)/shard_map/final/pallas_call | solution.py:362
  (4 shorter events, 0.0 us)
Async XLA Ops:
  1.3 1.2 copy-start
  2.5 3.4 %copy-start.2 = (bf16[256,128,128]{2,1,0:T(8,128)(2,1)S(1)}, bf16[256,128,128]{2,1,0:T(8,128)(2,1)}, u32[]{:S(2)}) copy-start(bf16[256,128,128]{2,1,0:T(8,128)(2,1)} %values_ref.1) | copy-start | bytes 25165828
  5.9 0.7 copy-start.3
  6.6 0.7 copy-start.4
  7.2 22.2 %copy-start.1 = (f32[16384,16]{0,1:T(8,128)S(1)}, f32[16384,16]{0,1:T(8,128)}, u32[]{:S(2)}) copy-start(f32[16384,16]{0,1:T(8,128)} %param.5) | copy-start | bytes 3145732
  20.5 8.9 %collective-permute-start.1 = (bf16[64,16,128]{2,1,0:T(8,128)(2,1)S(1)}, bf16[64,16,128]{2,1,0:T(8,128)(2,1)S(1)}, u32[]{:S(2)}, u32[]{:S(2)}) collective-permute-start(bf16[64,16,128]{2,1,0:T(8,128)(2,1)S(1)} %get-tuple-element.40), channel_id=1, source_target_pairs={{0,1},{1,0},{2,3},{3,2},{4,5},{5,4},{6,7},{7,6},{8,9},{9,8},{10,11... | collective-permute-start | bytes 786440 | tf_op jit(solution)/shard_map/ppermute | solution.py:314
  20.6 16.3 %collective-permute-start = (bf16[64,16,128]{2,1,0:T(8,128)(2,1)S(1)}, bf16[64,16,128]{2,1,0:T(8,128)(2,1)S(1)}, u32[]{:S(2)}, u32[]{:S(2)}) collective-permute-start(bf16[64,16,128]{2,1,0:T(8,128)(2,1)S(1)} %get-tuple-element.38), channel_id=1, source_target_pairs={{0,127},{1,2},{2,1},{3,4},{4,3},{5,6},{6,5},{7,8},{8,7},{9,10},{10... | collective-permute-start | bytes 786440 | tf_op jit(solution)/shard_map/ppermute | solution.py:313
  40.3 3.9 %collective-permute-start.3 = (bf16[64,16,128]{2,1,0:T(8,128)(2,1)S(1)}, bf16[64,16,128]{2,1,0:T(8,128)(2,1)S(1)}, u32[]{:S(2)}, u32[]{:S(2)}) collective-permute-start(bf16[64,16,128]{2,1,0:T(8,128)(2,1)S(1)} %get-tuple-element.45), channel_id=1, source_target_pairs={{0,1},{1,0},{2,3},{3,2},{4,5},{5,4},{6,7},{7,6},{8,9},{9,8},{10,11... | collective-permute-start | bytes 786440 | tf_op jit(solution)/shard_map/ppermute | solution.py:314
  40.4 11.3 %collective-permute-start.2 = (bf16[64,16,128]{2,1,0:T(8,128)(2,1)S(1)}, bf16[64,16,128]{2,1,0:T(8,128)(2,1)S(1)}, u32[]{:S(2)}, u32[]{:S(2)}) collective-permute-start(bf16[64,16,128]{2,1,0:T(8,128)(2,1)S(1)} %get-tuple-element.43), channel_id=1, source_target_pairs={{0,127},{1,2},{2,1},{3,4},{4,3},{5,6},{6,5},{7,8},{8,7},{9,10},{10... | collective-permute-start | bytes 786440 | tf_op jit(solution)/shard_map/ppermute | solution.py:313
  55.1 3.8 %collective-permute-start.5 = (bf16[64,16,128]{2,1,0:T(8,128)(2,1)S(1)}, bf16[64,16,128]{2,1,0:T(8,128)(2,1)S(1)}, u32[]{:S(2)}, u32[]{:S(2)}) collective-permute-start(bf16[64,16,128]{2,1,0:T(8,128)(2,1)S(1)} %get-tuple-element.52), channel_id=1, source_target_pairs={{0,1},{1,0},{2,3},{3,2},{4,5},{5,4},{6,7},{7,6},{8,9},{9,8},{10,11... | collective-permute-start | bytes 786440 | tf_op jit(solution)/shard_map/ppermute | solution.py:314
  55.2 11.9 %collective-permute-start.4 = (bf16[64,16,128]{2,1,0:T(8,128)(2,1)S(1)}, bf16[64,16,128]{2,1,0:T(8,128)(2,1)S(1)}, u32[]{:S(2)}, u32[]{:S(2)}) collective-permute-start(bf16[64,16,128]{2,1,0:T(8,128)(2,1)S(1)} %get-tuple-element.50), channel_id=1, source_target_pairs={{0,127},{1,2},{2,1},{3,4},{4,3},{5,6},{6,5},{7,8},{8,7},{9,10},{10... | collective-permute-start | bytes 786440 | tf_op jit(solution)/shard_map/ppermute | solution.py:313
  70.4 3.7 %collective-permute-start.7 = (bf16[64,16,128]{2,1,0:T(8,128)(2,1)S(1)}, bf16[64,16,128]{2,1,0:T(8,128)(2,1)S(1)}, u32[]{:S(2)}, u32[]{:S(2)}) collective-permute-start(bf16[64,16,128]{2,1,0:T(8,128)(2,1)S(1)} %get-tuple-element.59), channel_id=1, source_target_pairs={{0,1},{1,0},{2,3},{3,2},{4,5},{5,4},{6,7},{7,6},{8,9},{9,8},{10,11... | collective-permute-start | bytes 786440 | tf_op jit(solution)/shard_map/ppermute | solution.py:314
  70.5 11.9 %collective-permute-start.6 = (bf16[64,16,128]{2,1,0:T(8,128)(2,1)S(1)}, bf16[64,16,128]{2,1,0:T(8,128)(2,1)S(1)}, u32[]{:S(2)}, u32[]{:S(2)}) collective-permute-start(bf16[64,16,128]{2,1,0:T(8,128)(2,1)S(1)} %get-tuple-element.57), channel_id=1, source_target_pairs={{0,127},{1,2},{2,1},{3,4},{4,3},{5,6},{6,5},{7,8},{8,7},{9,10},{10... | collective-permute-start | bytes 786440 | tf_op jit(solution)/shard_map/ppermute | solution.py:313
  87.3 1.3 collective-permute-start.8
  88.6 4.1 %collective-permute-start.11 = (f32[80,128]{1,0:T(8,128)S(1)}, f32[80,128]{1,0:T(8,128)S(1)}, u32[]{:S(2)}, u32[]{:S(2)}) collective-permute-start(f32[80,128]{1,0:T(8,128)S(1)} %add.30), channel_id=1, source_target_pairs={{0,6},{1,7},{2,0},{3,1},{4,2},{5,3},{6,4},{7,5},{8,14},{9,15},{10,... | collective-permute-start | bytes 122888 | tf_op jit(solution)/shard_map/ppermute | solution.py:355
  88.6 5.7 %collective-permute-start.10 = (f32[80,128]{1,0:T(8,128)S(1)}, f32[80,128]{1,0:T(8,128)S(1)}, u32[]{:S(2)}, u32[]{:S(2)}) collective-permute-start(f32[80,128]{1,0:T(8,128)S(1)} %add.30), channel_id=1, source_target_pairs={{0,4},{1,5},{2,6},{3,7},{4,0},{5,1},{6,2},{7,3},{8,12},{9,13},{10,... | collective-permute-start | bytes 122888 | tf_op jit(solution)/shard_map/ppermute | solution.py:355
  89.2 6.1 %collective-permute-start.9 = (f32[80,128]{1,0:T(8,128)S(1)}, f32[80,128]{1,0:T(8,128)S(1)}, u32[]{:S(2)}, u32[]{:S(2)}) collective-permute-start(f32[80,128]{1,0:T(8,128)S(1)} %add.30), channel_id=1, source_target_pairs={{0,2},{1,3},{2,4},{3,5},{4,6},{5,7},{6,0},{7,1},{8,10},{9,11},{10,... | collective-permute-start | bytes 122888 | tf_op jit(solution)/shard_map/ppermute | solution.py:355
  95.3 4.1 %collective-permute-start.14 = (f32[80,128]{1,0:T(8,128)S(1)}, f32[80,128]{1,0:T(8,128)S(1)}, u32[]{:S(2)}, u32[]{:S(2)}) collective-permute-start(f32[80,128]{1,0:T(8,128)S(1)} %add_add_fusion.2), channel_id=1, source_target_pairs={{0,24},{1,25},{2,26},{3,27},{4,28},{5,29},{6,30},{7,31},{8,0},{9,1... | collective-permute-start | bytes 122888 | tf_op jit(solution)/shard_map/ppermute | solution.py:355
  95.4 5.8 %collective-permute-start.13 = (f32[80,128]{1,0:T(8,128)S(1)}, f32[80,128]{1,0:T(8,128)S(1)}, u32[]{:S(2)}, u32[]{:S(2)}) collective-permute-start(f32[80,128]{1,0:T(8,128)S(1)} %add_add_fusion.2), channel_id=1, source_target_pairs={{0,16},{1,17},{2,18},{3,19},{4,20},{5,21},{6,22},{7,23},{8,24},{9,... | collective-permute-start | bytes 122888 | tf_op jit(solution)/shard_map/ppermute | solution.py:355
  95.5 6.6 %collective-permute-start.12 = (f32[80,128]{1,0:T(8,128)S(1)}, f32[80,128]{1,0:T(8,128)S(1)}, u32[]{:S(2)}, u32[]{:S(2)}) collective-permute-start(f32[80,128]{1,0:T(8,128)S(1)} %add_add_fusion.2), channel_id=1, source_target_pairs={{0,8},{1,9},{2,10},{3,11},{4,12},{5,13},{6,14},{7,15},{8,16},{9,17... | collective-permute-start | bytes 122888 | tf_op jit(solution)/shard_map/ppermute | solution.py:355
  102.1 4.5 %collective-permute-start.17 = (f32[80,128]{1,0:T(8,128)S(1)}, f32[80,128]{1,0:T(8,128)S(1)}, u32[]{:S(2)}, u32[]{:S(2)}) collective-permute-start(f32[80,128]{1,0:T(8,128)S(1)} %add_add_fusion.1), channel_id=1, source_target_pairs={{0,96},{1,97},{2,98},{3,99},{4,100},{5,101},{6,102},{7,103},{8,104... | collective-permute-start | bytes 122888 | tf_op jit(solution)/shard_map/ppermute | solution.py:355
  104.9 5.6 %collective-permute-start.16 = (f32[80,128]{1,0:T(8,128)S(1)}, f32[80,128]{1,0:T(8,128)S(1)}, u32[]{:S(2)}, u32[]{:S(2)}) collective-permute-start(f32[80,128]{1,0:T(8,128)S(1)} %add_add_fusion.1), channel_id=1, source_target_pairs={{0,64},{1,65},{2,66},{3,67},{4,68},{5,69},{6,70},{7,71},{8,72},{9,... | collective-permute-start | bytes 122888 | tf_op jit(solution)/shard_map/ppermute | solution.py:355
  104.9 5.7 %collective-permute-start.15 = (f32[80,128]{1,0:T(8,128)S(1)}, f32[80,128]{1,0:T(8,128)S(1)}, u32[]{:S(2)}, u32[]{:S(2)}) collective-permute-start(f32[80,128]{1,0:T(8,128)S(1)} %add_add_fusion.1), channel_id=1, source_target_pairs={{0,32},{1,33},{2,34},{3,35},{4,36},{5,37},{6,38},{7,39},{8,40},{9,... | collective-permute-start | bytes 122888 | tf_op jit(solution)/shard_map/ppermute | solution.py:355
where the time goes:
time: 127 us
  Pallas kernels  76.2 us (60%)
  starting transfers between devices  28.2 us (22%)
  waiting for transfers between devices  15.2 us (12%)
  local copies, waits for them, and re-layouts  5.96 us (5%)
  between operations  1.4 us (1%)
    pallas_call x4, Pallas kernels, body(): pl.pallas_call(functools.partial(own_kernel, level - 1), out_shape=(acc_t...  31.5 us
    ppermute x4, starting transfers between devices, body(): got_b = lax.ppermute(send_b, AXIS, far)  19.9 us
    pallas_call x1, Pallas kernels, body(): pl.pallas_call(functools.partial(final_kernel, rows * n), grid=(rows // c...  16.4 us
    ppermute x10, waiting for transfers between devices, phase(): moved = moved + lax.ppermute(value, AXIS, perm)  15.2 us
    pallas_call x4, Pallas kernels, body(): pl.pallas_call(functools.partial(far_kernel, level, last), out_shape=outs...  14.9 us
    pallas_call x1, Pallas kernels, body(): pl.pallas_call(setup_kernel, out_shape=(shape((total, side, side), BF16),...  13.3 us
    ppermute x10, starting transfers between devices, phase(): moved = moved + lax.ppermute(value, AXIS, perm)  7.92 us
    unnamed x10, local copies, waits for them, and re-layouts  5.96 us
  transfers between devices with their start and end apart: 18, of which 9 were waited for; matrix products, arithmetic and copies ran while one was open for 0% of the time, Pallas kernels for 25%

commit v1 on v0

--- a/solution.py
+++ b/solution.py
@@ -23,6 +23,30 @@
 
 def tile_product(block, tile):
     return lax.dot_general(block, tile, (((1,), (1,)), ((), ())), preferred_element_type=F32)
+
+
+def quad_products(blocks, tiles):
+    zero = jnp.zeros_like(blocks[0])
+    join = jnp.concatenate
+    out = []
+    for i in range(0, len(blocks), 4):
+        x, t = blocks[i:i + 4], tiles[i:i + 4]
+        left = join([join([x[0], zero], 1), join([zero, x[1]], 1), join([x[2], zero], 1), join([zero, x[3]], 1)], 0)
+        right = join([join([t[0], t[1]], 1), join([t[2], t[3]], 1)], 0)
+        got = tile_product(left, right)
+        out += [got[:16, :128], got[16:32, :128], got[32:48, 128:], got[48:, 128:]]
+    return out
+
+
+def spread_tiles(count, unroll, acc_ref, block_at, tile_at, row_at):
+    def step(base, _):
+        at = [base * unroll + u for u in range(unroll)]
+        got = quad_products([block_at(t) for t in at], [tile_at(t) for t in at])
+        for t, product in zip(at, got):
+            acc_ref[row_at(t)] += product
+        return 0
+
+    lax.fori_loop(0, count // unroll, step, 0)
 
 
 def pack(plan_ref, scaled_ref, send_a_ref, send_b_ref):
@@ -82,26 +106,31 @@
 
     lax.fori_loop(0, half, send_plan, 0)
 
-    ones = jnp.ones((16, side), BF16)
+    row = lax.broadcasted_iota(jnp.int32, (16, 2 * side), 0)
+    lane = lax.broadcasted_iota(jnp.int32, (16, 2 * side), 1)
+    ones = jnp.where((row < 8) == (lane < side), 1.0, 0.0).astype(BF16)
+    join = jnp.concatenate
     for k in range(chunks):
         copy(k).wait()
-
-        def degree_step(base, _):
-            for u in range(8):
-                t = k * per + base * 8 + u
-                row = jnp.where(t < count, index_ref[0, t], blocks)
-                acc_ref[row] += tile_product(ones, tiles_ref[t])
-            return 0
-
-        lax.fori_loop(0, per // 8, degree_step, 0)
+        slots = [k * per + u for u in range(per)]
+        got = []
+        for i in range(0, per, 4):
+            t = [tiles_ref[slot] for slot in slots[i:i + 4]]
+            sums = tile_product(ones, join([join([t[0], t[1]], 1), join([t[2], t[3]], 1)], 0))
+            got += [sums[:8, :side], sums[8:, :side], sums[:8, side:], sums[8:, side:]]
+        for t, part in zip(slots, got):
+            target = index_ref[0, t]
+            if t >= ghosts:
+                target = jnp.where(t < count, target, blocks)
+            acc_ref[target] += part
 
     def scale_step(base, _):
         for u in range(8):
             b = base * 8 + u
-            factor = 1.0 / jnp.sqrt(1.0 + acc_ref[b])
+            factor = lax.rsqrt(1.0 + acc_ref[b])
             scale_ref[b] = factor
             at = pl.ds(pl.multiple_of(b * side, side), side)
-            scaled_ref[b] = (factor * start_ref[:, at]).astype(BF16)
+            scaled_ref[b] = (join([factor, factor], 0) * start_ref[:, at]).astype(BF16)
         return 0
 
     lax.fori_loop(0, blocks // 8, scale_step, 0)
@@ -139,23 +168,10 @@
     acc_ref[...] = jnp.zeros_like(acc_ref)
     ghosts = 2 * half
 
-    def own_step(base, _):
-        for u in range(8):
-            t = base * 8 + u
-            acc_ref[plan_ref[OROW, t]] += tile_product(
-                scaled_ref[plan_ref[OCOL, t]], tiles_ref[ghosts + t])
-        return 0
-
-    lax.fori_loop(0, ghosts // 8, own_step, 0)
-
-    def near_step(base, _):
-        for u in range(8):
-            g = base * 8 + u
-            acc_ref[plan_ref[GROW, g]] += tile_product(got_ref[g], tiles_ref[plan_ref[SLOT, g]])
-        return 0
-
-    lax.fori_loop(0, half // 8, near_step, 0)
-
+    spread_tiles(ghosts, 32, acc_ref, lambda t: scaled_ref[plan_ref[OCOL, t]],
+                 lambda t: tiles_ref[ghosts + t], lambda t: plan_ref[OROW, t])
+    spread_tiles(half, 32, acc_ref, lambda g: got_ref[g],
+                 lambda g: tiles_ref[plan_ref[SLOT, g]], lambda g: plan_ref[GROW, g])
     high, low = split(vec_ref[...])
     part_ref[:16] = high
     part_ref[16:] = low
@@ -164,7 +180,7 @@
 
 
 def far_kernel(level, last, *refs):
-    plan_ref, tiles_ref, got_ref, acc_in, scale_ref = refs[:5]
+    plan_ref, tiles_ref, got_ref, _, scale_ref = refs[:5]
     at = 5
     prev_ref = None
     if level > 1:
@@ -180,22 +196,14 @@
     half = got_ref.shape[0]
     side = tiles_ref.shape[1]
     blocks = scale_ref.shape[0]
-    acc_ref[...] = acc_in[...]
-
-    def far_step(base, _):
-        for u in range(8):
-            g = base * 8 + u
-            acc_ref[plan_ref[GROW, half + g]] += tile_product(
-                got_ref[g], tiles_ref[plan_ref[SLOT, half + g]])
-        return 0
-
-    lax.fori_loop(0, half // 8, far_step, 0)
+    spread_tiles(half, 32, acc_ref, lambda g: got_ref[g],
+                 lambda g: tiles_ref[plan_ref[SLOT, half + g]], lambda g: plan_ref[GROW, half + g])
 
     def close_step(base, _):
         for u in range(8):
             b = base * 8 + u
             where = pl.ds(pl.multiple_of(b * side, side), side)
-            factor = scale_ref[b]
+            factor = jnp.concatenate([scale_ref[b], scale_ref[b]], 0)
             value = factor * acc_ref[b]
             if level > 1:
                 value = 2.0 * value - prev_ref[:, where]
@@ -245,12 +253,10 @@
 
 def final_kernel(row_total, gram_in, *refs):
     parts = refs[:STEPS + 1]
-    basis_ref, gram_ref, mix_ref = refs[STEPS + 1:]
+    basis_ref, gram_ref, mix_ref, stage_ref, sems = refs[STEPS + 1:]
     width = gram_ref.shape[0]
-    chunk = basis_ref.shape[1]
-
-    @pl.when(pl.program_id(0) == 0)
-    def _():
+
+    if True:
         lower = gram_in[...] * (1.0 / row_total)
         row = lax.broadcasted_iota(jnp.int32, lower.shape, 0)
         lane = lax.broadcasted_iota(jnp.int32, lower.shape, 1)
@@ -263,11 +269,22 @@
         high, low = split(inverse[:, :width])
         mix_ref[...] = jnp.concatenate([high, low, high], 1)
 
-    at = pl.ds(pl.multiple_of(pl.program_id(0) * chunk, chunk), chunk)
-    tops = [p[:16, at] for p in parts]
-    lows = [p[16:, at] for p in parts]
-    stack = jnp.concatenate(tops + tops + lows, 0)
-    basis_ref[...] = jnp.dot(mix_ref[...], stack, preferred_element_type=F32)
+    pieces = stage_ref.shape[0]
+    chunk = stage_ref.shape[2]
+
+    def out(k):
+        return pltpu.make_async_copy(stage_ref.at[k], basis_ref.at[:, pl.ds(k * chunk, chunk)], sems.at[k])
+
+    mix = mix_ref[...]
+    for k in range(pieces):
+        at = slice(k * chunk, (k + 1) * chunk)
+        tops = [p[:16, at] for p in parts]
+        lows = [p[16:, at] for p in parts]
+        stack = jnp.concatenate(tops + tops + lows, 0)
+        stage_ref[k] = jnp.dot(mix, stack, preferred_element_type=F32)
+        out(k).start()
+    for k in range(pieces):
+        out(k).wait()
 
 
 def params(mib, **kw):
@@ -297,11 +314,11 @@
     tiles, plan, scale, scaled, send_a, send_b = pl.pallas_call(
         setup_kernel,
         out_shape=(shape((total, side, side), BF16), shape((8, 128), jnp.int32),
-                   shape((blocks, width, side), F32), scaled_t, send_t, send_t),
+                   shape((blocks, 8, side), F32), scaled_t, send_t, send_t),
         in_specs=[spec(SMEM), spec(SMEM), spec(SMEM), spec(pltpu.HBM), spec(VMEM)],
         out_specs=(spec(VMEM), spec(SMEM), spec(VMEM), spec(VMEM), spec(VMEM), spec(VMEM)),
-        scratch_shapes=[VMEM(acc_t.shape, F32), pltpu.SemaphoreType.DMA((16,))],
-        compiler_params=params(20),
+        scratch_shapes=[VMEM((blocks + 1, 8, side), F32), pltpu.SemaphoreType.DMA((16,))],
+        compiler_params=params(41),
         name="setup",
     )(tile_index.T, tile_count, ghost_send[0], tile_values, start)
 
@@ -328,23 +345,23 @@
             args.append(vectors[-2])
         if last:
             args += parts + [gram]
-            outs = (part_t, gram_t)
+            outs = (part_t, gram_t, acc_t)
         else:
-            outs = (vec_t, scaled_t, send_t, send_t)
+            outs = (vec_t, scaled_t, send_t, send_t, acc_t)
         got = pl.pallas_call(
             functools.partial(far_kernel, level, last),
             out_shape=outs,
             in_specs=[spec(SMEM)] + [spec(VMEM)] * (len(args) - 1),
             out_specs=(spec(VMEM),) * len(outs),
-            scratch_shapes=[VMEM(acc_t.shape, F32)],
+            input_output_aliases={3: len(outs) - 1},
             compiler_params=params(20),
             name="far",
         )(*args)
         if last:
-            part, gram = got
+            part, gram, _ = got
             parts.append(part)
         else:
-            vec, scaled, send_a, send_b = got
+            vec, scaled, send_a, send_b, _ = got
             vectors.append(vec)
 
     def phase(value, shift, count):
@@ -361,12 +378,11 @@
     chunk = 1024
     basis_out, gram_matrix = pl.pallas_call(
         functools.partial(final_kernel, rows * n),
-        grid=(rows // chunk,),
         out_shape=(shape((basis, rows), F32), shape((basis, basis), F32)),
         in_specs=[spec(VMEM)] * (STEPS + 2),
-        out_specs=(pl.BlockSpec((basis, chunk), lambda i: (0, i)),
-                   pl.BlockSpec((basis, basis), lambda i: (0, 0))),
-        scratch_shapes=[VMEM((basis, 3 * basis), BF16)],
+        out_specs=(spec(pltpu.HBM), spec(VMEM)),
+        scratch_shapes=[VMEM((basis, 3 * basis), BF16), VMEM((rows // chunk, basis, chunk), F32),
+                        pltpu.SemaphoreType.DMA((rows // chunk,))],
         compiler_params=params(20),
         name="final",
     )(gram, *parts)

time: 127 us -> 109 us (0.86)
  Pallas kernels: 76.2 us -> 48.8 us
  starting transfers between devices: 28.2 us -> 40.6 us
  local copies, waits for them, and re-layouts: 5.96 us -> 2.58 us
    pallas_call x4, Pallas kernels: 31.5 us -> 18 us  [body(): pl.pallas_call(functools.partial(own_kernel, level - 1), out_shape=(acc_t...]
    ppermute x4, starting transfers between devices: 19.9 us -> 29.7 us  [body(): got_b = lax.ppermute(send_b, AXIS, far)]
    pallas_call x1, Pallas kernels: 13.3 us -> 8.54 us  [body(): pl.pallas_call(setup_kernel, out_shape=(shape((total, side, side), BF16),...]
    pallas_call x4, Pallas kernels: 14.9 us -> 10.3 us  [body(): pl.pallas_call(functools.partial(far_kernel, level, last), out_shape=outs...]
    pallas_call x1, Pallas kernels: 16.4 us -> 12 us  [body(): pl.pallas_call(functools.partial(final_kernel, rows * n), out_shape=(shap...]
    unnamed x10 -> x6, local copies, waits for them, and re-layouts: 5.96 us -> 2.58 us
    ppermute x10, starting transfers between devices: 7.92 us -> 10.6 us  [phase(): moved = moved + lax.ppermute(value, AXIS, perm)]
  transfers between devices with their start and end apart: 18 -> 18, of which waited for: 9 -> 9; matrix products, arithmetic and copies ran while one was open for 0% -> 0% of each run, Pallas kernels for 25% -> 17%
where the time goes in v1:
time: 109 us
  Pallas kernels  48.8 us (45%)
  starting transfers between devices  40.6 us (37%)
  waiting for transfers between devices  15.2 us (14%)
  local copies, waits for them, and re-layouts  2.58 us (2%)
  between operations  1.57 us (1%)
    ppermute x4, starting transfers between devices, body(): got_b = lax.ppermute(send_b, AXIS, far)  29.7 us
    pallas_call x4, Pallas kernels, body(): pl.pallas_call(functools.partial(own_kernel, level - 1), out_shape=(acc_t...  18 us
    ppermute x10, waiting for transfers between devices, phase(): moved = moved + lax.ppermute(value, AXIS, perm)  15.2 us
    pallas_call x1, Pallas kernels, body(): pl.pallas_call(functools.partial(final_kernel, rows * n), out_shape=(shap...  12 us
    ppermute x10, starting transfers between devices, phase(): moved = moved + lax.ppermute(value, AXIS, perm)  10.6 us
    pallas_call x4, Pallas kernels, body(): pl.pallas_call(functools.partial(far_kernel, level, last), out_shape=outs...  10.3 us
    pallas_call x1, Pallas kernels, body(): pl.pallas_call(setup_kernel, out_shape=(shape((total, side, side), BF16),...  8.54 us
    unnamed x6, local copies, waits for them, and re-layouts  2.58 us
  transfers between devices with their start and end apart: 18, of which 9 were waited for; matrix products, arithmetic and copies ran while one was open for 0% of the time, Pallas kernels for 17%

profile of v1, /device:TPU:0, one launch (start us, length us, event | category | flops | bytes accessed | tf_op | source)
XLA Modules:
  0.0 108.8 jit_solution(16544863455537504660)
XLA Ops:
  1.3 0.0 copy-start
  1.3 1.2 %copy-done = f32[16384,16]{0,1:T(8,128)S(1)} copy-done((f32[16384,16]{0,1:T(8,128)S(1)}, f32[16384,16]{0,1:T(8,128)}, u32[]{:S(2)}) %copy-start) | copy-done | bytes 1048600
  2.5 0.0 copy-start.1
  2.5 0.7 copy-done.1
  3.2 0.0 copy-start.2
  3.2 0.7 copy-done.2
  3.9 8.5 %setup.1 = (bf16[256,128,128]{2,1,0:T(8,128)(2,1)S(1)}, s32[8,128]{1,0:T(8,128)S(1)}, f32[128,8,128]{2,1,0:T(8,128)S(1)}, bf16[128,16,128]{2,1,0:T(8,128)(2,1)S(...) custom-call(s32[2,256]{1,0:T(2,128)S(1)} %bitcast.7, s32[1]{0:T(128)S(6)} %copy.15.count_ref, ...), custom_call_target="tpu_custom_call" | custom-call | tf_op jit(solution)/shard_map/setup/pallas_call | solution.py:314
  12.4 0.1 collective-permute-start.1
  12.5 8.9 %collective-permute-start = (bf16[64,16,128]{2,1,0:T(8,128)(2,1)S(1)}, bf16[64,16,128]{2,1,0:T(8,128)(2,1)S(1)}, u32[]{:S(2)}, u32[]{:S(2)}) collective-permute-start(bf16[64,16,128]{2,1,0:T(8,128)(2,1)S(1)} %get-tuple-element.38), channel_id=1, source_target_pairs={{0,127},{1,2},{2,1},{3,4},{4,3},{5,6},{6,5},{7,8},{8,7},{9,10},{10... | collective-permute-start | bytes 786440 | tf_op jit(solution)/shard_map/ppermute | solution.py:330
  21.4 0.0 collective-permute-done.1.refs_3_
  21.4 4.1 %own.4 = (f32[129,16,128]{2,1,0:T(8,128)S(1)}, bf16[32,16384]{1,0:T(8,128)(2,1)S(1)}, f32[80,128]{1,0:T(8,128)S(1)}) custom-call(s32[8,128]{1,0:T(8,128)S(1)} %get-tuple-element.36.refs_0_, bf16[256,128,128]{2,1,0:T(8,128)(2,1)S(1)} %get-tuple-element.37.refs_1_, bf16[128,16,128]{2,1,0:T(8,128)(2,1)S(1)} %get-tuple-element.39.refs_2_, ...), custom_call_target="tpu_custom_call" | custom-call | flops 1000000000 | bytes 10000000 | tf_op jit(solution)/shard_map/own/pallas_call | solution.py:333
  25.5 0.0 collective-permute-done.refs_2_
  25.5 2.1 %far.4 = (f32[16,16384]{1,0:T(8,128)S(1)}, bf16[128,16,128]{2,1,0:T(8,128)(2,1)S(1)}, bf16[64,16,128]{2,1,0:T(8,128)(2,1)S(1)}, bf16[64,16,128]{2,1,0:T(8,128)(2,1)S(1)}, f32[129,16,128]{2,1,0:T(8,128)S(1)}) custom-call(s32[8,128]{1,0:T(8,128)S(1)} %get-tuple-element.36.refs_0_, ...), custom_call_target="tpu_custom_call", output_to_operand_aliasing={{4}: (3, {})} | custom-call | tf_op jit(solution)/shard_map/far/pallas_call | solution.py:351
  27.7 0.1 collective-permute-start.3
  27.8 7.2 %collective-permute-start.2 = (bf16[64,16,128]{2,1,0:T(8,128)(2,1)S(1)}, bf16[64,16,128]{2,1,0:T(8,128)(2,1)S(1)}, u32[]{:S(2)}, u32[]{:S(2)}) collective-permute-start(bf16[64,16,128]{2,1,0:T(8,128)(2,1)S(1)} %get-tuple-element.43), channel_id=1, source_target_pairs={{0,127},{1,2},{2,1},{3,4},{4,3},{5,6},{6,5},{7,8},{8,7},{9,10},{10... | collective-permute-start | bytes 786440 | tf_op jit(solution)/shard_map/ppermute | solution.py:330
  34.9 0.0 collective-permute-done.3.refs_3_
  35.0 4.2 %own.5 = (f32[129,16,128]{2,1,0:T(8,128)S(1)}, bf16[32,16384]{1,0:T(8,128)(2,1)S(1)}, f32[80,128]{1,0:T(8,128)S(1)}) custom-call(s32[8,128]{1,0:T(8,128)S(1)} %get-tuple-element.36.refs_0_, bf16[256,128,128]{2,1,0:T(8,128)(2,1)S(1)} %get-tuple-element.37.refs_1_, bf16[128,16,128]{2,1,0:T(8,128)(2,1)S(1)} %get-tuple-element.44.refs_2_, ...), custom_call_target="tpu_custom_call" | custom-call | flops 1000000000 | bytes 10000000 | tf_op jit(solution)/shard_map/own/pallas_call | solution.py:333
  39.1 0.0 collective-permute-done.2.refs_2_
  39.1 2.2 %far.5 = (f32[16,16384]{1,0:T(8,128)S(1)}, bf16[128,16,128]{2,1,0:T(8,128)(2,1)S(1)}, bf16[64,16,128]{2,1,0:T(8,128)(2,1)S(1)}, bf16[64,16,128]{2,1,0:T(8,128)(2,1)S(1)}, f32[129,16,128]{2,1,0:T(8,128)S(1)}) custom-call(s32[8,128]{1,0:T(8,128)S(1)} %get-tuple-element.36.refs_0_, ...), custom_call_target="tpu_custom_call", output_to_operand_aliasing={{4}: (3, {})} | custom-call | tf_op jit(solution)/shard_map/far/pallas_call | solution.py:351
  41.3 0.1 collective-permute-start.5
  41.4 7.1 %collective-permute-start.4 = (bf16[64,16,128]{2,1,0:T(8,128)(2,1)S(1)}, bf16[64,16,128]{2,1,0:T(8,128)(2,1)S(1)}, u32[]{:S(2)}, u32[]{:S(2)}) collective-permute-start(bf16[64,16,128]{2,1,0:T(8,128)(2,1)S(1)} %get-tuple-element.50), channel_id=1, source_target_pairs={{0,127},{1,2},{2,1},{3,4},{4,3},{5,6},{6,5},{7,8},{8,7},{9,10},{10... | collective-permute-start | bytes 786440 | tf_op jit(solution)/shard_map/ppermute | solution.py:330
  48.5 0.0 collective-permute-done.5.refs_3_
  48.5 4.7 %own.6 = (f32[129,16,128]{2,1,0:T(8,128)S(1)}, bf16[32,16384]{1,0:T(8,128)(2,1)S(1)}, f32[80,128]{1,0:T(8,128)S(1)}) custom-call(s32[8,128]{1,0:T(8,128)S(1)} %get-tuple-element.36.refs_0_, bf16[256,128,128]{2,1,0:T(8,128)(2,1)S(1)} %get-tuple-element.37.refs_1_, bf16[128,16,128]{2,1,0:T(8,128)(2,1)S(1)} %get-tuple-element.51.refs_2_, ...), custom_call_target="tpu_custom_call" | custom-call | flops 1000000000 | bytes 10000000 | tf_op jit(solution)/shard_map/own/pallas_call | solution.py:333
  53.3 0.0 collective-permute-done.4.refs_2_
  53.3 2.2 %far.6 = (f32[16,16384]{1,0:T(8,128)S(1)}, bf16[128,16,128]{2,1,0:T(8,128)(2,1)S(1)}, bf16[64,16,128]{2,1,0:T(8,128)(2,1)S(1)}, bf16[64,16,128]{2,1,0:T(8,128)(2,1)S(1)}, f32[129,16,128]{2,1,0:T(8,128)S(1)}) custom-call(s32[8,128]{1,0:T(8,128)S(1)} %get-tuple-element.36.refs_0_, ...), custom_call_target="tpu_custom_call", output_to_operand_aliasing={{4}: (3, {})} | custom-call | tf_op jit(solution)/shard_map/far/pallas_call | solution.py:351
  55.5 0.1 collective-permute-start.7
  55.6 6.5 %collective-permute-start.6 = (bf16[64,16,128]{2,1,0:T(8,128)(2,1)S(1)}, bf16[64,16,128]{2,1,0:T(8,128)(2,1)S(1)}, u32[]{:S(2)}, u32[]{:S(2)}) collective-permute-start(bf16[64,16,128]{2,1,0:T(8,128)(2,1)S(1)} %get-tuple-element.57), channel_id=1, source_target_pairs={{0,127},{1,2},{2,1},{3,4},{4,3},{5,6},{6,5},{7,8},{8,7},{9,10},{10... | collective-permute-start | bytes 786440 | tf_op jit(solution)/shard_map/ppermute | solution.py:330
  62.1 0.0 collective-permute-done.7.refs_3_
  62.1 5.0 %own.7 = (f32[129,16,128]{2,1,0:T(8,128)S(1)}, bf16[32,16384]{1,0:T(8,128)(2,1)S(1)}, f32[80,128]{1,0:T(8,128)S(1)}) custom-call(s32[8,128]{1,0:T(8,128)S(1)} %get-tuple-element.36.refs_0_, bf16[256,128,128]{2,1,0:T(8,128)(2,1)S(1)} %get-tuple-element.37.refs_1_, bf16[128,16,128]{2,1,0:T(8,128)(2,1)S(1)} %get-tuple-element.58.refs_2_, ...), custom_call_target="tpu_custom_call" | custom-call | flops 1000000000 | bytes 10000000 | tf_op jit(solution)/shard_map/own/pallas_call | solution.py:333
  67.1 0.0 collective-permute-done.6.refs_2_
  67.1 3.7 %far.7 = (bf16[32,16384]{1,0:T(8,128)(2,1)S(1)}, f32[80,128]{1,0:T(8,128)S(1)}, f32[129,16,128]{2,1,0:T(8,128)S(1)}) custom-call(s32[8,128]{1,0:T(8,128)S(1)} %get-tuple-element.36.refs_0_, bf16[256,128,128]{2,1,0:T(8,128)(2,1)S(1)} %get-tuple-element.37.refs_1_, ...), custom_call_target="tpu_custom_call", output_to_operand_aliasing={{2}: (3, {})} | custom-call | tf_op jit(solution)/shard_map/far/pallas_call | solution.py:351
  70.8 0.0 collective-permute-start.8
  70.8 1.2 %collective-permute-done.8 = f32[80,128]{1,0:T(8,128)S(1)} collective-permute-done((f32[80,128]{1,0:T(8,128)S(1)}, f32[80,128]{1,0:T(8,128)S(1)}, u32[]{:S(2)}, u32[]{:S(2)}) %collective-permute-start.8) | collective-permute-done | bytes 40992 | tf_op jit(solution)/shard_map/ppermute | solution.py:372
  72.1 0.0 collective-permute-start.11
  72.1 0.1 collective-permute-start.10
  72.2 1.9 %collective-permute-start.9 = (f32[80,128]{1,0:T(8,128)S(1)}, f32[80,128]{1,0:T(8,128)S(1)}, u32[]{:S(2)}, u32[]{:S(2)}) collective-permute-start(f32[80,128]{1,0:T(8,128)S(1)} %add.30), channel_id=1, source_target_pairs={{0,2},{1,3},{2,4},{3,5},{4,6},{5,7},{6,0},{7,1},{8,10},{9,11},{10,... | collective-permute-start | bytes 122888 | tf_op jit(solution)/shard_map/ppermute | solution.py:372
  74.1 2.0 %collective-permute-done.11 = f32[80,128]{1,0:T(8,128)S(1)} collective-permute-done((f32[80,128]{1,0:T(8,128)S(1)}, f32[80,128]{1,0:T(8,128)S(1)}, u32[]{:S(2)}, u32[]{:S(2)}) %collective-permute-start.11) | collective-permute-done | bytes 40992 | tf_op jit(solution)/shard_map/ppermute | solution.py:372
  76.1 1.6 %collective-permute-done.10 = f32[80,128]{1,0:T(8,128)S(1)} collective-permute-done((f32[80,128]{1,0:T(8,128)S(1)}, f32[80,128]{1,0:T(8,128)S(1)}, u32[]{:S(2)}, u32[]{:S(2)}) %collective-permute-start.10) | collective-permute-done | bytes 40992 | tf_op jit(solution)/shard_map/ppermute | solution.py:372
  77.8 1.0 collective-permute-done.9
  78.8 0.1 collective-permute-start.14
  78.8 0.1 collective-permute-start.13
  78.9 1.9 %collective-permute-start.12 = (f32[80,128]{1,0:T(8,128)S(1)}, f32[80,128]{1,0:T(8,128)S(1)}, u32[]{:S(2)}, u32[]{:S(2)}) collective-permute-start(f32[80,128]{1,0:T(8,128)S(1)} %add_add_fusion.2), channel_id=1, source_target_pairs={{0,8},{1,9},{2,10},{3,11},{4,12},{5,13},{6,14},{7,15},{8,16},{9,17... | collective-permute-start | bytes 122888 | tf_op jit(solution)/shard_map/ppermute | solution.py:372
  80.9 2.0 %collective-permute-done.14 = f32[80,128]{1,0:T(8,128)S(1)} collective-permute-done((f32[80,128]{1,0:T(8,128)S(1)}, f32[80,128]{1,0:T(8,128)S(1)}, u32[]{:S(2)}, u32[]{:S(2)}) %collective-permute-start.14) | collective-permute-done | bytes 40992 | tf_op jit(solution)/shard_map/ppermute | solution.py:372
  82.8 1.9 %collective-permute-done.13 = f32[80,128]{1,0:T(8,128)S(1)} collective-permute-done((f32[80,128]{1,0:T(8,128)S(1)}, f32[80,128]{1,0:T(8,128)S(1)}, u32[]{:S(2)}, u32[]{:S(2)}) %collective-permute-start.13) | collective-permute-done | bytes 40992 | tf_op jit(solution)/shard_map/ppermute | solution.py:372
  84.7 0.8 collective-permute-done.12
  85.5 5.5 %collective-permute-start.17 = (f32[80,128]{1,0:T(8,128)S(1)}, f32[80,128]{1,0:T(8,128)S(1)}, u32[]{:S(2)}, u32[]{:S(2)}) collective-permute-start(f32[80,128]{1,0:T(8,128)S(1)} %add_add_fusion.1), channel_id=1, source_target_pairs={{0,96},{1,97},{2,98},{3,99},{4,100},{5,101},{6,102},{7,103},{8,104... | collective-permute-start | bytes 122888 | tf_op jit(solution)/shard_map/ppermute | solution.py:372
  91.0 0.0 collective-permute-start.16
  91.0 0.9 collective-permute-start.15
  91.9 0.7 collective-permute-done.17
  92.7 3.9 %collective-permute-done.16 = f32[80,128]{1,0:T(8,128)S(1)} collective-permute-done((f32[80,128]{1,0:T(8,128)S(1)}, f32[80,128]{1,0:T(8,128)S(1)}, u32[]{:S(2)}, u32[]{:S(2)}) %collective-permute-start.16) | collective-permute-done | bytes 40992 | tf_op jit(solution)/shard_map/ppermute | solution.py:372
  96.6 0.0 collective-permute-done.15
  96.7 12.0 %final.1 = (f32[80,16384]{1,0:T(8,128)}, f32[80,80]{1,0:T(8,128)}) custom-call(f32[80,128]{1,0:T(8,128)S(1)} %add_add_fusion.gram_in, bf16[32,16384]{1,0:T(8,128)(2,1)S(1)} %get-tuple-element.47.refs_5_.refs_6_.refs_0_, bf16[32,16384]{1,0:T(8,128)(2,1)S(1)} %get-tuple-element.54.refs_6_.refs_7_.refs_1_, ...), custom_call_target="tpu_custom_call" | custom-call | tf_op jit(solution)/shard_map/final/pallas_call | solution.py:379
  (4 shorter events, 0.0 us)
Async XLA Ops:
  1.3 1.2 %copy-start = (f32[16384,16]{0,1:T(8,128)S(1)}, f32[16384,16]{0,1:T(8,128)}, u32[]{:S(2)}) copy-start(f32[16384,16]{0,1:T(8,128)} %param.5) | copy-start | bytes 3145732
  2.5 0.7 copy-start.1
  3.2 0.7 copy-start.2
  12.4 9.0 %collective-permute-start.1 = (bf16[64,16,128]{2,1,0:T(8,128)(2,1)S(1)}, bf16[64,16,128]{2,1,0:T(8,128)(2,1)S(1)}, u32[]{:S(2)}, u32[]{:S(2)}) collective-permute-start(bf16[64,16,128]{2,1,0:T(8,128)(2,1)S(1)} %get-tuple-element.40), channel_id=1, source_target_pairs={{0,1},{1,0},{2,3},{3,2},{4,5},{5,4},{6,7},{7,6},{8,9},{9,8},{10,11... | collective-permute-start | bytes 786440 | tf_op jit(solution)/shard_map/ppermute | solution.py:331
  12.5 13.0 %collective-permute-start = (bf16[64,16,128]{2,1,0:T(8,128)(2,1)S(1)}, bf16[64,16,128]{2,1,0:T(8,128)(2,1)S(1)}, u32[]{:S(2)}, u32[]{:S(2)}) collective-permute-start(bf16[64,16,128]{2,1,0:T(8,128)(2,1)S(1)} %get-tuple-element.38), channel_id=1, source_target_pairs={{0,127},{1,2},{2,1},{3,4},{4,3},{5,6},{6,5},{7,8},{8,7},{9,10},{10... | collective-permute-start | bytes 786440 | tf_op jit(solution)/shard_map/ppermute | solution.py:330
  27.7 7.3 %collective-permute-start.3 = (bf16[64,16,128]{2,1,0:T(8,128)(2,1)S(1)}, bf16[64,16,128]{2,1,0:T(8,128)(2,1)S(1)}, u32[]{:S(2)}, u32[]{:S(2)}) collective-permute-start(bf16[64,16,128]{2,1,0:T(8,128)(2,1)S(1)} %get-tuple-element.45), channel_id=1, source_target_pairs={{0,1},{1,0},{2,3},{3,2},{4,5},{5,4},{6,7},{7,6},{8,9},{9,8},{10,11... | collective-permute-start | bytes 786440 | tf_op jit(solution)/shard_map/ppermute | solution.py:331
  27.8 11.4 %collective-permute-start.2 = (bf16[64,16,128]{2,1,0:T(8,128)(2,1)S(1)}, bf16[64,16,128]{2,1,0:T(8,128)(2,1)S(1)}, u32[]{:S(2)}, u32[]{:S(2)}) collective-permute-start(bf16[64,16,128]{2,1,0:T(8,128)(2,1)S(1)} %get-tuple-element.43), channel_id=1, source_target_pairs={{0,127},{1,2},{2,1},{3,4},{4,3},{5,6},{6,5},{7,8},{8,7},{9,10},{10... | collective-permute-start | bytes 786440 | tf_op jit(solution)/shard_map/ppermute | solution.py:330
  41.3 7.2 %collective-permute-start.5 = (bf16[64,16,128]{2,1,0:T(8,128)(2,1)S(1)}, bf16[64,16,128]{2,1,0:T(8,128)(2,1)S(1)}, u32[]{:S(2)}, u32[]{:S(2)}) collective-permute-start(bf16[64,16,128]{2,1,0:T(8,128)(2,1)S(1)} %get-tuple-element.52), channel_id=1, source_target_pairs={{0,1},{1,0},{2,3},{3,2},{4,5},{5,4},{6,7},{7,6},{8,9},{9,8},{10,11... | collective-permute-start | bytes 786440 | tf_op jit(solution)/shard_map/ppermute | solution.py:331
  41.4 11.8 %collective-permute-start.4 = (bf16[64,16,128]{2,1,0:T(8,128)(2,1)S(1)}, bf16[64,16,128]{2,1,0:T(8,128)(2,1)S(1)}, u32[]{:S(2)}, u32[]{:S(2)}) collective-permute-start(bf16[64,16,128]{2,1,0:T(8,128)(2,1)S(1)} %get-tuple-element.50), channel_id=1, source_target_pairs={{0,127},{1,2},{2,1},{3,4},{4,3},{5,6},{6,5},{7,8},{8,7},{9,10},{10... | collective-permute-start | bytes 786440 | tf_op jit(solution)/shard_map/ppermute | solution.py:330
  55.5 6.6 %collective-permute-start.7 = (bf16[64,16,128]{2,1,0:T(8,128)(2,1)S(1)}, bf16[64,16,128]{2,1,0:T(8,128)(2,1)S(1)}, u32[]{:S(2)}, u32[]{:S(2)}) collective-permute-start(bf16[64,16,128]{2,1,0:T(8,128)(2,1)S(1)} %get-tuple-element.59), channel_id=1, source_target_pairs={{0,1},{1,0},{2,3},{3,2},{4,5},{5,4},{6,7},{7,6},{8,9},{9,8},{10,11... | collective-permute-start | bytes 786440 | tf_op jit(solution)/shard_map/ppermute | solution.py:331
  55.6 11.5 %collective-permute-start.6 = (bf16[64,16,128]{2,1,0:T(8,128)(2,1)S(1)}, bf16[64,16,128]{2,1,0:T(8,128)(2,1)S(1)}, u32[]{:S(2)}, u32[]{:S(2)}) collective-permute-start(bf16[64,16,128]{2,1,0:T(8,128)(2,1)S(1)} %get-tuple-element.57), channel_id=1, source_target_pairs={{0,127},{1,2},{2,1},{3,4},{4,3},{5,6},{6,5},{7,8},{8,7},{9,10},{10... | collective-permute-start | bytes 786440 | tf_op jit(solution)/shard_map/ppermute | solution.py:330
  70.8 1.3 %collective-permute-start.8 = (f32[80,128]{1,0:T(8,128)S(1)}, f32[80,128]{1,0:T(8,128)S(1)}, u32[]{:S(2)}, u32[]{:S(2)}) collective-permute-start(f32[80,128]{1,0:T(8,128)S(1)} %get-tuple-element.66), channel_id=1, source_target_pairs={{0,1},{1,0},{2,3},{3,2},{4,5},{5,4},{6,7},{7,6},{8,9},{9,8},{10,11... | collective-permute-start | bytes 122888 | tf_op jit(solution)/shard_map/ppermute | solution.py:372
  72.1 4.1 %collective-permute-start.11 = (f32[80,128]{1,0:T(8,128)S(1)}, f32[80,128]{1,0:T(8,128)S(1)}, u32[]{:S(2)}, u32[]{:S(2)}) collective-permute-start(f32[80,128]{1,0:T(8,128)S(1)} %add.30), channel_id=1, source_target_pairs={{0,6},{1,7},{2,0},{3,1},{4,2},{5,3},{6,4},{7,5},{8,14},{9,15},{10,... | collective-permute-start | bytes 122888 | tf_op jit(solution)/shard_map/ppermute | solution.py:372
  72.1 5.7 %collective-permute-start.10 = (f32[80,128]{1,0:T(8,128)S(1)}, f32[80,128]{1,0:T(8,128)S(1)}, u32[]{:S(2)}, u32[]{:S(2)}) collective-permute-start(f32[80,128]{1,0:T(8,128)S(1)} %add.30), channel_id=1, source_target_pairs={{0,4},{1,5},{2,6},{3,7},{4,0},{5,1},{6,2},{7,3},{8,12},{9,13},{10,... | collective-permute-start | bytes 122888 | tf_op jit(solution)/shard_map/ppermute | solution.py:372
  72.2 6.6 %collective-permute-start.9 = (f32[80,128]{1,0:T(8,128)S(1)}, f32[80,128]{1,0:T(8,128)S(1)}, u32[]{:S(2)}, u32[]{:S(2)}) collective-permute-start(f32[80,128]{1,0:T(8,128)S(1)} %add.30), channel_id=1, source_target_pairs={{0,2},{1,3},{2,4},{3,5},{4,6},{5,7},{6,0},{7,1},{8,10},{9,11},{10,... | collective-permute-start | bytes 122888 | tf_op jit(solution)/shard_map/ppermute | solution.py:372
  78.8 4.1 %collective-permute-start.14 = (f32[80,128]{1,0:T(8,128)S(1)}, f32[80,128]{1,0:T(8,128)S(1)}, u32[]{:S(2)}, u32[]{:S(2)}) collective-permute-start(f32[80,128]{1,0:T(8,128)S(1)} %add_add_fusion.2), channel_id=1, source_target_pairs={{0,24},{1,25},{2,26},{3,27},{4,28},{5,29},{6,30},{7,31},{8,0},{9,1... | collective-permute-start | bytes 122888 | tf_op jit(solution)/shard_map/ppermute | solution.py:372
  78.8 5.8 %collective-permute-start.13 = (f32[80,128]{1,0:T(8,128)S(1)}, f32[80,128]{1,0:T(8,128)S(1)}, u32[]{:S(2)}, u32[]{:S(2)}) collective-permute-start(f32[80,128]{1,0:T(8,128)S(1)} %add_add_fusion.2), channel_id=1, source_target_pairs={{0,16},{1,17},{2,18},{3,19},{4,20},{5,21},{6,22},{7,23},{8,24},{9,... | collective-permute-start | bytes 122888 | tf_op jit(solution)/shard_map/ppermute | solution.py:372
  78.9 6.6 %collective-permute-start.12 = (f32[80,128]{1,0:T(8,128)S(1)}, f32[80,128]{1,0:T(8,128)S(1)}, u32[]{:S(2)}, u32[]{:S(2)}) collective-permute-start(f32[80,128]{1,0:T(8,128)S(1)} %add_add_fusion.2), channel_id=1, source_target_pairs={{0,8},{1,9},{2,10},{3,11},{4,12},{5,13},{6,14},{7,15},{8,16},{9,17... | collective-permute-start | bytes 122888 | tf_op jit(solution)/shard_map/ppermute | solution.py:372
  85.5 7.2 %collective-permute-start.17 = (f32[80,128]{1,0:T(8,128)S(1)}, f32[80,128]{1,0:T(8,128)S(1)}, u32[]{:S(2)}, u32[]{:S(2)}) collective-permute-start(f32[80,128]{1,0:T(8,128)S(1)} %add_add_fusion.1), channel_id=1, source_target_pairs={{0,96},{1,97},{2,98},{3,99},{4,100},{5,101},{6,102},{7,103},{8,104... | collective-permute-start | bytes 122888 | tf_op jit(solution)/shard_map/ppermute | solution.py:372
  91.0 5.6 %collective-permute-start.16 = (f32[80,128]{1,0:T(8,128)S(1)}, f32[80,128]{1,0:T(8,128)S(1)}, u32[]{:S(2)}, u32[]{:S(2)}) collective-permute-start(f32[80,128]{1,0:T(8,128)S(1)} %add_add_fusion.1), channel_id=1, source_target_pairs={{0,64},{1,65},{2,66},{3,67},{4,68},{5,69},{6,70},{7,71},{8,72},{9,... | collective-permute-start | bytes 122888 | tf_op jit(solution)/shard_map/ppermute | solution.py:372
  91.0 5.7 %collective-permute-start.15 = (f32[80,128]{1,0:T(8,128)S(1)}, f32[80,128]{1,0:T(8,128)S(1)}, u32[]{:S(2)}, u32[]{:S(2)}) collective-permute-start(f32[80,128]{1,0:T(8,128)S(1)} %add_add_fusion.1), channel_id=1, source_target_pairs={{0,32},{1,33},{2,34},{3,35},{4,36},{5,37},{6,38},{7,39},{8,40},{9,... | collective-permute-start | bytes 122888 | tf_op jit(solution)/shard_map/ppermute | solution.py:372

commit v2 on v1

--- a/solution.py
+++ b/solution.py
@@ -64,14 +64,14 @@
     lax.fori_loop(0, half // 8, step, 0)
 
 
-def setup_kernel(index_ref, count_ref, ghost_ref, values_ref, start_ref,
+def setup_kernel(index_in, ghost_in, values_ref, start_in, count_ref,
                  tiles_ref, plan_ref, scale_ref, scaled_ref, send_a_ref, send_b_ref,
-                 acc_ref, sems):
+                 acc_ref, index_ref, ghost_ref, start_ref, sems):
     total, side = values_ref.shape[0], values_ref.shape[1]
     blocks = scaled_ref.shape[0]
     half = send_a_ref.shape[0]
     ghosts = 2 * half
-    chunks = sems.shape[0]
+    chunks = sems.shape[0] - 3
     per = total // chunks
 
     def copy(k):
@@ -79,8 +79,15 @@
             values_ref.at[pl.ds(k * per, per)], tiles_ref.at[pl.ds(k * per, per)], sems.at[k]
         )
 
+    small = [pltpu.make_async_copy(a, b, sems.at[chunks + i]) for i, (a, b) in enumerate(
+        ((index_in, index_ref), (ghost_in, ghost_ref), (start_in, start_ref)))]
+    for c in small[:2]:
+        c.start()
     for k in range(chunks):
         copy(k).start()
+    small[2].start()
+    for c in small[:2]:
+        c.wait()
 
     odd = lax.rem(lax.axis_index(AXIS), 2)
     flip = (1 - odd) * half
@@ -123,6 +130,8 @@
             if t >= ghosts:
                 target = jnp.where(t < count, target, blocks)
             acc_ref[target] += part
+
+    small[2].wait()
 
     def scale_step(base, _):
         for u in range(8):
@@ -225,29 +234,57 @@
 
 
 def inverse_factor(gram):
-    size = gram.shape[0]
-    row = lax.broadcasted_iota(jnp.int32, gram.shape, 0)
-    lane = lax.broadcasted_iota(jnp.int32, gram.shape, 1)
-    left, right = gram, jnp.where(row == lane, 1.0, 0.0)
-    row8 = lax.broadcasted_iota(jnp.int32, (8, 128), 0)
+    groups = gram.shape[0] // 8
+    full = (8, 128)
+    row8 = lax.broadcasted_iota(jnp.int32, full, 0)
+    lane = lax.broadcasted_iota(jnp.int32, full, 1)
+    left = [gram[8 * g:8 * g + 8] for g in range(groups)]
+    right = [jnp.where(lane == row8 + 8 * g, 1.0, 0.0) for g in range(groups)]
+
+    def across(value, at):
+        return jnp.broadcast_to(value[:, at:at + 1], full)
+
+    def down(value, at):
+        return jnp.broadcast_to(value[at:at + 1, :], full)
+
+    def column(entries):
+        out = jnp.zeros(full, F32)
+        for i, entry in entries:
+            out = jnp.where(row8 == i, entry, out)
+        return out
+
+    def combine(columns, value):
+        return sum(c * down(value, k) for k, c in enumerate(columns))
+
     done = []
-    for base in range(0, size, 8):
-        a, b = left[:8], right[:8]
+    for p in range(groups):
+        a, b = left[p], right[p]
+        spread = [across(a, 8 * p + k) for k in range(8)]
+        e = [[down(spread[k], i) for k in range(i + 1)] for i in range(8)]
+        scale = []
+        for k in range(8):
+            scale.append(lax.rsqrt(e[k][k]))
+            for i in range(k + 1, 8):
+                e[i][k] = e[i][k] * scale[k]
+            for i in range(k + 1, 8):
+                for j in range(k + 1, i + 1):
+                    e[i][j] = e[i][j] - e[i][k] * e[j][k]
+        m = [[None] * 8 for _ in range(8)]
         for j in range(8):
-            at = base + j
-            scale = lax.rsqrt(a[j:j + 1, at:at + 1])
-            line_a, line_b = a[j:j + 1] * scale, b[j:j + 1] * scale
-            column = jnp.where(row8 > j, a[:, at:at + 1] * scale, 0.0)
-            a = jnp.where(row8 == j, line_a, a - column * line_a)
-            b = jnp.where(row8 == j, line_b, b - column * line_b)
-        done.append(b)
-        if base + 8 < size:
-            both = jnp.concatenate([a, b], 1)
-            change = lax.dot_general(
-                a.T[base + 8:size], both, (((1,), (0,)), ((), ())),
-                precision=lax.Precision.HIGHEST, preferred_element_type=F32)
-            left = left[8:] - change[:, :128]
-            right = right[8:] - change[:, 128:]
+            m[j][j] = scale[j]
+            for i in range(j + 1, 8):
+                m[i][j] = -scale[i] * sum(e[i][k] * m[k][j] for k in range(j, i))
+        solve = [column([(i, m[i][k]) for i in range(k, 8)]) for k in range(8)]
+        ua, ub = combine(solve, a), combine(solve, b)
+        done.append(ub)
+        if p + 1 < groups:
+            back = [column([(k, m[i][k]) for k in range(i + 1)]) for i in range(8)]
+            wa, wb = combine(back, ua), combine(back, ub)
+            wa, wb = [down(wa, k) for k in range(8)], [down(wb, k) for k in range(8)]
+            for g in range(p + 1, groups):
+                factors = [across(left[g], 8 * p + k) for k in range(8)]
+                left[g] = left[g] - sum(f * w for f, w in zip(factors, wa))
+                right[g] = right[g] - sum(f * w for f, w in zip(factors, wb))
     return jnp.concatenate(done, 0)
 
 
@@ -315,12 +352,14 @@
         setup_kernel,
         out_shape=(shape((total, side, side), BF16), shape((8, 128), jnp.int32),
                    shape((blocks, 8, side), F32), scaled_t, send_t, send_t),
-        in_specs=[spec(SMEM), spec(SMEM), spec(SMEM), spec(pltpu.HBM), spec(VMEM)],
+        in_specs=[spec(pltpu.HBM)] * 4 + [spec(SMEM)],
         out_specs=(spec(VMEM), spec(SMEM), spec(VMEM), spec(VMEM), spec(VMEM), spec(VMEM)),
-        scratch_shapes=[VMEM((blocks + 1, 8, side), F32), pltpu.SemaphoreType.DMA((16,))],
+        scratch_shapes=[VMEM((blocks + 1, 8, side), F32), SMEM((2, total), jnp.int32),
+                        SMEM((2, half), jnp.int32), VMEM((width, rows), F32), pltpu.SemaphoreType.DMA((4 + 3,))],
         compiler_params=params(41),
         name="setup",
-    )(tile_index.T, tile_count, ghost_send[0], tile_values, start)
+    )(*[pltpu.with_memory_space_constraint(v, pltpu.HBM)
+        for v in (tile_index.T, ghost_send[0], tile_values, start)], tile_count)
 
     vectors = [start]
     parts = []

time: 109 us -> 99.1 us (0.909)
  Pallas kernels: 48.8 us -> 41.9 us
  local copies, waits for them, and re-layouts: 2.58 us -> 0.01 us
    pallas_call x1, Pallas kernels: 12 us -> 6.28 us  [body(): pl.pallas_call(functools.partial(final_kernel, rows * n), out_shape=(shap...]
    unnamed x6 -> x2, local copies, waits for them, and re-layouts: 2.58 us -> 0.01 us
    pallas_call x1, Pallas kernels: 8.54 us -> 7.22 us  [body(): pl.pallas_call(setup_kernel, out_shape=(shape((total, side, side), BF16),...]
  transfers between devices with their start and end apart: 18 -> 18, of which waited for: 9 -> 9; matrix products, arithmetic and copies ran while one was open for 0% -> 0% of each run, Pallas kernels for 17% -> 18%
where the time goes in v2:
time: 99.1 us; the launch traced here: 99 us
  Pallas kernels  41.9 us (42%)
  starting transfers between devices  40.3 us (41%)
  waiting for transfers between devices  15.2 us (15%)
  between operations  1.57 us (2%)
    ppermute x4, starting transfers between devices, body(): got_b = lax.ppermute(send_b, AXIS, far)  29.4 us
    pallas_call x4, Pallas kernels, body(): pl.pallas_call(functools.partial(own_kernel, level - 1), out_shape=(acc_t...  18.2 us
    ppermute x10, waiting for transfers between devices, phase(): moved = moved + lax.ppermute(value, AXIS, perm)  15.2 us
    ppermute x10, starting transfers between devices, phase(): moved = moved + lax.ppermute(value, AXIS, perm)  10.5 us
    pallas_call x4, Pallas kernels, body(): pl.pallas_call(functools.partial(far_kernel, level, last), out_shape=outs...  10.3 us
    pallas_call x1, Pallas kernels, body(): pl.pallas_call(setup_kernel, out_shape=(shape((total, side, side), BF16),...  7.22 us
    pallas_call x1, Pallas kernels, body(): pl.pallas_call(functools.partial(final_kernel, rows * n), out_shape=(shap...  6.28 us
  transfers between devices with their start and end apart: 18, of which 9 were waited for; matrix products, arithmetic and copies ran while one was open for 0% of the time, Pallas kernels for 18%

profile of v2, /device:TPU:0, one launch (start us, length us, event | category | flops | bytes accessed | tf_op | source)
XLA Modules:
  0.0 99.0 jit_solution(15588699495611029525)
XLA Ops:
  1.3 0.0 copy-start
  1.3 7.2 %setup.1 = (bf16[256,128,128]{2,1,0:T(8,128)(2,1)S(1)}, s32[8,128]{1,0:T(8,128)S(1)}, f32[128,8,128]{2,1,0:T(8,128)S(1)}, bf16[128,16,128]{2,1,0:T(8,128)(2,1)S(...) custom-call(s32[2,256]{1,0:T(2,128)} %bitcast.7, s32[2,64]{1,0:T(2,128)} %bitcast.8, ...), custom_call_target="tpu_custom_call" | custom-call | tf_op jit(solution)/shard_map/setup/pallas_call | solution.py:351
  8.5 0.1 collective-permute-start.1
  8.6 8.8 %collective-permute-start = (bf16[64,16,128]{2,1,0:T(8,128)(2,1)S(1)}, bf16[64,16,128]{2,1,0:T(8,128)(2,1)S(1)}, u32[]{:S(2)}, u32[]{:S(2)}) collective-permute-start(bf16[64,16,128]{2,1,0:T(8,128)(2,1)S(1)} %get-tuple-element.38), channel_id=1, source_target_pairs={{0,127},{1,2},{2,1},{3,4},{4,3},{5,6},{6,5},{7,8},{8,7},{9,10},{10... | collective-permute-start | bytes 786440 | tf_op jit(solution)/shard_map/ppermute | solution.py:369
  17.4 0.0 collective-permute-done.1.refs_3_
  17.4 0.0 copy-done
  17.4 4.2 %own.4 = (f32[129,16,128]{2,1,0:T(8,128)S(1)}, bf16[32,16384]{1,0:T(8,128)(2,1)S(1)}, f32[80,128]{1,0:T(8,128)S(1)}) custom-call(s32[8,128]{1,0:T(8,128)S(1)} %get-tuple-element.36.refs_0_, bf16[256,128,128]{2,1,0:T(8,128)(2,1)S(1)} %get-tuple-element.37.refs_1_, bf16[128,16,128]{2,1,0:T(8,128)(2,1)S(1)} %get-tuple-element.39.refs_2_, ...), custom_call_target="tpu_custom_call" | custom-call | flops 1000000000 | bytes 10000000 | tf_op jit(solution)/shard_map/own/pallas_call | solution.py:372
  21.6 0.0 collective-permute-done.refs_2_
  21.6 2.1 %far.4 = (f32[16,16384]{1,0:T(8,128)S(1)}, bf16[128,16,128]{2,1,0:T(8,128)(2,1)S(1)}, bf16[64,16,128]{2,1,0:T(8,128)(2,1)S(1)}, bf16[64,16,128]{2,1,0:T(8,128)(2,1)S(1)}, f32[129,16,128]{2,1,0:T(8,128)S(1)}) custom-call(s32[8,128]{1,0:T(8,128)S(1)} %get-tuple-element.36.refs_0_, ...), custom_call_target="tpu_custom_call", output_to_operand_aliasing={{4}: (3, {})} | custom-call | tf_op jit(solution)/shard_map/far/pallas_call | solution.py:390
  23.7 0.1 collective-permute-start.3
  23.8 7.1 %collective-permute-start.2 = (bf16[64,16,128]{2,1,0:T(8,128)(2,1)S(1)}, bf16[64,16,128]{2,1,0:T(8,128)(2,1)S(1)}, u32[]{:S(2)}, u32[]{:S(2)}) collective-permute-start(bf16[64,16,128]{2,1,0:T(8,128)(2,1)S(1)} %get-tuple-element.43), channel_id=1, source_target_pairs={{0,127},{1,2},{2,1},{3,4},{4,3},{5,6},{6,5},{7,8},{8,7},{9,10},{10... | collective-permute-start | bytes 786440 | tf_op jit(solution)/shard_map/ppermute | solution.py:369
  30.9 0.0 collective-permute-done.3.refs_3_
  30.9 4.2 %own.5 = (f32[129,16,128]{2,1,0:T(8,128)S(1)}, bf16[32,16384]{1,0:T(8,128)(2,1)S(1)}, f32[80,128]{1,0:T(8,128)S(1)}) custom-call(s32[8,128]{1,0:T(8,128)S(1)} %get-tuple-element.36.refs_0_, bf16[256,128,128]{2,1,0:T(8,128)(2,1)S(1)} %get-tuple-element.37.refs_1_, bf16[128,16,128]{2,1,0:T(8,128)(2,1)S(1)} %get-tuple-element.44.refs_2_, ...), custom_call_target="tpu_custom_call" | custom-call | flops 1000000000 | bytes 10000000 | tf_op jit(solution)/shard_map/own/pallas_call | solution.py:372
  35.2 0.0 collective-permute-done.2.refs_2_
  35.2 2.2 %far.5 = (f32[16,16384]{1,0:T(8,128)S(1)}, bf16[128,16,128]{2,1,0:T(8,128)(2,1)S(1)}, bf16[64,16,128]{2,1,0:T(8,128)(2,1)S(1)}, bf16[64,16,128]{2,1,0:T(8,128)(2,1)S(1)}, f32[129,16,128]{2,1,0:T(8,128)S(1)}) custom-call(s32[8,128]{1,0:T(8,128)S(1)} %get-tuple-element.36.refs_0_, ...), custom_call_target="tpu_custom_call", output_to_operand_aliasing={{4}: (3, {})} | custom-call | tf_op jit(solution)/shard_map/far/pallas_call | solution.py:390
  37.4 0.1 collective-permute-start.5
  37.5 7.0 %collective-permute-start.4 = (bf16[64,16,128]{2,1,0:T(8,128)(2,1)S(1)}, bf16[64,16,128]{2,1,0:T(8,128)(2,1)S(1)}, u32[]{:S(2)}, u32[]{:S(2)}) collective-permute-start(bf16[64,16,128]{2,1,0:T(8,128)(2,1)S(1)} %get-tuple-element.50), channel_id=1, source_target_pairs={{0,127},{1,2},{2,1},{3,4},{4,3},{5,6},{6,5},{7,8},{8,7},{9,10},{10... | collective-permute-start | bytes 786440 | tf_op jit(solution)/shard_map/ppermute | solution.py:369
  44.5 0.0 collective-permute-done.5.refs_3_
  44.5 4.8 %own.6 = (f32[129,16,128]{2,1,0:T(8,128)S(1)}, bf16[32,16384]{1,0:T(8,128)(2,1)S(1)}, f32[80,128]{1,0:T(8,128)S(1)}) custom-call(s32[8,128]{1,0:T(8,128)S(1)} %get-tuple-element.36.refs_0_, bf16[256,128,128]{2,1,0:T(8,128)(2,1)S(1)} %get-tuple-element.37.refs_1_, bf16[128,16,128]{2,1,0:T(8,128)(2,1)S(1)} %get-tuple-element.51.refs_2_, ...), custom_call_target="tpu_custom_call" | custom-call | flops 1000000000 | bytes 10000000 | tf_op jit(solution)/shard_map/own/pallas_call | solution.py:372
  49.3 0.0 collective-permute-done.4.refs_2_
  49.3 2.2 %far.6 = (f32[16,16384]{1,0:T(8,128)S(1)}, bf16[128,16,128]{2,1,0:T(8,128)(2,1)S(1)}, bf16[64,16,128]{2,1,0:T(8,128)(2,1)S(1)}, bf16[64,16,128]{2,1,0:T(8,128)(2,1)S(1)}, f32[129,16,128]{2,1,0:T(8,128)S(1)}) custom-call(s32[8,128]{1,0:T(8,128)S(1)} %get-tuple-element.36.refs_0_, ...), custom_call_target="tpu_custom_call", output_to_operand_aliasing={{4}: (3, {})} | custom-call | tf_op jit(solution)/shard_map/far/pallas_call | solution.py:390
  51.5 0.1 collective-permute-start.7
  51.6 6.5 %collective-permute-start.6 = (bf16[64,16,128]{2,1,0:T(8,128)(2,1)S(1)}, bf16[64,16,128]{2,1,0:T(8,128)(2,1)S(1)}, u32[]{:S(2)}, u32[]{:S(2)}) collective-permute-start(bf16[64,16,128]{2,1,0:T(8,128)(2,1)S(1)} %get-tuple-element.57), channel_id=1, source_target_pairs={{0,127},{1,2},{2,1},{3,4},{4,3},{5,6},{6,5},{7,8},{8,7},{9,10},{10... | collective-permute-start | bytes 786440 | tf_op jit(solution)/shard_map/ppermute | solution.py:369
  58.1 0.0 collective-permute-done.7.refs_3_
  58.1 5.0 %own.7 = (f32[129,16,128]{2,1,0:T(8,128)S(1)}, bf16[32,16384]{1,0:T(8,128)(2,1)S(1)}, f32[80,128]{1,0:T(8,128)S(1)}) custom-call(s32[8,128]{1,0:T(8,128)S(1)} %get-tuple-element.36.refs_0_, bf16[256,128,128]{2,1,0:T(8,128)(2,1)S(1)} %get-tuple-element.37.refs_1_, bf16[128,16,128]{2,1,0:T(8,128)(2,1)S(1)} %get-tuple-element.58.refs_2_, ...), custom_call_target="tpu_custom_call" | custom-call | flops 1000000000 | bytes 10000000 | tf_op jit(solution)/shard_map/own/pallas_call | solution.py:372
  63.1 0.0 collective-permute-done.6.refs_2_
  63.1 3.7 %far.7 = (bf16[32,16384]{1,0:T(8,128)(2,1)S(1)}, f32[80,128]{1,0:T(8,128)S(1)}, f32[129,16,128]{2,1,0:T(8,128)S(1)}) custom-call(s32[8,128]{1,0:T(8,128)S(1)} %get-tuple-element.36.refs_0_, bf16[256,128,128]{2,1,0:T(8,128)(2,1)S(1)} %get-tuple-element.37.refs_1_, ...), custom_call_target="tpu_custom_call", output_to_operand_aliasing={{2}: (3, {})} | custom-call | tf_op jit(solution)/shard_map/far/pallas_call | solution.py:390
  66.8 0.0 collective-permute-start.8
  66.9 1.2 %collective-permute-done.8 = f32[80,128]{1,0:T(8,128)S(1)} collective-permute-done((f32[80,128]{1,0:T(8,128)S(1)}, f32[80,128]{1,0:T(8,128)S(1)}, u32[]{:S(2)}, u32[]{:S(2)}) %collective-permute-start.8) | collective-permute-done | bytes 40992 | tf_op jit(solution)/shard_map/ppermute | solution.py:411
  68.1 0.0 collective-permute-start.11
  68.1 0.3 collective-permute-start.10
  68.4 1.7 %collective-permute-start.9 = (f32[80,128]{1,0:T(8,128)S(1)}, f32[80,128]{1,0:T(8,128)S(1)}, u32[]{:S(2)}, u32[]{:S(2)}) collective-permute-start(f32[80,128]{1,0:T(8,128)S(1)} %add.30), channel_id=1, source_target_pairs={{0,2},{1,3},{2,4},{3,5},{4,6},{5,7},{6,0},{7,1},{8,10},{9,11},{10,... | collective-permute-start | bytes 122888 | tf_op jit(solution)/shard_map/ppermute | solution.py:411
  70.1 2.0 %collective-permute-done.11 = f32[80,128]{1,0:T(8,128)S(1)} collective-permute-done((f32[80,128]{1,0:T(8,128)S(1)}, f32[80,128]{1,0:T(8,128)S(1)}, u32[]{:S(2)}, u32[]{:S(2)}) %collective-permute-start.11) | collective-permute-done | bytes 40992 | tf_op jit(solution)/shard_map/ppermute | solution.py:411
  72.2 1.8 %collective-permute-done.10 = f32[80,128]{1,0:T(8,128)S(1)} collective-permute-done((f32[80,128]{1,0:T(8,128)S(1)}, f32[80,128]{1,0:T(8,128)S(1)}, u32[]{:S(2)}, u32[]{:S(2)}) %collective-permute-start.10) | collective-permute-done | bytes 40992 | tf_op jit(solution)/shard_map/ppermute | solution.py:411
  74.0 0.8 collective-permute-done.9
  74.8 0.1 collective-permute-start.14
  74.9 0.1 collective-permute-start.13
  75.0 1.9 %collective-permute-start.12 = (f32[80,128]{1,0:T(8,128)S(1)}, f32[80,128]{1,0:T(8,128)S(1)}, u32[]{:S(2)}, u32[]{:S(2)}) collective-permute-start(f32[80,128]{1,0:T(8,128)S(1)} %add_add_fusion.2), channel_id=1, source_target_pairs={{0,8},{1,9},{2,10},{3,11},{4,12},{5,13},{6,14},{7,15},{8,16},{9,17... | collective-permute-start | bytes 122888 | tf_op jit(solution)/shard_map/ppermute | solution.py:411
  76.9 2.0 %collective-permute-done.14 = f32[80,128]{1,0:T(8,128)S(1)} collective-permute-done((f32[80,128]{1,0:T(8,128)S(1)}, f32[80,128]{1,0:T(8,128)S(1)}, u32[]{:S(2)}, u32[]{:S(2)}) %collective-permute-start.14) | collective-permute-done | bytes 40992 | tf_op jit(solution)/shard_map/ppermute | solution.py:411
  78.9 1.8 %collective-permute-done.13 = f32[80,128]{1,0:T(8,128)S(1)} collective-permute-done((f32[80,128]{1,0:T(8,128)S(1)}, f32[80,128]{1,0:T(8,128)S(1)}, u32[]{:S(2)}, u32[]{:S(2)}) %collective-permute-start.13) | collective-permute-done | bytes 40992 | tf_op jit(solution)/shard_map/ppermute | solution.py:411
  80.7 0.9 collective-permute-done.12
  81.5 5.4 %collective-permute-start.17 = (f32[80,128]{1,0:T(8,128)S(1)}, f32[80,128]{1,0:T(8,128)S(1)}, u32[]{:S(2)}, u32[]{:S(2)}) collective-permute-start(f32[80,128]{1,0:T(8,128)S(1)} %add_add_fusion.1), channel_id=1, source_target_pairs={{0,96},{1,97},{2,98},{3,99},{4,100},{5,101},{6,102},{7,103},{8,104... | collective-permute-start | bytes 122888 | tf_op jit(solution)/shard_map/ppermute | solution.py:411
  86.9 0.0 collective-permute-start.16
  86.9 0.9 collective-permute-start.15
  87.9 0.7 collective-permute-done.17
  88.6 3.9 %collective-permute-done.16 = f32[80,128]{1,0:T(8,128)S(1)} collective-permute-done((f32[80,128]{1,0:T(8,128)S(1)}, f32[80,128]{1,0:T(8,128)S(1)}, u32[]{:S(2)}, u32[]{:S(2)}) %collective-permute-start.16) | collective-permute-done | bytes 40992 | tf_op jit(solution)/shard_map/ppermute | solution.py:411
  92.5 0.0 collective-permute-done.15
  92.6 6.3 %final.1 = (f32[80,16384]{1,0:T(8,128)}, f32[80,80]{1,0:T(8,128)}) custom-call(f32[80,128]{1,0:T(8,128)S(1)} %add_add_fusion.gram_in, bf16[32,16384]{1,0:T(8,128)(2,1)S(1)} %get-tuple-element.47.refs_5_.refs_6_.refs_0_, bf16[32,16384]{1,0:T(8,128)(2,1)S(1)} %get-tuple-element.54.refs_6_.refs_7_.refs_1_, ...), custom_call_target="tpu_custom_call" | custom-call | tf_op jit(solution)/shard_map/final/pallas_call | solution.py:418
  (4 shorter events, 0.0 us)
Async XLA Ops:
  1.3 16.1 %copy-start = (f32[16384,16]{0,1:T(8,128)S(1)}, f32[16384,16]{0,1:T(8,128)}, u32[]{:S(2)}) copy-start(f32[16384,16]{0,1:T(8,128)} %param.5) | copy-start | bytes 3145732
  8.5 8.9 %collective-permute-start.1 = (bf16[64,16,128]{2,1,0:T(8,128)(2,1)S(1)}, bf16[64,16,128]{2,1,0:T(8,128)(2,1)S(1)}, u32[]{:S(2)}, u32[]{:S(2)}) collective-permute-start(bf16[64,16,128]{2,1,0:T(8,128)(2,1)S(1)} %get-tuple-element.40), channel_id=1, source_target_pairs={{0,1},{1,0},{2,3},{3,2},{4,5},{5,4},{6,7},{7,6},{8,9},{9,8},{10,11... | collective-permute-start | bytes 786440 | tf_op jit(solution)/shard_map/ppermute | solution.py:370
  8.6 13.0 %collective-permute-start = (bf16[64,16,128]{2,1,0:T(8,128)(2,1)S(1)}, bf16[64,16,128]{2,1,0:T(8,128)(2,1)S(1)}, u32[]{:S(2)}, u32[]{:S(2)}) collective-permute-start(bf16[64,16,128]{2,1,0:T(8,128)(2,1)S(1)} %get-tuple-element.38), channel_id=1, source_target_pairs={{0,127},{1,2},{2,1},{3,4},{4,3},{5,6},{6,5},{7,8},{8,7},{9,10},{10... | collective-permute-start | bytes 786440 | tf_op jit(solution)/shard_map/ppermute | solution.py:369
  23.7 7.2 %collective-permute-start.3 = (bf16[64,16,128]{2,1,0:T(8,128)(2,1)S(1)}, bf16[64,16,128]{2,1,0:T(8,128)(2,1)S(1)}, u32[]{:S(2)}, u32[]{:S(2)}) collective-permute-start(bf16[64,16,128]{2,1,0:T(8,128)(2,1)S(1)} %get-tuple-element.45), channel_id=1, source_target_pairs={{0,1},{1,0},{2,3},{3,2},{4,5},{5,4},{6,7},{7,6},{8,9},{9,8},{10,11... | collective-permute-start | bytes 786440 | tf_op jit(solution)/shard_map/ppermute | solution.py:370
  23.8 11.4 %collective-permute-start.2 = (bf16[64,16,128]{2,1,0:T(8,128)(2,1)S(1)}, bf16[64,16,128]{2,1,0:T(8,128)(2,1)S(1)}, u32[]{:S(2)}, u32[]{:S(2)}) collective-permute-start(bf16[64,16,128]{2,1,0:T(8,128)(2,1)S(1)} %get-tuple-element.43), channel_id=1, source_target_pairs={{0,127},{1,2},{2,1},{3,4},{4,3},{5,6},{6,5},{7,8},{8,7},{9,10},{10... | collective-permute-start | bytes 786440 | tf_op jit(solution)/shard_map/ppermute | solution.py:369
  37.4 7.1 %collective-permute-start.5 = (bf16[64,16,128]{2,1,0:T(8,128)(2,1)S(1)}, bf16[64,16,128]{2,1,0:T(8,128)(2,1)S(1)}, u32[]{:S(2)}, u32[]{:S(2)}) collective-permute-start(bf16[64,16,128]{2,1,0:T(8,128)(2,1)S(1)} %get-tuple-element.52), channel_id=1, source_target_pairs={{0,1},{1,0},{2,3},{3,2},{4,5},{5,4},{6,7},{7,6},{8,9},{9,8},{10,11... | collective-permute-start | bytes 786440 | tf_op jit(solution)/shard_map/ppermute | solution.py:370
  37.5 11.8 %collective-permute-start.4 = (bf16[64,16,128]{2,1,0:T(8,128)(2,1)S(1)}, bf16[64,16,128]{2,1,0:T(8,128)(2,1)S(1)}, u32[]{:S(2)}, u32[]{:S(2)}) collective-permute-start(bf16[64,16,128]{2,1,0:T(8,128)(2,1)S(1)} %get-tuple-element.50), channel_id=1, source_target_pairs={{0,127},{1,2},{2,1},{3,4},{4,3},{5,6},{6,5},{7,8},{8,7},{9,10},{10... | collective-permute-start | bytes 786440 | tf_op jit(solution)/shard_map/ppermute | solution.py:369
  51.5 6.6 %collective-permute-start.7 = (bf16[64,16,128]{2,1,0:T(8,128)(2,1)S(1)}, bf16[64,16,128]{2,1,0:T(8,128)(2,1)S(1)}, u32[]{:S(2)}, u32[]{:S(2)}) collective-permute-start(bf16[64,16,128]{2,1,0:T(8,128)(2,1)S(1)} %get-tuple-element.59), channel_id=1, source_target_pairs={{0,1},{1,0},{2,3},{3,2},{4,5},{5,4},{6,7},{7,6},{8,9},{9,8},{10,11... | collective-permute-start | bytes 786440 | tf_op jit(solution)/shard_map/ppermute | solution.py:370
  51.6 11.5 %collective-permute-start.6 = (bf16[64,16,128]{2,1,0:T(8,128)(2,1)S(1)}, bf16[64,16,128]{2,1,0:T(8,128)(2,1)S(1)}, u32[]{:S(2)}, u32[]{:S(2)}) collective-permute-start(bf16[64,16,128]{2,1,0:T(8,128)(2,1)S(1)} %get-tuple-element.57), channel_id=1, source_target_pairs={{0,127},{1,2},{2,1},{3,4},{4,3},{5,6},{6,5},{7,8},{8,7},{9,10},{10... | collective-permute-start | bytes 786440 | tf_op jit(solution)/shard_map/ppermute | solution.py:369
  66.8 1.3 %collective-permute-start.8 = (f32[80,128]{1,0:T(8,128)S(1)}, f32[80,128]{1,0:T(8,128)S(1)}, u32[]{:S(2)}, u32[]{:S(2)}) collective-permute-start(f32[80,128]{1,0:T(8,128)S(1)} %get-tuple-element.66), channel_id=1, source_target_pairs={{0,1},{1,0},{2,3},{3,2},{4,5},{5,4},{6,7},{7,6},{8,9},{9,8},{10,11... | collective-permute-start | bytes 122888 | tf_op jit(solution)/shard_map/ppermute | solution.py:411
  68.1 4.1 %collective-permute-start.11 = (f32[80,128]{1,0:T(8,128)S(1)}, f32[80,128]{1,0:T(8,128)S(1)}, u32[]{:S(2)}, u32[]{:S(2)}) collective-permute-start(f32[80,128]{1,0:T(8,128)S(1)} %add.30), channel_id=1, source_target_pairs={{0,6},{1,7},{2,0},{3,1},{4,2},{5,3},{6,4},{7,5},{8,14},{9,15},{10,... | collective-permute-start | bytes 122888 | tf_op jit(solution)/shard_map/ppermute | solution.py:411
  68.1 5.9 %collective-permute-start.10 = (f32[80,128]{1,0:T(8,128)S(1)}, f32[80,128]{1,0:T(8,128)S(1)}, u32[]{:S(2)}, u32[]{:S(2)}) collective-permute-start(f32[80,128]{1,0:T(8,128)S(1)} %add.30), channel_id=1, source_target_pairs={{0,4},{1,5},{2,6},{3,7},{4,0},{5,1},{6,2},{7,3},{8,12},{9,13},{10,... | collective-permute-start | bytes 122888 | tf_op jit(solution)/shard_map/ppermute | solution.py:411
  68.4 6.4 %collective-permute-start.9 = (f32[80,128]{1,0:T(8,128)S(1)}, f32[80,128]{1,0:T(8,128)S(1)}, u32[]{:S(2)}, u32[]{:S(2)}) collective-permute-start(f32[80,128]{1,0:T(8,128)S(1)} %add.30), channel_id=1, source_target_pairs={{0,2},{1,3},{2,4},{3,5},{4,6},{5,7},{6,0},{7,1},{8,10},{9,11},{10,... | collective-permute-start | bytes 122888 | tf_op jit(solution)/shard_map/ppermute | solution.py:411
  74.8 4.1 %collective-permute-start.14 = (f32[80,128]{1,0:T(8,128)S(1)}, f32[80,128]{1,0:T(8,128)S(1)}, u32[]{:S(2)}, u32[]{:S(2)}) collective-permute-start(f32[80,128]{1,0:T(8,128)S(1)} %add_add_fusion.2), channel_id=1, source_target_pairs={{0,24},{1,25},{2,26},{3,27},{4,28},{5,29},{6,30},{7,31},{8,0},{9,1... | collective-permute-start | bytes 122888 | tf_op jit(solution)/shard_map/ppermute | solution.py:411
  74.9 5.8 %collective-permute-start.13 = (f32[80,128]{1,0:T(8,128)S(1)}, f32[80,128]{1,0:T(8,128)S(1)}, u32[]{:S(2)}, u32[]{:S(2)}) collective-permute-start(f32[80,128]{1,0:T(8,128)S(1)} %add_add_fusion.2), channel_id=1, source_target_pairs={{0,16},{1,17},{2,18},{3,19},{4,20},{5,21},{6,22},{7,23},{8,24},{9,... | collective-permute-start | bytes 122888 | tf_op jit(solution)/shard_map/ppermute | solution.py:411
  75.0 6.6 %collective-permute-start.12 = (f32[80,128]{1,0:T(8,128)S(1)}, f32[80,128]{1,0:T(8,128)S(1)}, u32[]{:S(2)}, u32[]{:S(2)}) collective-permute-start(f32[80,128]{1,0:T(8,128)S(1)} %add_add_fusion.2), channel_id=1, source_target_pairs={{0,8},{1,9},{2,10},{3,11},{4,12},{5,13},{6,14},{7,15},{8,16},{9,17... | collective-permute-start | bytes 122888 | tf_op jit(solution)/shard_map/ppermute | solution.py:411
  81.5 7.1 %collective-permute-start.17 = (f32[80,128]{1,0:T(8,128)S(1)}, f32[80,128]{1,0:T(8,128)S(1)}, u32[]{:S(2)}, u32[]{:S(2)}) collective-permute-start(f32[80,128]{1,0:T(8,128)S(1)} %add_add_fusion.1), channel_id=1, source_target_pairs={{0,96},{1,97},{2,98},{3,99},{4,100},{5,101},{6,102},{7,103},{8,104... | collective-permute-start | bytes 122888 | tf_op jit(solution)/shard_map/ppermute | solution.py:411
  86.9 5.6 %collective-permute-start.16 = (f32[80,128]{1,0:T(8,128)S(1)}, f32[80,128]{1,0:T(8,128)S(1)}, u32[]{:S(2)}, u32[]{:S(2)}) collective-permute-start(f32[80,128]{1,0:T(8,128)S(1)} %add_add_fusion.1), channel_id=1, source_target_pairs={{0,64},{1,65},{2,66},{3,67},{4,68},{5,69},{6,70},{7,71},{8,72},{9,... | collective-permute-start | bytes 122888 | tf_op jit(solution)/shard_map/ppermute | solution.py:411
  86.9 5.7 %collective-permute-start.15 = (f32[80,128]{1,0:T(8,128)S(1)}, f32[80,128]{1,0:T(8,128)S(1)}, u32[]{:S(2)}, u32[]{:S(2)}) collective-permute-start(f32[80,128]{1,0:T(8,128)S(1)} %add_add_fusion.1), channel_id=1, source_target_pairs={{0,32},{1,33},{2,34},{3,35},{4,36},{5,37},{6,38},{7,39},{8,40},{9,... | collective-permute-start | bytes 122888 | tf_op jit(solution)/shard_map/ppermute | solution.py:411

commit v3 on v2

--- a/solution.py
+++ b/solution.py
@@ -15,6 +15,7 @@
 BF16 = jnp.bfloat16
 
 SLOT, GROW, OCOL, OROW, SEND = range(5)
+LIST = 128
 
 
 def spec(space):
@@ -55,10 +56,10 @@
     def step(base, _):
         for u in range(8):
             g = base * 8 + u
-            send_b_ref[g] = scaled_ref[plan_ref[SEND, half + g]]
+            send_b_ref[g] = scaled_ref[plan_ref[SEND * LIST + half + g]]
         for u in range(8):
             g = base * 8 + u
-            send_a_ref[g] = scaled_ref[plan_ref[SEND, g]]
+            send_a_ref[g] = scaled_ref[plan_ref[SEND * LIST + g]]
         return 0
 
     lax.fori_loop(0, half // 8, step, 0)
@@ -98,17 +99,17 @@
         for u in range(4):
             t = base * 4 + u
             place = jnp.bitwise_xor(index_ref[1, t] - blocks, flip)
-            plan_ref[SLOT, place] = t
-            plan_ref[GROW, place] = index_ref[0, t]
-            plan_ref[OCOL, t] = index_ref[1, ghosts + t]
-            plan_ref[OROW, t] = jnp.where(ghosts + t < count, index_ref[0, ghosts + t], blocks)
+            plan_ref[SLOT * LIST + place] = t
+            plan_ref[GROW * LIST + place] = index_ref[0, t]
+            plan_ref[OCOL * LIST + t] = index_ref[1, ghosts + t]
+            plan_ref[OROW * LIST + t] = jnp.where(ghosts + t < count, index_ref[0, ghosts + t], blocks)
         return 0
 
     lax.fori_loop(0, ghosts // 4, ghost_plan, 0)
 
     def send_plan(g, _):
-        plan_ref[SEND, g] = ghost_ref[odd, g]
-        plan_ref[SEND, half + g] = ghost_ref[1 - odd, g]
+        plan_ref[SEND * LIST + g] = ghost_ref[odd, g]
+        plan_ref[SEND * LIST + half + g] = ghost_ref[1 - odd, g]
         return 0
 
     lax.fori_loop(0, half, send_plan, 0)
@@ -155,13 +156,17 @@
     rows = parts[0].shape[1]
     chunk = 1024
     width = 16 * (level + 1)
-    acc = jnp.zeros((32, 2 * width), F32)
+    acc = jnp.zeros((2 * width, 32), F32)
     for k in range(rows // chunk):
         at = slice(k * chunk, (k + 1) * chunk)
         right = jnp.concatenate([p[:16, at] for p in parts] + [p[16:, at] for p in parts], 0)
-        acc += lax.dot_general(parts[-1][:, at], right, (((1,), (1,)), ((), ())), preferred_element_type=F32)
-    both = acc[:16] + acc[16:]
-    gram_ref[16 * level:16 * (level + 1), :width] = both[:, :width] + both[:, width:]
+        acc += lax.dot_general(right, parts[-1][:, at], (((1,), (1,)), ((), ())), preferred_element_type=F32)
+    acc = jnp.concatenate([acc, jnp.zeros((2 * width, 96), F32)], 1)
+    if 2 * width % 128:
+        acc = jnp.concatenate([acc, jnp.zeros(((-2 * width) % 128, 128), F32)], 0)
+    acc = acc.T
+    both = acc[:16] + acc[16:32]
+    gram_ref[16 * level:16 * (level + 1), :width] = both[:, :width] + both[:, width:2 * width]
 
 
 def own_kernel(level, *refs):
@@ -177,10 +182,10 @@
     acc_ref[...] = jnp.zeros_like(acc_ref)
     ghosts = 2 * half
 
-    spread_tiles(ghosts, 32, acc_ref, lambda t: scaled_ref[plan_ref[OCOL, t]],
-                 lambda t: tiles_ref[ghosts + t], lambda t: plan_ref[OROW, t])
+    spread_tiles(ghosts, 32, acc_ref, lambda t: scaled_ref[plan_ref[OCOL * LIST + t]],
+                 lambda t: tiles_ref[ghosts + t], lambda t: plan_ref[OROW * LIST + t])
     spread_tiles(half, 32, acc_ref, lambda g: got_ref[g],
-                 lambda g: tiles_ref[plan_ref[SLOT, g]], lambda g: plan_ref[GROW, g])
+                 lambda g: tiles_ref[plan_ref[SLOT * LIST + g]], lambda g: plan_ref[GROW * LIST + g])
     high, low = split(vec_ref[...])
     part_ref[:16] = high
     part_ref[16:] = low
@@ -206,7 +211,7 @@
     side = tiles_ref.shape[1]
     blocks = scale_ref.shape[0]
     spread_tiles(half, 32, acc_ref, lambda g: got_ref[g],
-                 lambda g: tiles_ref[plan_ref[SLOT, half + g]], lambda g: plan_ref[GROW, half + g])
+                 lambda g: tiles_ref[plan_ref[SLOT * LIST + half + g]], lambda g: plan_ref[GROW * LIST + half + g])
 
     def close_step(base, _):
         for u in range(8):
@@ -350,7 +355,7 @@
     start = start_vectors.T
     tiles, plan, scale, scaled, send_a, send_b = pl.pallas_call(
         setup_kernel,
-        out_shape=(shape((total, side, side), BF16), shape((8, 128), jnp.int32),
+        out_shape=(shape((total, side, side), BF16), SMEM((5 * LIST,), jnp.int32),
                    shape((blocks, 8, side), F32), scaled_t, send_t, send_t),
         in_specs=[spec(pltpu.HBM)] * 4 + [spec(SMEM)],
         out_specs=(spec(VMEM), spec(SMEM), spec(VMEM), spec(VMEM), spec(VMEM), spec(VMEM)),

time: 99.1 us -> 94.8 us (0.957)
  Pallas kernels: 41.9 us -> 34.2 us
  starting transfers between devices: 40.3 us -> 42.3 us
  waiting for transfers between devices: 15.2 us -> 16.5 us
    pallas_call x4, Pallas kernels: 18.2 us -> 15 us  [body(): pl.pallas_call(functools.partial(own_kernel, level - 1), out_shape=(acc_t...]
    pallas_call x4, Pallas kernels: 10.3 us -> 7.08 us  [body(): pl.pallas_call(functools.partial(far_kernel, level, last), out_shape=outs...]
    pallas_call x1, Pallas kernels: 7.22 us -> 5.85 us  [body(): pl.pallas_call(setup_kernel, out_shape=(shape((total, side, side), BF16),...]
    ppermute x4, waiting for transfers between devices: 0.01 us -> 1.32 us  [body(): got_b = lax.ppermute(send_b, AXIS, far)]
    ppermute x4, starting transfers between devices: 29.4 us -> 30.6 us  [body(): got_b = lax.ppermute(send_b, AXIS, far)]
  transfers between devices with their start and end apart: 18 -> 18, of which waited for: 9 -> 12; matrix products, arithmetic and copies ran while one was open for 0% -> 0% of each run, Pallas kernels for 18% -> 16%
where the time goes in v3:
time: 94.8 us; the launch traced here: 94.7 us
  starting transfers between devices  42.3 us (45%)
  Pallas kernels  34.2 us (36%)
  waiting for transfers between devices  16.5 us (17%)
  between operations  1.57 us (2%)
    ppermute x4, starting transfers between devices, body(): got_b = lax.ppermute(send_b, AXIS, far)  30.6 us
    ppermute x10, waiting for transfers between devices, phase(): moved = moved + lax.ppermute(value, AXIS, perm)  15.2 us
    pallas_call x4, Pallas kernels, body(): pl.pallas_call(functools.partial(own_kernel, level - 1), out_shape=(acc_t...  15 us
    ppermute x10, starting transfers between devices, phase(): moved = moved + lax.ppermute(value, AXIS, perm)  11.4 us
    pallas_call x4, Pallas kernels, body(): pl.pallas_call(functools.partial(far_kernel, level, last), out_shape=outs...  7.08 us
    pallas_call x1, Pallas kernels, body(): pl.pallas_call(functools.partial(final_kernel, rows * n), out_shape=(shap...  6.27 us
    pallas_call x1, Pallas kernels, body(): pl.pallas_call(setup_kernel, out_shape=(shape((total, side, side), BF16),...  5.85 us
  transfers between devices with their start and end apart: 18, of which 12 were waited for; matrix products, arithmetic and copies ran while one was open for 0% of the time, Pallas kernels for 16%

profile of v3, /device:TPU:0, one launch (start us, length us, event | category | flops | bytes accessed | tf_op | source)
XLA Modules:
  0.0 94.7 jit_solution(18395640065490515579)
XLA Ops:
  1.3 0.0 copy-start
  1.3 5.9 %setup.1 = (bf16[256,128,128]{2,1,0:T(8,128)(2,1)S(1)}, s32[640]{0:T(1024)S(4)}, f32[128,8,128]{2,1,0:T(8,128)S(1)}, bf16[128,16,128]{2,1,0:T(8,128)(2,1)S(1)}, ...) custom-call(s32[2,256]{1,0:T(2,128)} %bitcast.7, s32[2,64]{1,0:T(2,128)} %bitcast.8, ...), custom_call_target="tpu_custom_call" | custom-call | tf_op jit(solution)/shard_map/setup/pallas_call | solution.py:356
  7.1 0.1 collective-permute-start.1
  7.2 8.9 %collective-permute-start = (bf16[64,16,128]{2,1,0:T(8,128)(2,1)S(1)}, bf16[64,16,128]{2,1,0:T(8,128)(2,1)S(1)}, u32[]{:S(2)}, u32[]{:S(2)}) collective-permute-start(bf16[64,16,128]{2,1,0:T(8,128)(2,1)S(1)} %get-tuple-element.38), channel_id=1, source_target_pairs={{0,127},{1,2},{2,1},{3,4},{4,3},{5,6},{6,5},{7,8},{8,7},{9,10},{10... | collective-permute-start | bytes 786440 | tf_op jit(solution)/shard_map/ppermute | solution.py:374
  16.1 0.0 collective-permute-done.1.refs_3_
  16.1 0.0 copy-done
  16.1 3.3 %own.4 = (f32[129,16,128]{2,1,0:T(8,128)S(1)}, bf16[32,16384]{1,0:T(8,128)(2,1)S(1)}, f32[80,128]{1,0:T(8,128)S(1)}) custom-call(s32[640]{0:T(1024)S(4)} %get-tuple-element.36.refs_0_, bf16[256,128,128]{2,1,0:T(8,128)(2,1)S(1)} %get-tuple-element.37.refs_1_, bf16[128,16,128]{2,1,0:T(8,128)(2,1)S(1)} %get-tuple-element.39.refs_2_, ...), custom_call_target="tpu_custom_call" | custom-call | flops 1000000000 | bytes 10000000 | tf_op jit(solution)/shard_map/own/pallas_call | solution.py:377
  19.5 0.7 collective-permute-done.refs_2_
  20.2 1.3 %far.4 = (f32[16,16384]{1,0:T(8,128)S(1)}, bf16[128,16,128]{2,1,0:T(8,128)(2,1)S(1)}, bf16[64,16,128]{2,1,0:T(8,128)(2,1)S(1)}, bf16[64,16,128]{2,1,0:T(8,128)(2,1)S(1)}, f32[129,16,128]{2,1,0:T(8,128)S(1)}) custom-call(s32[640]{0:T(1024)S(4)} %get-tuple-element.36.refs_0_, ...), custom_call_target="tpu_custom_call", output_to_operand_aliasing={{4}: (3, {})} | custom-call | tf_op jit(solution)/shard_map/far/pallas_call | solution.py:395
  21.5 0.1 collective-permute-start.3
  21.6 7.3 %collective-permute-start.2 = (bf16[64,16,128]{2,1,0:T(8,128)(2,1)S(1)}, bf16[64,16,128]{2,1,0:T(8,128)(2,1)S(1)}, u32[]{:S(2)}, u32[]{:S(2)}) collective-permute-start(bf16[64,16,128]{2,1,0:T(8,128)(2,1)S(1)} %get-tuple-element.43), channel_id=1, source_target_pairs={{0,127},{1,2},{2,1},{3,4},{4,3},{5,6},{6,5},{7,8},{8,7},{9,10},{10... | collective-permute-start | bytes 786440 | tf_op jit(solution)/shard_map/ppermute | solution.py:374
  28.9 0.0 collective-permute-done.3.refs_3_
  28.9 3.6 %own.5 = (f32[129,16,128]{2,1,0:T(8,128)S(1)}, bf16[32,16384]{1,0:T(8,128)(2,1)S(1)}, f32[80,128]{1,0:T(8,128)S(1)}) custom-call(s32[640]{0:T(1024)S(4)} %get-tuple-element.36.refs_0_, bf16[256,128,128]{2,1,0:T(8,128)(2,1)S(1)} %get-tuple-element.37.refs_1_, bf16[128,16,128]{2,1,0:T(8,128)(2,1)S(1)} %get-tuple-element.44.refs_2_, ...), custom_call_target="tpu_custom_call" | custom-call | flops 1000000000 | bytes 10000000 | tf_op jit(solution)/shard_map/own/pallas_call | solution.py:377
  32.5 0.4 collective-permute-done.2.refs_2_
  32.9 1.4 %far.5 = (f32[16,16384]{1,0:T(8,128)S(1)}, bf16[128,16,128]{2,1,0:T(8,128)(2,1)S(1)}, bf16[64,16,128]{2,1,0:T(8,128)(2,1)S(1)}, bf16[64,16,128]{2,1,0:T(8,128)(2,1)S(1)}, f32[129,16,128]{2,1,0:T(8,128)S(1)}) custom-call(s32[640]{0:T(1024)S(4)} %get-tuple-element.36.refs_0_, ...), custom_call_target="tpu_custom_call", output_to_operand_aliasing={{4}: (3, {})} | custom-call | tf_op jit(solution)/shard_map/far/pallas_call | solution.py:395
  34.4 0.1 collective-permute-start.5
  34.5 7.3 %collective-permute-start.4 = (bf16[64,16,128]{2,1,0:T(8,128)(2,1)S(1)}, bf16[64,16,128]{2,1,0:T(8,128)(2,1)S(1)}, u32[]{:S(2)}, u32[]{:S(2)}) collective-permute-start(bf16[64,16,128]{2,1,0:T(8,128)(2,1)S(1)} %get-tuple-element.50), channel_id=1, source_target_pairs={{0,127},{1,2},{2,1},{3,4},{4,3},{5,6},{6,5},{7,8},{8,7},{9,10},{10... | collective-permute-start | bytes 786440 | tf_op jit(solution)/shard_map/ppermute | solution.py:374
  41.7 0.0 collective-permute-done.5.refs_3_
  41.7 3.9 %own.6 = (f32[129,16,128]{2,1,0:T(8,128)S(1)}, bf16[32,16384]{1,0:T(8,128)(2,1)S(1)}, f32[80,128]{1,0:T(8,128)S(1)}) custom-call(s32[640]{0:T(1024)S(4)} %get-tuple-element.36.refs_0_, bf16[256,128,128]{2,1,0:T(8,128)(2,1)S(1)} %get-tuple-element.37.refs_1_, bf16[128,16,128]{2,1,0:T(8,128)(2,1)S(1)} %get-tuple-element.51.refs_2_, ...), custom_call_target="tpu_custom_call" | custom-call | flops 1000000000 | bytes 10000000 | tf_op jit(solution)/shard_map/own/pallas_call | solution.py:377
  45.6 0.2 collective-permute-done.4.refs_2_
  45.8 1.4 %far.6 = (f32[16,16384]{1,0:T(8,128)S(1)}, bf16[128,16,128]{2,1,0:T(8,128)(2,1)S(1)}, bf16[64,16,128]{2,1,0:T(8,128)(2,1)S(1)}, bf16[64,16,128]{2,1,0:T(8,128)(2,1)S(1)}, f32[129,16,128]{2,1,0:T(8,128)S(1)}) custom-call(s32[640]{0:T(1024)S(4)} %get-tuple-element.36.refs_0_, ...), custom_call_target="tpu_custom_call", output_to_operand_aliasing={{4}: (3, {})} | custom-call | tf_op jit(solution)/shard_map/far/pallas_call | solution.py:395
  47.2 0.1 collective-permute-start.7
  47.3 7.3 %collective-permute-start.6 = (bf16[64,16,128]{2,1,0:T(8,128)(2,1)S(1)}, bf16[64,16,128]{2,1,0:T(8,128)(2,1)S(1)}, u32[]{:S(2)}, u32[]{:S(2)}) collective-permute-start(bf16[64,16,128]{2,1,0:T(8,128)(2,1)S(1)} %get-tuple-element.57), channel_id=1, source_target_pairs={{0,127},{1,2},{2,1},{3,4},{4,3},{5,6},{6,5},{7,8},{8,7},{9,10},{10... | collective-permute-start | bytes 786440 | tf_op jit(solution)/shard_map/ppermute | solution.py:374
  54.5 0.0 collective-permute-done.7.refs_3_
  54.5 4.1 %own.7 = (f32[129,16,128]{2,1,0:T(8,128)S(1)}, bf16[32,16384]{1,0:T(8,128)(2,1)S(1)}, f32[80,128]{1,0:T(8,128)S(1)}) custom-call(s32[640]{0:T(1024)S(4)} %get-tuple-element.36.refs_0_, bf16[256,128,128]{2,1,0:T(8,128)(2,1)S(1)} %get-tuple-element.37.refs_1_, bf16[128,16,128]{2,1,0:T(8,128)(2,1)S(1)} %get-tuple-element.58.refs_2_, ...), custom_call_target="tpu_custom_call" | custom-call | flops 1000000000 | bytes 10000000 | tf_op jit(solution)/shard_map/own/pallas_call | solution.py:377
  58.7 0.0 collective-permute-done.6.refs_2_
  58.7 2.9 %far.7 = (bf16[32,16384]{1,0:T(8,128)(2,1)S(1)}, f32[80,128]{1,0:T(8,128)S(1)}, f32[129,16,128]{2,1,0:T(8,128)S(1)}) custom-call(s32[640]{0:T(1024)S(4)} %get-tuple-element.36.refs_0_, bf16[256,128,128]{2,1,0:T(8,128)(2,1)S(1)} %get-tuple-element.37.refs_1_, ...), custom_call_target="tpu_custom_call", output_to_operand_aliasing={{2}: (3, {})} | custom-call | tf_op jit(solution)/shard_map/far/pallas_call | solution.py:395
  61.6 0.1 collective-permute-start.8
  61.6 1.2 %collective-permute-done.8 = f32[80,128]{1,0:T(8,128)S(1)} collective-permute-done((f32[80,128]{1,0:T(8,128)S(1)}, f32[80,128]{1,0:T(8,128)S(1)}, u32[]{:S(2)}, u32[]{:S(2)}) %collective-permute-start.8) | collective-permute-done | bytes 40992 | tf_op jit(solution)/shard_map/ppermute | solution.py:416
  62.9 0.0 collective-permute-start.11
  62.9 0.3 collective-permute-start.10
  63.1 1.7 %collective-permute-start.9 = (f32[80,128]{1,0:T(8,128)S(1)}, f32[80,128]{1,0:T(8,128)S(1)}, u32[]{:S(2)}, u32[]{:S(2)}) collective-permute-start(f32[80,128]{1,0:T(8,128)S(1)} %add.30), channel_id=1, source_target_pairs={{0,2},{1,3},{2,4},{3,5},{4,6},{5,7},{6,0},{7,1},{8,10},{9,11},{10,... | collective-permute-start | bytes 122888 | tf_op jit(solution)/shard_map/ppermute | solution.py:416
  64.9 2.0 %collective-permute-done.11 = f32[80,128]{1,0:T(8,128)S(1)} collective-permute-done((f32[80,128]{1,0:T(8,128)S(1)}, f32[80,128]{1,0:T(8,128)S(1)}, u32[]{:S(2)}, u32[]{:S(2)}) %collective-permute-start.11) | collective-permute-done | bytes 40992 | tf_op jit(solution)/shard_map/ppermute | solution.py:416
  66.9 1.8 %collective-permute-done.10 = f32[80,128]{1,0:T(8,128)S(1)} collective-permute-done((f32[80,128]{1,0:T(8,128)S(1)}, f32[80,128]{1,0:T(8,128)S(1)}, u32[]{:S(2)}, u32[]{:S(2)}) %collective-permute-start.10) | collective-permute-done | bytes 40992 | tf_op jit(solution)/shard_map/ppermute | solution.py:416
  68.7 0.8 collective-permute-done.9
  69.6 0.1 collective-permute-start.14
  69.6 0.1 collective-permute-start.13
  69.7 1.9 %collective-permute-start.12 = (f32[80,128]{1,0:T(8,128)S(1)}, f32[80,128]{1,0:T(8,128)S(1)}, u32[]{:S(2)}, u32[]{:S(2)}) collective-permute-start(f32[80,128]{1,0:T(8,128)S(1)} %add_add_fusion.2), channel_id=1, source_target_pairs={{0,8},{1,9},{2,10},{3,11},{4,12},{5,13},{6,14},{7,15},{8,16},{9,17... | collective-permute-start | bytes 122888 | tf_op jit(solution)/shard_map/ppermute | solution.py:416
  71.7 2.0 %collective-permute-done.14 = f32[80,128]{1,0:T(8,128)S(1)} collective-permute-done((f32[80,128]{1,0:T(8,128)S(1)}, f32[80,128]{1,0:T(8,128)S(1)}, u32[]{:S(2)}, u32[]{:S(2)}) %collective-permute-start.14) | collective-permute-done | bytes 40992 | tf_op jit(solution)/shard_map/ppermute | solution.py:416
  73.6 1.8 %collective-permute-done.13 = f32[80,128]{1,0:T(8,128)S(1)} collective-permute-done((f32[80,128]{1,0:T(8,128)S(1)}, f32[80,128]{1,0:T(8,128)S(1)}, u32[]{:S(2)}, u32[]{:S(2)}) %collective-permute-start.13) | collective-permute-done | bytes 40992 | tf_op jit(solution)/shard_map/ppermute | solution.py:416
  75.4 0.9 collective-permute-done.12
  76.3 6.3 %collective-permute-start.17 = (f32[80,128]{1,0:T(8,128)S(1)}, f32[80,128]{1,0:T(8,128)S(1)}, u32[]{:S(2)}, u32[]{:S(2)}) collective-permute-start(f32[80,128]{1,0:T(8,128)S(1)} %add_add_fusion.1), channel_id=1, source_target_pairs={{0,96},{1,97},{2,98},{3,99},{4,100},{5,101},{6,102},{7,103},{8,104... | collective-permute-start | bytes 122888 | tf_op jit(solution)/shard_map/ppermute | solution.py:416
  82.6 0.0 collective-permute-start.16
  82.6 0.9 %collective-permute-start.15 = (f32[80,128]{1,0:T(8,128)S(1)}, f32[80,128]{1,0:T(8,128)S(1)}, u32[]{:S(2)}, u32[]{:S(2)}) collective-permute-start(f32[80,128]{1,0:T(8,128)S(1)} %add_add_fusion.1), channel_id=1, source_target_pairs={{0,32},{1,33},{2,34},{3,35},{4,36},{5,37},{6,38},{7,39},{8,40},{9,... | collective-permute-start | bytes 122888 | tf_op jit(solution)/shard_map/ppermute | solution.py:416
  83.5 0.7 collective-permute-done.17
  84.3 3.9 %collective-permute-done.16 = f32[80,128]{1,0:T(8,128)S(1)} collective-permute-done((f32[80,128]{1,0:T(8,128)S(1)}, f32[80,128]{1,0:T(8,128)S(1)}, u32[]{:S(2)}, u32[]{:S(2)}) %collective-permute-start.16) | collective-permute-done | bytes 40992 | tf_op jit(solution)/shard_map/ppermute | solution.py:416
  88.2 0.0 collective-permute-done.15
  88.2 6.3 %final.1 = (f32[80,16384]{1,0:T(8,128)}, f32[80,80]{1,0:T(8,128)}) custom-call(f32[80,128]{1,0:T(8,128)S(1)} %add_add_fusion.gram_in, bf16[32,16384]{1,0:T(8,128)(2,1)S(1)} %get-tuple-element.47.refs_5_.refs_6_.refs_0_, bf16[32,16384]{1,0:T(8,128)(2,1)S(1)} %get-tuple-element.54.refs_6_.refs_7_.refs_1_, ...), custom_call_target="tpu_custom_call" | custom-call | tf_op jit(solution)/shard_map/final/pallas_call | solution.py:423
  (4 shorter events, 0.0 us)
Async XLA Ops:
  1.3 14.9 %copy-start = (f32[16384,16]{0,1:T(8,128)S(1)}, f32[16384,16]{0,1:T(8,128)}, u32[]{:S(2)}) copy-start(f32[16384,16]{0,1:T(8,128)} %param.5) | copy-start | bytes 3145732
  7.1 9.0 %collective-permute-start.1 = (bf16[64,16,128]{2,1,0:T(8,128)(2,1)S(1)}, bf16[64,16,128]{2,1,0:T(8,128)(2,1)S(1)}, u32[]{:S(2)}, u32[]{:S(2)}) collective-permute-start(bf16[64,16,128]{2,1,0:T(8,128)(2,1)S(1)} %get-tuple-element.40), channel_id=1, source_target_pairs={{0,1},{1,0},{2,3},{3,2},{4,5},{5,4},{6,7},{7,6},{8,9},{9,8},{10,11... | collective-permute-start | bytes 786440 | tf_op jit(solution)/shard_map/ppermute | solution.py:375
  7.2 12.9 %collective-permute-start = (bf16[64,16,128]{2,1,0:T(8,128)(2,1)S(1)}, bf16[64,16,128]{2,1,0:T(8,128)(2,1)S(1)}, u32[]{:S(2)}, u32[]{:S(2)}) collective-permute-start(bf16[64,16,128]{2,1,0:T(8,128)(2,1)S(1)} %get-tuple-element.38), channel_id=1, source_target_pairs={{0,127},{1,2},{2,1},{3,4},{4,3},{5,6},{6,5},{7,8},{8,7},{9,10},{10... | collective-permute-start | bytes 786440 | tf_op jit(solution)/shard_map/ppermute | solution.py:374
  21.5 7.3 %collective-permute-start.3 = (bf16[64,16,128]{2,1,0:T(8,128)(2,1)S(1)}, bf16[64,16,128]{2,1,0:T(8,128)(2,1)S(1)}, u32[]{:S(2)}, u32[]{:S(2)}) collective-permute-start(bf16[64,16,128]{2,1,0:T(8,128)(2,1)S(1)} %get-tuple-element.45), channel_id=1, source_target_pairs={{0,1},{1,0},{2,3},{3,2},{4,5},{5,4},{6,7},{7,6},{8,9},{9,8},{10,11... | collective-permute-start | bytes 786440 | tf_op jit(solution)/shard_map/ppermute | solution.py:375
  21.6 11.3 %collective-permute-start.2 = (bf16[64,16,128]{2,1,0:T(8,128)(2,1)S(1)}, bf16[64,16,128]{2,1,0:T(8,128)(2,1)S(1)}, u32[]{:S(2)}, u32[]{:S(2)}) collective-permute-start(bf16[64,16,128]{2,1,0:T(8,128)(2,1)S(1)} %get-tuple-element.43), channel_id=1, source_target_pairs={{0,127},{1,2},{2,1},{3,4},{4,3},{5,6},{6,5},{7,8},{8,7},{9,10},{10... | collective-permute-start | bytes 786440 | tf_op jit(solution)/shard_map/ppermute | solution.py:374
  34.4 7.3 %collective-permute-start.5 = (bf16[64,16,128]{2,1,0:T(8,128)(2,1)S(1)}, bf16[64,16,128]{2,1,0:T(8,128)(2,1)S(1)}, u32[]{:S(2)}, u32[]{:S(2)}) collective-permute-start(bf16[64,16,128]{2,1,0:T(8,128)(2,1)S(1)} %get-tuple-element.52), channel_id=1, source_target_pairs={{0,1},{1,0},{2,3},{3,2},{4,5},{5,4},{6,7},{7,6},{8,9},{9,8},{10,11... | collective-permute-start | bytes 786440 | tf_op jit(solution)/shard_map/ppermute | solution.py:375
  34.5 11.3 %collective-permute-start.4 = (bf16[64,16,128]{2,1,0:T(8,128)(2,1)S(1)}, bf16[64,16,128]{2,1,0:T(8,128)(2,1)S(1)}, u32[]{:S(2)}, u32[]{:S(2)}) collective-permute-start(bf16[64,16,128]{2,1,0:T(8,128)(2,1)S(1)} %get-tuple-element.50), channel_id=1, source_target_pairs={{0,127},{1,2},{2,1},{3,4},{4,3},{5,6},{6,5},{7,8},{8,7},{9,10},{10... | collective-permute-start | bytes 786440 | tf_op jit(solution)/shard_map/ppermute | solution.py:374
  47.2 7.3 %collective-permute-start.7 = (bf16[64,16,128]{2,1,0:T(8,128)(2,1)S(1)}, bf16[64,16,128]{2,1,0:T(8,128)(2,1)S(1)}, u32[]{:S(2)}, u32[]{:S(2)}) collective-permute-start(bf16[64,16,128]{2,1,0:T(8,128)(2,1)S(1)} %get-tuple-element.59), channel_id=1, source_target_pairs={{0,1},{1,0},{2,3},{3,2},{4,5},{5,4},{6,7},{7,6},{8,9},{9,8},{10,11... | collective-permute-start | bytes 786440 | tf_op jit(solution)/shard_map/ppermute | solution.py:375
  47.3 11.4 %collective-permute-start.6 = (bf16[64,16,128]{2,1,0:T(8,128)(2,1)S(1)}, bf16[64,16,128]{2,1,0:T(8,128)(2,1)S(1)}, u32[]{:S(2)}, u32[]{:S(2)}) collective-permute-start(bf16[64,16,128]{2,1,0:T(8,128)(2,1)S(1)} %get-tuple-element.57), channel_id=1, source_target_pairs={{0,127},{1,2},{2,1},{3,4},{4,3},{5,6},{6,5},{7,8},{8,7},{9,10},{10... | collective-permute-start | bytes 786440 | tf_op jit(solution)/shard_map/ppermute | solution.py:374
  61.6 1.3 %collective-permute-start.8 = (f32[80,128]{1,0:T(8,128)S(1)}, f32[80,128]{1,0:T(8,128)S(1)}, u32[]{:S(2)}, u32[]{:S(2)}) collective-permute-start(f32[80,128]{1,0:T(8,128)S(1)} %get-tuple-element.66), channel_id=1, source_target_pairs={{0,1},{1,0},{2,3},{3,2},{4,5},{5,4},{6,7},{7,6},{8,9},{9,8},{10,11... | collective-permute-start | bytes 122888 | tf_op jit(solution)/shard_map/ppermute | solution.py:416
  62.9 4.1 %collective-permute-start.11 = (f32[80,128]{1,0:T(8,128)S(1)}, f32[80,128]{1,0:T(8,128)S(1)}, u32[]{:S(2)}, u32[]{:S(2)}) collective-permute-start(f32[80,128]{1,0:T(8,128)S(1)} %add.30), channel_id=1, source_target_pairs={{0,6},{1,7},{2,0},{3,1},{4,2},{5,3},{6,4},{7,5},{8,14},{9,15},{10,... | collective-permute-start | bytes 122888 | tf_op jit(solution)/shard_map/ppermute | solution.py:416
  62.9 5.9 %collective-permute-start.10 = (f32[80,128]{1,0:T(8,128)S(1)}, f32[80,128]{1,0:T(8,128)S(1)}, u32[]{:S(2)}, u32[]{:S(2)}) collective-permute-start(f32[80,128]{1,0:T(8,128)S(1)} %add.30), channel_id=1, source_target_pairs={{0,4},{1,5},{2,6},{3,7},{4,0},{5,1},{6,2},{7,3},{8,12},{9,13},{10,... | collective-permute-start | bytes 122888 | tf_op jit(solution)/shard_map/ppermute | solution.py:416
  63.1 6.4 %collective-permute-start.9 = (f32[80,128]{1,0:T(8,128)S(1)}, f32[80,128]{1,0:T(8,128)S(1)}, u32[]{:S(2)}, u32[]{:S(2)}) collective-permute-start(f32[80,128]{1,0:T(8,128)S(1)} %add.30), channel_id=1, source_target_pairs={{0,2},{1,3},{2,4},{3,5},{4,6},{5,7},{6,0},{7,1},{8,10},{9,11},{10,... | collective-permute-start | bytes 122888 | tf_op jit(solution)/shard_map/ppermute | solution.py:416
  69.6 4.1 %collective-permute-start.14 = (f32[80,128]{1,0:T(8,128)S(1)}, f32[80,128]{1,0:T(8,128)S(1)}, u32[]{:S(2)}, u32[]{:S(2)}) collective-permute-start(f32[80,128]{1,0:T(8,128)S(1)} %add_add_fusion.2), channel_id=1, source_target_pairs={{0,24},{1,25},{2,26},{3,27},{4,28},{5,29},{6,30},{7,31},{8,0},{9,1... | collective-permute-start | bytes 122888 | tf_op jit(solution)/shard_map/ppermute | solution.py:416
  69.6 5.8 %collective-permute-start.13 = (f32[80,128]{1,0:T(8,128)S(1)}, f32[80,128]{1,0:T(8,128)S(1)}, u32[]{:S(2)}, u32[]{:S(2)}) collective-permute-start(f32[80,128]{1,0:T(8,128)S(1)} %add_add_fusion.2), channel_id=1, source_target_pairs={{0,16},{1,17},{2,18},{3,19},{4,20},{5,21},{6,22},{7,23},{8,24},{9,... | collective-permute-start | bytes 122888 | tf_op jit(solution)/shard_map/ppermute | solution.py:416
  69.7 6.6 %collective-permute-start.12 = (f32[80,128]{1,0:T(8,128)S(1)}, f32[80,128]{1,0:T(8,128)S(1)}, u32[]{:S(2)}, u32[]{:S(2)}) collective-permute-start(f32[80,128]{1,0:T(8,128)S(1)} %add_add_fusion.2), channel_id=1, source_target_pairs={{0,8},{1,9},{2,10},{3,11},{4,12},{5,13},{6,14},{7,15},{8,16},{9,17... | collective-permute-start | bytes 122888 | tf_op jit(solution)/shard_map/ppermute | solution.py:416
  76.3 7.9 %collective-permute-start.17 = (f32[80,128]{1,0:T(8,128)S(1)}, f32[80,128]{1,0:T(8,128)S(1)}, u32[]{:S(2)}, u32[]{:S(2)}) collective-permute-start(f32[80,128]{1,0:T(8,128)S(1)} %add_add_fusion.1), channel_id=1, source_target_pairs={{0,96},{1,97},{2,98},{3,99},{4,100},{5,101},{6,102},{7,103},{8,104... | collective-permute-start | bytes 122888 | tf_op jit(solution)/shard_map/ppermute | solution.py:416
  82.6 5.6 %collective-permute-start.16 = (f32[80,128]{1,0:T(8,128)S(1)}, f32[80,128]{1,0:T(8,128)S(1)}, u32[]{:S(2)}, u32[]{:S(2)}) collective-permute-start(f32[80,128]{1,0:T(8,128)S(1)} %add_add_fusion.1), channel_id=1, source_target_pairs={{0,64},{1,65},{2,66},{3,67},{4,68},{5,69},{6,70},{7,71},{8,72},{9,... | collective-permute-start | bytes 122888 | tf_op jit(solution)/shard_map/ppermute | solution.py:416
  82.6 5.7 %collective-permute-start.15 = (f32[80,128]{1,0:T(8,128)S(1)}, f32[80,128]{1,0:T(8,128)S(1)}, u32[]{:S(2)}, u32[]{:S(2)}) collective-permute-start(f32[80,128]{1,0:T(8,128)S(1)} %add_add_fusion.1), channel_id=1, source_target_pairs={{0,32},{1,33},{2,34},{3,35},{4,36},{5,37},{6,38},{7,39},{8,40},{9,... | collective-permute-start | bytes 122888 | tf_op jit(solution)/shard_map/ppermute | solution.py:416

commit v4 on v3

--- a/solution.py
+++ b/solution.py
@@ -16,6 +16,7 @@
 
 SLOT, GROW, OCOL, OROW, SEND = range(5)
 LIST = 128
+CHUNKS = (0, 128, 256)
 
 
 def spec(space):
@@ -72,13 +73,11 @@
     blocks = scaled_ref.shape[0]
     half = send_a_ref.shape[0]
     ghosts = 2 * half
-    chunks = sems.shape[0] - 3
-    per = total // chunks
+    chunks = len(CHUNKS) - 1
 
     def copy(k):
-        return pltpu.make_async_copy(
-            values_ref.at[pl.ds(k * per, per)], tiles_ref.at[pl.ds(k * per, per)], sems.at[k]
-        )
+        at = pl.ds(CHUNKS[k], CHUNKS[k + 1] - CHUNKS[k])
+        return pltpu.make_async_copy(values_ref.at[at], tiles_ref.at[at], sems.at[k])
 
     small = [pltpu.make_async_copy(a, b, sems.at[chunks + i]) for i, (a, b) in enumerate(
         ((index_in, index_ref), (ghost_in, ghost_ref), (start_in, start_ref)))]
@@ -120,9 +119,9 @@
     join = jnp.concatenate
     for k in range(chunks):
         copy(k).wait()
-        slots = [k * per + u for u in range(per)]
+        slots = list(range(CHUNKS[k], CHUNKS[k + 1]))
         got = []
-        for i in range(0, per, 4):
+        for i in range(0, len(slots), 4):
             t = [tiles_ref[slot] for slot in slots[i:i + 4]]
             sums = tile_product(ones, join([join([t[0], t[1]], 1), join([t[2], t[3]], 1)], 0))
             got += [sums[:8, :side], sums[8:, :side], sums[:8, side:], sums[8:, side:]]
@@ -152,21 +151,29 @@
     return high, (value - high.astype(F32)).astype(BF16)
 
 
-def gram_rows(parts, gram_ref, level):
+def gram_place(level):
+    width = 16 * (level + 1)
+    first = {4: 0, 2: 80, 3: 128, 1: 192, 0: 224}[level]
+    return slice(first, first + width)
+
+
+def gram_rows(parts, gram_ref, level, prepare):
     rows = parts[0].shape[1]
     chunk = 1024
     width = 16 * (level + 1)
     acc = jnp.zeros((2 * width, 32), F32)
     for k in range(rows // chunk):
         at = slice(k * chunk, (k + 1) * chunk)
-        right = jnp.concatenate([p[:16, at] for p in parts] + [p[16:, at] for p in parts], 0)
-        acc += lax.dot_general(right, parts[-1][:, at], (((1,), (1,)), ((), ())), preferred_element_type=F32)
+        last = prepare(at)
+        right = jnp.concatenate([p[:16, at] for p in parts[:-1]] + [last[:16]]
+                                + [p[16:, at] for p in parts[:-1]] + [last[16:]], 0)
+        acc += lax.dot_general(right, last, (((1,), (1,)), ((), ())), preferred_element_type=F32)
     acc = jnp.concatenate([acc, jnp.zeros((2 * width, 96), F32)], 1)
     if 2 * width % 128:
         acc = jnp.concatenate([acc, jnp.zeros(((-2 * width) % 128, 128), F32)], 0)
     acc = acc.T
     both = acc[:16] + acc[16:32]
-    gram_ref[16 * level:16 * (level + 1), :width] = both[:, :width] + both[:, width:2 * width]
+    gram_ref[:, gram_place(level)] = both[:, :width] + both[:, width:2 * width]
 
 
 def own_kernel(level, *refs):
@@ -186,11 +193,14 @@
                  lambda t: tiles_ref[ghosts + t], lambda t: plan_ref[OROW * LIST + t])
     spread_tiles(half, 32, acc_ref, lambda g: got_ref[g],
                  lambda g: tiles_ref[plan_ref[SLOT * LIST + g]], lambda g: plan_ref[GROW * LIST + g])
-    high, low = split(vec_ref[...])
-    part_ref[:16] = high
-    part_ref[16:] = low
     gram_ref[...] = gram_in[...] if level else jnp.zeros_like(gram_ref)
-    gram_rows(tuple(older) + (part_ref,), gram_ref, level)
+
+    def prepare(where):
+        stacked = jnp.concatenate(split(vec_ref[:, where]), 0)
+        part_ref[:, where] = stacked
+        return stacked
+
+    gram_rows(tuple(older) + (part_ref,), gram_ref, level, prepare)
 
 
 def far_kernel(level, last, *refs):
@@ -213,29 +223,37 @@
     spread_tiles(half, 32, acc_ref, lambda g: got_ref[g],
                  lambda g: tiles_ref[plan_ref[SLOT * LIST + half + g]], lambda g: plan_ref[GROW * LIST + half + g])
 
+    def close(b, where):
+        factor = jnp.concatenate([scale_ref[b], scale_ref[b]], 0)
+        value = factor * acc_ref[b]
+        if level > 1:
+            value = 2.0 * value - prev_ref[:, where]
+        return factor, value
+
+    if last:
+        def prepare(where):
+            values = []
+            for first in range(where.start, where.stop, side):
+                values.append(close(first // side, slice(first, first + side))[1])
+            stacked = jnp.concatenate(split(jnp.concatenate(values, 1)), 0)
+            part_ref[:, where] = stacked
+            return stacked
+
+        gram_ref[...] = gram_in[...]
+        gram_rows(tuple(older) + (part_ref,), gram_ref, level, prepare)
+        return
+
     def close_step(base, _):
         for u in range(8):
             b = base * 8 + u
             where = pl.ds(pl.multiple_of(b * side, side), side)
-            factor = jnp.concatenate([scale_ref[b], scale_ref[b]], 0)
-            value = factor * acc_ref[b]
-            if level > 1:
-                value = 2.0 * value - prev_ref[:, where]
-            if last:
-                high, low = split(value)
-                part_ref[:16, where] = high
-                part_ref[16:, where] = low
-            else:
-                vec_ref[:, where] = value
-                scaled_ref[b] = (factor * value).astype(BF16)
+            factor, value = close(b, where)
+            vec_ref[:, where] = value
+            scaled_ref[b] = (factor * value).astype(BF16)
         return 0
 
     lax.fori_loop(0, blocks // 8, close_step, 0)
-    if last:
-        gram_ref[...] = gram_in[...]
-        gram_rows(tuple(older) + (part_ref,), gram_ref, level)
-    else:
-        pack(plan_ref, scaled_ref, send_a_ref, send_b_ref)
+    pack(plan_ref, scaled_ref, send_a_ref, send_b_ref)
 
 
 def inverse_factor(gram):
@@ -299,7 +317,9 @@
     width = gram_ref.shape[0]
 
     if True:
-        lower = gram_in[...] * (1.0 / row_total)
+        groups = [gram_in[:, gram_place(k)] * (1.0 / row_total) for k in range(STEPS + 1)]
+        lower = jnp.concatenate(
+            [jnp.concatenate([g, jnp.zeros((16, 128 - g.shape[1]), F32)], 1) for g in groups], 0)
         row = lax.broadcasted_iota(jnp.int32, lower.shape, 0)
         lane = lax.broadcasted_iota(jnp.int32, lower.shape, 1)
         lower = jnp.where(row >= lane, lower, 0.0)
@@ -347,7 +367,7 @@
     vec_t = shape((width, rows), F32)
     part_t = shape((2 * width, rows), BF16)
     acc_t = shape((blocks + 1, width, side), F32)
-    gram_t = shape((basis, 128), F32)
+    gram_t = shape((16, 256), F32)
 
     near = [(i, i ^ 1) for i in range(n)]
     far = [(i, (i + 1) % n if i % 2 else (i - 1) % n) for i in range(n)]
@@ -360,7 +380,7 @@
         in_specs=[spec(pltpu.HBM)] * 4 + [spec(SMEM)],
         out_specs=(spec(VMEM), spec(SMEM), spec(VMEM), spec(VMEM), spec(VMEM), spec(VMEM)),
         scratch_shapes=[VMEM((blocks + 1, 8, side), F32), SMEM((2, total), jnp.int32),
-                        SMEM((2, half), jnp.int32), VMEM((width, rows), F32), pltpu.SemaphoreType.DMA((4 + 3,))],
+                        SMEM((2, half), jnp.int32), VMEM((width, rows), F32), pltpu.SemaphoreType.DMA((len(CHUNKS) + 2,))],
         compiler_params=params(41),
         name="setup",
     )(*[pltpu.with_memory_space_constraint(v, pltpu.HBM)

time: 94.8 us -> 93.1 us (0.982)
  waiting for transfers between devices: 16.5 us -> 15 us
    ppermute x10, waiting for transfers between devices: 15.2 us -> 14.2 us  [phase(): moved = moved + lax.ppermute(value, AXIS, perm)]
  transfers between devices with their start and end apart: 18 -> 18, of which waited for: 12 -> 11; matrix products, arithmetic and copies ran while one was open for 0% -> 0% of each run, Pallas kernels for 16% -> 17%
where the time goes in v4:
time: 93.1 us; the launch traced here: 93 us
  starting transfers between devices  41.9 us (45%)
  Pallas kernels  34.4 us (37%)
  waiting for transfers between devices  15 us (16%)
  between operations  1.56 us (2%)
    ppermute x4, starting transfers between devices, body(): got_b = lax.ppermute(send_b, AXIS, far)  30.6 us
    pallas_call x4, Pallas kernels, body(): pl.pallas_call(functools.partial(own_kernel, level - 1), out_shape=(acc_t...  15.6 us
    ppermute x10, waiting for transfers between devices, phase(): moved = moved + lax.ppermute(value, AXIS, perm)  14.2 us
    ppermute x10, starting transfers between devices, phase(): moved = moved + lax.ppermute(value, AXIS, perm)  11 us
    pallas_call x4, Pallas kernels, body(): pl.pallas_call(functools.partial(far_kernel, level, last), out_shape=outs...  6.69 us
    pallas_call x1, Pallas kernels, body(): pl.pallas_call(functools.partial(final_kernel, rows * n), out_shape=(shap...  6.35 us
    pallas_call x1, Pallas kernels, body(): pl.pallas_call(setup_kernel, out_shape=(shape((total, side, side), BF16),...  5.74 us
  transfers between devices with their start and end apart: 18, of which 11 were waited for; matrix products, arithmetic and copies ran while one was open for 0% of the time, Pallas kernels for 17%

profile of v4, /device:TPU:0, one launch (start us, length us, event | category | flops | bytes accessed | tf_op | source)
XLA Modules:
  0.0 93.0 jit_solution(12654561557901232811)
XLA Ops:
  1.3 0.0 copy-start
  1.3 5.7 %setup.1 = (bf16[256,128,128]{2,1,0:T(8,128)(2,1)S(1)}, s32[640]{0:T(1024)S(4)}, f32[128,8,128]{2,1,0:T(8,128)S(1)}, bf16[128,16,128]{2,1,0:T(8,128)(2,1)S(1)}, ...) custom-call(s32[2,256]{1,0:T(2,128)} %bitcast.7, s32[2,64]{1,0:T(2,128)} %bitcast.8, ...), custom_call_target="tpu_custom_call" | custom-call | tf_op jit(solution)/shard_map/setup/pallas_call | solution.py:376
  7.0 0.1 collective-permute-start.1
  7.1 8.9 %collective-permute-start = (bf16[64,16,128]{2,1,0:T(8,128)(2,1)S(1)}, bf16[64,16,128]{2,1,0:T(8,128)(2,1)S(1)}, u32[]{:S(2)}, u32[]{:S(2)}) collective-permute-start(bf16[64,16,128]{2,1,0:T(8,128)(2,1)S(1)} %get-tuple-element.38), channel_id=1, source_target_pairs={{0,127},{1,2},{2,1},{3,4},{4,3},{5,6},{6,5},{7,8},{8,7},{9,10},{10... | collective-permute-start | bytes 786440 | tf_op jit(solution)/shard_map/ppermute | solution.py:394
  16.0 0.0 collective-permute-done.1.refs_3_
  16.0 0.0 copy-done
  16.0 3.5 %own.4 = (f32[129,16,128]{2,1,0:T(8,128)S(1)}, bf16[32,16384]{1,0:T(8,128)(2,1)S(1)}, f32[16,256]{1,0:T(8,128)S(1)}) custom-call(s32[640]{0:T(1024)S(4)} %get-tuple-element.36.refs_0_, bf16[256,128,128]{2,1,0:T(8,128)(2,1)S(1)} %get-tuple-element.37.refs_1_, bf16[128,16,128]{2,1,0:T(8,128)(2,1)S(1)} %get-tuple-element.39.refs_2_, ...), custom_call_target="tpu_custom_call" | custom-call | flops 1000000000 | bytes 10000000 | tf_op jit(solution)/shard_map/own/pallas_call | solution.py:397
  19.5 0.5 collective-permute-done.refs_2_
  20.1 1.3 %far.4 = (f32[16,16384]{1,0:T(8,128)S(1)}, bf16[128,16,128]{2,1,0:T(8,128)(2,1)S(1)}, bf16[64,16,128]{2,1,0:T(8,128)(2,1)S(1)}, bf16[64,16,128]{2,1,0:T(8,128)(2,1)S(1)}, f32[129,16,128]{2,1,0:T(8,128)S(1)}) custom-call(s32[640]{0:T(1024)S(4)} %get-tuple-element.36.refs_0_, ...), custom_call_target="tpu_custom_call", output_to_operand_aliasing={{4}: (3, {})} | custom-call | tf_op jit(solution)/shard_map/far/pallas_call | solution.py:415
  21.4 0.1 collective-permute-start.3
  21.5 7.3 %collective-permute-start.2 = (bf16[64,16,128]{2,1,0:T(8,128)(2,1)S(1)}, bf16[64,16,128]{2,1,0:T(8,128)(2,1)S(1)}, u32[]{:S(2)}, u32[]{:S(2)}) collective-permute-start(bf16[64,16,128]{2,1,0:T(8,128)(2,1)S(1)} %get-tuple-element.43), channel_id=1, source_target_pairs={{0,127},{1,2},{2,1},{3,4},{4,3},{5,6},{6,5},{7,8},{8,7},{9,10},{10... | collective-permute-start | bytes 786440 | tf_op jit(solution)/shard_map/ppermute | solution.py:394
  28.8 0.0 collective-permute-done.3.refs_3_
  28.8 3.8 %own.5 = (f32[129,16,128]{2,1,0:T(8,128)S(1)}, bf16[32,16384]{1,0:T(8,128)(2,1)S(1)}, f32[16,256]{1,0:T(8,128)S(1)}) custom-call(s32[640]{0:T(1024)S(4)} %get-tuple-element.36.refs_0_, bf16[256,128,128]{2,1,0:T(8,128)(2,1)S(1)} %get-tuple-element.37.refs_1_, bf16[128,16,128]{2,1,0:T(8,128)(2,1)S(1)} %get-tuple-element.44.refs_2_, ...), custom_call_target="tpu_custom_call" | custom-call | flops 1000000000 | bytes 10000000 | tf_op jit(solution)/shard_map/own/pallas_call | solution.py:397
  32.6 0.3 collective-permute-done.2.refs_2_
  32.8 1.4 %far.5 = (f32[16,16384]{1,0:T(8,128)S(1)}, bf16[128,16,128]{2,1,0:T(8,128)(2,1)S(1)}, bf16[64,16,128]{2,1,0:T(8,128)(2,1)S(1)}, bf16[64,16,128]{2,1,0:T(8,128)(2,1)S(1)}, f32[129,16,128]{2,1,0:T(8,128)S(1)}) custom-call(s32[640]{0:T(1024)S(4)} %get-tuple-element.36.refs_0_, ...), custom_call_target="tpu_custom_call", output_to_operand_aliasing={{4}: (3, {})} | custom-call | tf_op jit(solution)/shard_map/far/pallas_call | solution.py:415
  34.2 0.1 collective-permute-start.5
  34.3 7.3 %collective-permute-start.4 = (bf16[64,16,128]{2,1,0:T(8,128)(2,1)S(1)}, bf16[64,16,128]{2,1,0:T(8,128)(2,1)S(1)}, u32[]{:S(2)}, u32[]{:S(2)}) collective-permute-start(bf16[64,16,128]{2,1,0:T(8,128)(2,1)S(1)} %get-tuple-element.50), channel_id=1, source_target_pairs={{0,127},{1,2},{2,1},{3,4},{4,3},{5,6},{6,5},{7,8},{8,7},{9,10},{10... | collective-permute-start | bytes 786440 | tf_op jit(solution)/shard_map/ppermute | solution.py:394
  41.6 0.0 collective-permute-done.5.refs_3_
  41.6 4.1 %own.6 = (f32[129,16,128]{2,1,0:T(8,128)S(1)}, bf16[32,16384]{1,0:T(8,128)(2,1)S(1)}, f32[16,256]{1,0:T(8,128)S(1)}) custom-call(s32[640]{0:T(1024)S(4)} %get-tuple-element.36.refs_0_, bf16[256,128,128]{2,1,0:T(8,128)(2,1)S(1)} %get-tuple-element.37.refs_1_, bf16[128,16,128]{2,1,0:T(8,128)(2,1)S(1)} %get-tuple-element.51.refs_2_, ...), custom_call_target="tpu_custom_call" | custom-call | flops 1000000000 | bytes 10000000 | tf_op jit(solution)/shard_map/own/pallas_call | solution.py:397
  45.6 0.0 collective-permute-done.4.refs_2_
  45.6 1.4 %far.6 = (f32[16,16384]{1,0:T(8,128)S(1)}, bf16[128,16,128]{2,1,0:T(8,128)(2,1)S(1)}, bf16[64,16,128]{2,1,0:T(8,128)(2,1)S(1)}, bf16[64,16,128]{2,1,0:T(8,128)(2,1)S(1)}, f32[129,16,128]{2,1,0:T(8,128)S(1)}) custom-call(s32[640]{0:T(1024)S(4)} %get-tuple-element.36.refs_0_, ...), custom_call_target="tpu_custom_call", output_to_operand_aliasing={{4}: (3, {})} | custom-call | tf_op jit(solution)/shard_map/far/pallas_call | solution.py:415
  47.1 0.1 collective-permute-start.7
  47.2 7.2 %collective-permute-start.6 = (bf16[64,16,128]{2,1,0:T(8,128)(2,1)S(1)}, bf16[64,16,128]{2,1,0:T(8,128)(2,1)S(1)}, u32[]{:S(2)}, u32[]{:S(2)}) collective-permute-start(bf16[64,16,128]{2,1,0:T(8,128)(2,1)S(1)} %get-tuple-element.57), channel_id=1, source_target_pairs={{0,127},{1,2},{2,1},{3,4},{4,3},{5,6},{6,5},{7,8},{8,7},{9,10},{10... | collective-permute-start | bytes 786440 | tf_op jit(solution)/shard_map/ppermute | solution.py:394
  54.4 0.0 collective-permute-done.7.refs_3_
  54.4 4.2 %own.7 = (f32[129,16,128]{2,1,0:T(8,128)S(1)}, bf16[32,16384]{1,0:T(8,128)(2,1)S(1)}, f32[16,256]{1,0:T(8,128)S(1)}) custom-call(s32[640]{0:T(1024)S(4)} %get-tuple-element.36.refs_0_, bf16[256,128,128]{2,1,0:T(8,128)(2,1)S(1)} %get-tuple-element.37.refs_1_, bf16[128,16,128]{2,1,0:T(8,128)(2,1)S(1)} %get-tuple-element.58.refs_2_, ...), custom_call_target="tpu_custom_call" | custom-call | flops 1000000000 | bytes 10000000 | tf_op jit(solution)/shard_map/own/pallas_call | solution.py:397
  58.6 0.0 collective-permute-done.6.refs_2_
  58.6 2.5 %far.7 = (bf16[32,16384]{1,0:T(8,128)(2,1)S(1)}, f32[16,256]{1,0:T(8,128)S(1)}, f32[129,16,128]{2,1,0:T(8,128)S(1)}) custom-call(s32[640]{0:T(1024)S(4)} %get-tuple-element.36.refs_0_, bf16[256,128,128]{2,1,0:T(8,128)(2,1)S(1)} %get-tuple-element.37.refs_1_, ...), custom_call_target="tpu_custom_call", output_to_operand_aliasing={{2}: (3, {})} | custom-call | tf_op jit(solution)/shard_map/far/pallas_call | solution.py:415
  61.2 0.1 collective-permute-start.8
  61.2 1.2 %collective-permute-done.8 = f32[16,256]{1,0:T(8,128)S(1)} collective-permute-done((f32[16,256]{1,0:T(8,128)S(1)}, f32[16,256]{1,0:T(8,128)S(1)}, u32[]{:S(2)}, u32[]{:S(2)}) %collective-permute-start.8) | collective-permute-done | bytes 16416 | tf_op jit(solution)/shard_map/ppermute | solution.py:436
  62.4 0.0 collective-permute-start.11
  62.4 0.1 collective-permute-start.10
  62.5 1.9 %collective-permute-start.9 = (f32[16,256]{1,0:T(8,128)S(1)}, f32[16,256]{1,0:T(8,128)S(1)}, u32[]{:S(2)}, u32[]{:S(2)}) collective-permute-start(f32[16,256]{1,0:T(8,128)S(1)} %add.30), channel_id=1, source_target_pairs={{0,2},{1,3},{2,4},{3,5},{4,6},{5,7},{6,0},{7,1},{8,10},{9,11},{10,... | collective-permute-start | bytes 49160 | tf_op jit(solution)/shard_map/ppermute | solution.py:436
  64.4 1.7 %collective-permute-done.11 = f32[16,256]{1,0:T(8,128)S(1)} collective-permute-done((f32[16,256]{1,0:T(8,128)S(1)}, f32[16,256]{1,0:T(8,128)S(1)}, u32[]{:S(2)}, u32[]{:S(2)}) %collective-permute-start.11) | collective-permute-done | bytes 16416 | tf_op jit(solution)/shard_map/ppermute | solution.py:436
  66.1 1.6 %collective-permute-done.10 = f32[16,256]{1,0:T(8,128)S(1)} collective-permute-done((f32[16,256]{1,0:T(8,128)S(1)}, f32[16,256]{1,0:T(8,128)S(1)}, u32[]{:S(2)}, u32[]{:S(2)}) %collective-permute-start.10) | collective-permute-done | bytes 16416 | tf_op jit(solution)/shard_map/ppermute | solution.py:436
  67.7 1.1 %collective-permute-done.9 = f32[16,256]{1,0:T(8,128)S(1)} collective-permute-done((f32[16,256]{1,0:T(8,128)S(1)}, f32[16,256]{1,0:T(8,128)S(1)}, u32[]{:S(2)}, u32[]{:S(2)}) %collective-permute-start.9) | collective-permute-done | bytes 16416 | tf_op jit(solution)/shard_map/ppermute | solution.py:436
  68.8 0.0 collective-permute-start.14
  68.8 0.1 collective-permute-start.13
  68.9 1.9 %collective-permute-start.12 = (f32[16,256]{1,0:T(8,128)S(1)}, f32[16,256]{1,0:T(8,128)S(1)}, u32[]{:S(2)}, u32[]{:S(2)}) collective-permute-start(f32[16,256]{1,0:T(8,128)S(1)} %add_add_fusion.2), channel_id=1, source_target_pairs={{0,8},{1,9},{2,10},{3,11},{4,12},{5,13},{6,14},{7,15},{8,16},{9,17... | collective-permute-start | bytes 49160 | tf_op jit(solution)/shard_map/ppermute | solution.py:436
  70.9 1.7 %collective-permute-done.14 = f32[16,256]{1,0:T(8,128)S(1)} collective-permute-done((f32[16,256]{1,0:T(8,128)S(1)}, f32[16,256]{1,0:T(8,128)S(1)}, u32[]{:S(2)}, u32[]{:S(2)}) %collective-permute-start.14) | collective-permute-done | bytes 16416 | tf_op jit(solution)/shard_map/ppermute | solution.py:436
  72.6 1.7 %collective-permute-done.13 = f32[16,256]{1,0:T(8,128)S(1)} collective-permute-done((f32[16,256]{1,0:T(8,128)S(1)}, f32[16,256]{1,0:T(8,128)S(1)}, u32[]{:S(2)}, u32[]{:S(2)}) %collective-permute-start.13) | collective-permute-done | bytes 16416 | tf_op jit(solution)/shard_map/ppermute | solution.py:436
  74.3 1.0 %collective-permute-done.12 = f32[16,256]{1,0:T(8,128)S(1)} collective-permute-done((f32[16,256]{1,0:T(8,128)S(1)}, f32[16,256]{1,0:T(8,128)S(1)}, u32[]{:S(2)}, u32[]{:S(2)}) %collective-permute-start.12) | collective-permute-done | bytes 16416 | tf_op jit(solution)/shard_map/ppermute | solution.py:436
  75.2 5.9 %collective-permute-start.17 = (f32[16,256]{1,0:T(8,128)S(1)}, f32[16,256]{1,0:T(8,128)S(1)}, u32[]{:S(2)}, u32[]{:S(2)}) collective-permute-start(f32[16,256]{1,0:T(8,128)S(1)} %add_add_fusion.1), channel_id=1, source_target_pairs={{0,96},{1,97},{2,98},{3,99},{4,100},{5,101},{6,102},{7,103},{8,104... | collective-permute-start | bytes 49160 | tf_op jit(solution)/shard_map/ppermute | solution.py:436
  81.2 0.0 collective-permute-start.16
  81.2 0.9 %collective-permute-start.15 = (f32[16,256]{1,0:T(8,128)S(1)}, f32[16,256]{1,0:T(8,128)S(1)}, u32[]{:S(2)}, u32[]{:S(2)}) collective-permute-start(f32[16,256]{1,0:T(8,128)S(1)} %add_add_fusion.1), channel_id=1, source_target_pairs={{0,32},{1,33},{2,34},{3,35},{4,36},{5,37},{6,38},{7,39},{8,40},{9,... | collective-permute-start | bytes 49160 | tf_op jit(solution)/shard_map/ppermute | solution.py:436
  82.1 0.5 collective-permute-done.17
  82.6 3.8 %collective-permute-done.16 = f32[16,256]{1,0:T(8,128)S(1)} collective-permute-done((f32[16,256]{1,0:T(8,128)S(1)}, f32[16,256]{1,0:T(8,128)S(1)}, u32[]{:S(2)}, u32[]{:S(2)}) %collective-permute-start.16) | collective-permute-done | bytes 16416 | tf_op jit(solution)/shard_map/ppermute | solution.py:436
  86.4 0.0 collective-permute-done.15
  86.4 6.3 %final.1 = (f32[80,16384]{1,0:T(8,128)}, f32[80,80]{1,0:T(8,128)}) custom-call(f32[16,256]{1,0:T(8,128)S(1)} %add_add_fusion.gram_in, bf16[32,16384]{1,0:T(8,128)(2,1)S(1)} %get-tuple-element.47.refs_5_.refs_6_.refs_0_, bf16[32,16384]{1,0:T(8,128)(2,1)S(1)} %get-tuple-element.54.refs_6_.refs_7_.refs_1_, ...), custom_call_target="tpu_custom_call" | custom-call | tf_op jit(solution)/shard_map/final/pallas_call | solution.py:443
  (4 shorter events, 0.0 us)
Async XLA Ops:
  1.3 14.7 %copy-start = (f32[16384,16]{0,1:T(8,128)S(1)}, f32[16384,16]{0,1:T(8,128)}, u32[]{:S(2)}) copy-start(f32[16384,16]{0,1:T(8,128)} %param.5) | copy-start | bytes 3145732
  7.0 9.0 %collective-permute-start.1 = (bf16[64,16,128]{2,1,0:T(8,128)(2,1)S(1)}, bf16[64,16,128]{2,1,0:T(8,128)(2,1)S(1)}, u32[]{:S(2)}, u32[]{:S(2)}) collective-permute-start(bf16[64,16,128]{2,1,0:T(8,128)(2,1)S(1)} %get-tuple-element.40), channel_id=1, source_target_pairs={{0,1},{1,0},{2,3},{3,2},{4,5},{5,4},{6,7},{7,6},{8,9},{9,8},{10,11... | collective-permute-start | bytes 786440 | tf_op jit(solution)/shard_map/ppermute | solution.py:395
  7.1 12.9 %collective-permute-start = (bf16[64,16,128]{2,1,0:T(8,128)(2,1)S(1)}, bf16[64,16,128]{2,1,0:T(8,128)(2,1)S(1)}, u32[]{:S(2)}, u32[]{:S(2)}) collective-permute-start(bf16[64,16,128]{2,1,0:T(8,128)(2,1)S(1)} %get-tuple-element.38), channel_id=1, source_target_pairs={{0,127},{1,2},{2,1},{3,4},{4,3},{5,6},{6,5},{7,8},{8,7},{9,10},{10... | collective-permute-start | bytes 786440 | tf_op jit(solution)/shard_map/ppermute | solution.py:394
  21.4 7.3 %collective-permute-start.3 = (bf16[64,16,128]{2,1,0:T(8,128)(2,1)S(1)}, bf16[64,16,128]{2,1,0:T(8,128)(2,1)S(1)}, u32[]{:S(2)}, u32[]{:S(2)}) collective-permute-start(bf16[64,16,128]{2,1,0:T(8,128)(2,1)S(1)} %get-tuple-element.45), channel_id=1, source_target_pairs={{0,1},{1,0},{2,3},{3,2},{4,5},{5,4},{6,7},{7,6},{8,9},{9,8},{10,11... | collective-permute-start | bytes 786440 | tf_op jit(solution)/shard_map/ppermute | solution.py:395
  21.5 11.3 %collective-permute-start.2 = (bf16[64,16,128]{2,1,0:T(8,128)(2,1)S(1)}, bf16[64,16,128]{2,1,0:T(8,128)(2,1)S(1)}, u32[]{:S(2)}, u32[]{:S(2)}) collective-permute-start(bf16[64,16,128]{2,1,0:T(8,128)(2,1)S(1)} %get-tuple-element.43), channel_id=1, source_target_pairs={{0,127},{1,2},{2,1},{3,4},{4,3},{5,6},{6,5},{7,8},{8,7},{9,10},{10... | collective-permute-start | bytes 786440 | tf_op jit(solution)/shard_map/ppermute | solution.py:394
  34.2 7.3 %collective-permute-start.5 = (bf16[64,16,128]{2,1,0:T(8,128)(2,1)S(1)}, bf16[64,16,128]{2,1,0:T(8,128)(2,1)S(1)}, u32[]{:S(2)}, u32[]{:S(2)}) collective-permute-start(bf16[64,16,128]{2,1,0:T(8,128)(2,1)S(1)} %get-tuple-element.52), channel_id=1, source_target_pairs={{0,1},{1,0},{2,3},{3,2},{4,5},{5,4},{6,7},{7,6},{8,9},{9,8},{10,11... | collective-permute-start | bytes 786440 | tf_op jit(solution)/shard_map/ppermute | solution.py:395
  34.3 11.3 %collective-permute-start.4 = (bf16[64,16,128]{2,1,0:T(8,128)(2,1)S(1)}, bf16[64,16,128]{2,1,0:T(8,128)(2,1)S(1)}, u32[]{:S(2)}, u32[]{:S(2)}) collective-permute-start(bf16[64,16,128]{2,1,0:T(8,128)(2,1)S(1)} %get-tuple-element.50), channel_id=1, source_target_pairs={{0,127},{1,2},{2,1},{3,4},{4,3},{5,6},{6,5},{7,8},{8,7},{9,10},{10... | collective-permute-start | bytes 786440 | tf_op jit(solution)/shard_map/ppermute | solution.py:394
  47.1 7.3 %collective-permute-start.7 = (bf16[64,16,128]{2,1,0:T(8,128)(2,1)S(1)}, bf16[64,16,128]{2,1,0:T(8,128)(2,1)S(1)}, u32[]{:S(2)}, u32[]{:S(2)}) collective-permute-start(bf16[64,16,128]{2,1,0:T(8,128)(2,1)S(1)} %get-tuple-element.59), channel_id=1, source_target_pairs={{0,1},{1,0},{2,3},{3,2},{4,5},{5,4},{6,7},{7,6},{8,9},{9,8},{10,11... | collective-permute-start | bytes 786440 | tf_op jit(solution)/shard_map/ppermute | solution.py:395
  47.2 11.5 %collective-permute-start.6 = (bf16[64,16,128]{2,1,0:T(8,128)(2,1)S(1)}, bf16[64,16,128]{2,1,0:T(8,128)(2,1)S(1)}, u32[]{:S(2)}, u32[]{:S(2)}) collective-permute-start(bf16[64,16,128]{2,1,0:T(8,128)(2,1)S(1)} %get-tuple-element.57), channel_id=1, source_target_pairs={{0,127},{1,2},{2,1},{3,4},{4,3},{5,6},{6,5},{7,8},{8,7},{9,10},{10... | collective-permute-start | bytes 786440 | tf_op jit(solution)/shard_map/ppermute | solution.py:394
  61.2 1.2 %collective-permute-start.8 = (f32[16,256]{1,0:T(8,128)S(1)}, f32[16,256]{1,0:T(8,128)S(1)}, u32[]{:S(2)}, u32[]{:S(2)}) collective-permute-start(f32[16,256]{1,0:T(8,128)S(1)} %get-tuple-element.66), channel_id=1, source_target_pairs={{0,1},{1,0},{2,3},{3,2},{4,5},{5,4},{6,7},{7,6},{8,9},{9,8},{10,11... | collective-permute-start | bytes 49160 | tf_op jit(solution)/shard_map/ppermute | solution.py:436
  62.4 3.7 %collective-permute-start.11 = (f32[16,256]{1,0:T(8,128)S(1)}, f32[16,256]{1,0:T(8,128)S(1)}, u32[]{:S(2)}, u32[]{:S(2)}) collective-permute-start(f32[16,256]{1,0:T(8,128)S(1)} %add.30), channel_id=1, source_target_pairs={{0,6},{1,7},{2,0},{3,1},{4,2},{5,3},{6,4},{7,5},{8,14},{9,15},{10,... | collective-permute-start | bytes 49160 | tf_op jit(solution)/shard_map/ppermute | solution.py:436
  62.4 5.3 %collective-permute-start.10 = (f32[16,256]{1,0:T(8,128)S(1)}, f32[16,256]{1,0:T(8,128)S(1)}, u32[]{:S(2)}, u32[]{:S(2)}) collective-permute-start(f32[16,256]{1,0:T(8,128)S(1)} %add.30), channel_id=1, source_target_pairs={{0,4},{1,5},{2,6},{3,7},{4,0},{5,1},{6,2},{7,3},{8,12},{9,13},{10,... | collective-permute-start | bytes 49160 | tf_op jit(solution)/shard_map/ppermute | solution.py:436
  62.5 6.3 %collective-permute-start.9 = (f32[16,256]{1,0:T(8,128)S(1)}, f32[16,256]{1,0:T(8,128)S(1)}, u32[]{:S(2)}, u32[]{:S(2)}) collective-permute-start(f32[16,256]{1,0:T(8,128)S(1)} %add.30), channel_id=1, source_target_pairs={{0,2},{1,3},{2,4},{3,5},{4,6},{5,7},{6,0},{7,1},{8,10},{9,11},{10,... | collective-permute-start | bytes 49160 | tf_op jit(solution)/shard_map/ppermute | solution.py:436
  68.8 3.7 %collective-permute-start.14 = (f32[16,256]{1,0:T(8,128)S(1)}, f32[16,256]{1,0:T(8,128)S(1)}, u32[]{:S(2)}, u32[]{:S(2)}) collective-permute-start(f32[16,256]{1,0:T(8,128)S(1)} %add_add_fusion.2), channel_id=1, source_target_pairs={{0,24},{1,25},{2,26},{3,27},{4,28},{5,29},{6,30},{7,31},{8,0},{9,1... | collective-permute-start | bytes 49160 | tf_op jit(solution)/shard_map/ppermute | solution.py:436
  68.8 5.5 %collective-permute-start.13 = (f32[16,256]{1,0:T(8,128)S(1)}, f32[16,256]{1,0:T(8,128)S(1)}, u32[]{:S(2)}, u32[]{:S(2)}) collective-permute-start(f32[16,256]{1,0:T(8,128)S(1)} %add_add_fusion.2), channel_id=1, source_target_pairs={{0,16},{1,17},{2,18},{3,19},{4,20},{5,21},{6,22},{7,23},{8,24},{9,... | collective-permute-start | bytes 49160 | tf_op jit(solution)/shard_map/ppermute | solution.py:436
  68.9 6.3 %collective-permute-start.12 = (f32[16,256]{1,0:T(8,128)S(1)}, f32[16,256]{1,0:T(8,128)S(1)}, u32[]{:S(2)}, u32[]{:S(2)}) collective-permute-start(f32[16,256]{1,0:T(8,128)S(1)} %add_add_fusion.2), channel_id=1, source_target_pairs={{0,8},{1,9},{2,10},{3,11},{4,12},{5,13},{6,14},{7,15},{8,16},{9,17... | collective-permute-start | bytes 49160 | tf_op jit(solution)/shard_map/ppermute | solution.py:436
  75.2 7.4 %collective-permute-start.17 = (f32[16,256]{1,0:T(8,128)S(1)}, f32[16,256]{1,0:T(8,128)S(1)}, u32[]{:S(2)}, u32[]{:S(2)}) collective-permute-start(f32[16,256]{1,0:T(8,128)S(1)} %add_add_fusion.1), channel_id=1, source_target_pairs={{0,96},{1,97},{2,98},{3,99},{4,100},{5,101},{6,102},{7,103},{8,104... | collective-permute-start | bytes 49160 | tf_op jit(solution)/shard_map/ppermute | solution.py:436
  81.2 5.2 %collective-permute-start.16 = (f32[16,256]{1,0:T(8,128)S(1)}, f32[16,256]{1,0:T(8,128)S(1)}, u32[]{:S(2)}, u32[]{:S(2)}) collective-permute-start(f32[16,256]{1,0:T(8,128)S(1)} %add_add_fusion.1), channel_id=1, source_target_pairs={{0,64},{1,65},{2,66},{3,67},{4,68},{5,69},{6,70},{7,71},{8,72},{9,... | collective-permute-start | bytes 49160 | tf_op jit(solution)/shard_map/ppermute | solution.py:436
  81.2 5.2 %collective-permute-start.15 = (f32[16,256]{1,0:T(8,128)S(1)}, f32[16,256]{1,0:T(8,128)S(1)}, u32[]{:S(2)}, u32[]{:S(2)}) collective-permute-start(f32[16,256]{1,0:T(8,128)S(1)} %add_add_fusion.1), channel_id=1, source_target_pairs={{0,32},{1,33},{2,34},{3,35},{4,36},{5,37},{6,38},{7,39},{8,40},{9,... | collective-permute-start | bytes 49160 | tf_op jit(solution)/shard_map/ppermute | solution.py:436

commit v5 on v4

--- a/solution.py
+++ b/solution.py
@@ -428,16 +428,25 @@
             vec, scaled, send_a, send_b, _ = got
             vectors.append(vec)
 
-    def phase(value, shift, count):
+    def phase(value, shift, count, upward):
         mask = (count - 1) << shift
         moved = value
-        for d in range(1, count):
-            perm = [(i, (i & ~mask) | ((((i >> shift) + d) & (count - 1)) << shift)) for i in range(n)]
+        for d in range(count - 1, 0, -1):
+            perm = []
+            for i in range(n):
+                step = d if upward(i) else count - d
+                perm.append((i, (i & ~mask) | ((((i >> shift) + step) & (count - 1)) << shift)))
             moved = moved + lax.ppermute(value, AXIS, perm)
         return moved
 
-    for shift, count in ((0, 2), (1, 4), (3, 4), (5, 4)):
-        gram = phase(gram, shift, count)
+    def high_z(i):
+        return i >= n // 2
+
+    def high_y(i):
+        return (i >> 4) & 1 == 1
+
+    for shift, count, upward in ((0, 2, high_z), (1, 4, high_z), (3, 4, high_z), (5, 4, high_y)):
+        gram = phase(gram, shift, count, upward)
 
     chunk = 1024
     basis_out, gram_matrix = pl.pallas_call(

time: 93.1 us -> 92.7 us (level)
  no operation moved by 1% of the time
where the time goes in v5:
time: 92.7 us; the launch traced here: 92.6 us
  starting transfers between devices  41.6 us (45%)
  Pallas kernels  34.3 us (37%)
  waiting for transfers between devices  15.1 us (16%)
  between operations  1.56 us (2%)
    ppermute x4, starting transfers between devices, body(): got_b = lax.ppermute(send_b, AXIS, far)  30.5 us
    pallas_call x4, Pallas kernels, body(): pl.pallas_call(functools.partial(own_kernel, level - 1), out_shape=(acc_t...  15.5 us
    ppermute x10, waiting for transfers between devices, phase(): moved = moved + lax.ppermute(value, AXIS, perm)  14.2 us
    ppermute x10, starting transfers between devices, phase(): moved = moved + lax.ppermute(value, AXIS, perm)  10.8 us
    pallas_call x4, Pallas kernels, body(): pl.pallas_call(functools.partial(far_kernel, level, last), out_shape=outs...  6.67 us
    pallas_call x1, Pallas kernels, body(): pl.pallas_call(functools.partial(final_kernel, rows * n), out_shape=(shap...  6.35 us
    pallas_call x1, Pallas kernels, body(): pl.pallas_call(setup_kernel, out_shape=(shape((total, side, side), BF16),...  5.71 us
  transfers between devices with their start and end apart: 18, of which 11 were waited for; matrix products, arithmetic and copies ran while one was open for 0% of the time, Pallas kernels for 17%

profile of v5, /device:TPU:0, one launch (start us, length us, event | category | flops | bytes accessed | tf_op | source)
XLA Modules:
  0.0 92.6 jit_solution(17112554823705079448)
XLA Ops:
  1.3 0.0 copy-start
  1.3 5.7 %setup.1 = (bf16[256,128,128]{2,1,0:T(8,128)(2,1)S(1)}, s32[640]{0:T(1024)S(4)}, f32[128,8,128]{2,1,0:T(8,128)S(1)}, bf16[128,16,128]{2,1,0:T(8,128)(2,1)S(1)}, ...) custom-call(s32[2,256]{1,0:T(2,128)} %bitcast.7, s32[2,64]{1,0:T(2,128)} %bitcast.8, ...), custom_call_target="tpu_custom_call" | custom-call | tf_op jit(solution)/shard_map/setup/pallas_call | solution.py:376
  7.0 0.1 collective-permute-start.1
  7.1 8.8 %collective-permute-start = (bf16[64,16,128]{2,1,0:T(8,128)(2,1)S(1)}, bf16[64,16,128]{2,1,0:T(8,128)(2,1)S(1)}, u32[]{:S(2)}, u32[]{:S(2)}) collective-permute-start(bf16[64,16,128]{2,1,0:T(8,128)(2,1)S(1)} %get-tuple-element.38), channel_id=1, source_target_pairs={{0,127},{1,2},{2,1},{3,4},{4,3},{5,6},{6,5},{7,8},{8,7},{9,10},{10... | collective-permute-start | bytes 786440 | tf_op jit(solution)/shard_map/ppermute | solution.py:394
  15.9 0.0 collective-permute-done.1.refs_3_
  15.9 0.0 copy-done
  15.9 3.5 %own.4 = (f32[129,16,128]{2,1,0:T(8,128)S(1)}, bf16[32,16384]{1,0:T(8,128)(2,1)S(1)}, f32[16,256]{1,0:T(8,128)S(1)}) custom-call(s32[640]{0:T(1024)S(4)} %get-tuple-element.36.refs_0_, bf16[256,128,128]{2,1,0:T(8,128)(2,1)S(1)} %get-tuple-element.37.refs_1_, bf16[128,16,128]{2,1,0:T(8,128)(2,1)S(1)} %get-tuple-element.39.refs_2_, ...), custom_call_target="tpu_custom_call" | custom-call | flops 1000000000 | bytes 10000000 | tf_op jit(solution)/shard_map/own/pallas_call | solution.py:397
  19.4 0.5 collective-permute-done.refs_2_
  19.9 1.3 %far.4 = (f32[16,16384]{1,0:T(8,128)S(1)}, bf16[128,16,128]{2,1,0:T(8,128)(2,1)S(1)}, bf16[64,16,128]{2,1,0:T(8,128)(2,1)S(1)}, bf16[64,16,128]{2,1,0:T(8,128)(2,1)S(1)}, f32[129,16,128]{2,1,0:T(8,128)S(1)}) custom-call(s32[640]{0:T(1024)S(4)} %get-tuple-element.36.refs_0_, ...), custom_call_target="tpu_custom_call", output_to_operand_aliasing={{4}: (3, {})} | custom-call | tf_op jit(solution)/shard_map/far/pallas_call | solution.py:415
  21.3 0.1 collective-permute-start.3
  21.4 7.3 %collective-permute-start.2 = (bf16[64,16,128]{2,1,0:T(8,128)(2,1)S(1)}, bf16[64,16,128]{2,1,0:T(8,128)(2,1)S(1)}, u32[]{:S(2)}, u32[]{:S(2)}) collective-permute-start(bf16[64,16,128]{2,1,0:T(8,128)(2,1)S(1)} %get-tuple-element.43), channel_id=1, source_target_pairs={{0,127},{1,2},{2,1},{3,4},{4,3},{5,6},{6,5},{7,8},{8,7},{9,10},{10... | collective-permute-start | bytes 786440 | tf_op jit(solution)/shard_map/ppermute | solution.py:394
  28.6 0.0 collective-permute-done.3.refs_3_
  28.6 3.8 %own.5 = (f32[129,16,128]{2,1,0:T(8,128)S(1)}, bf16[32,16384]{1,0:T(8,128)(2,1)S(1)}, f32[16,256]{1,0:T(8,128)S(1)}) custom-call(s32[640]{0:T(1024)S(4)} %get-tuple-element.36.refs_0_, bf16[256,128,128]{2,1,0:T(8,128)(2,1)S(1)} %get-tuple-element.37.refs_1_, bf16[128,16,128]{2,1,0:T(8,128)(2,1)S(1)} %get-tuple-element.44.refs_2_, ...), custom_call_target="tpu_custom_call" | custom-call | flops 1000000000 | bytes 10000000 | tf_op jit(solution)/shard_map/own/pallas_call | solution.py:397
  32.4 0.3 collective-permute-done.2.refs_2_
  32.7 1.4 %far.5 = (f32[16,16384]{1,0:T(8,128)S(1)}, bf16[128,16,128]{2,1,0:T(8,128)(2,1)S(1)}, bf16[64,16,128]{2,1,0:T(8,128)(2,1)S(1)}, bf16[64,16,128]{2,1,0:T(8,128)(2,1)S(1)}, f32[129,16,128]{2,1,0:T(8,128)S(1)}) custom-call(s32[640]{0:T(1024)S(4)} %get-tuple-element.36.refs_0_, ...), custom_call_target="tpu_custom_call", output_to_operand_aliasing={{4}: (3, {})} | custom-call | tf_op jit(solution)/shard_map/far/pallas_call | solution.py:415
  34.1 0.1 collective-permute-start.5
  34.2 7.3 %collective-permute-start.4 = (bf16[64,16,128]{2,1,0:T(8,128)(2,1)S(1)}, bf16[64,16,128]{2,1,0:T(8,128)(2,1)S(1)}, u32[]{:S(2)}, u32[]{:S(2)}) collective-permute-start(bf16[64,16,128]{2,1,0:T(8,128)(2,1)S(1)} %get-tuple-element.50), channel_id=1, source_target_pairs={{0,127},{1,2},{2,1},{3,4},{4,3},{5,6},{6,5},{7,8},{8,7},{9,10},{10... | collective-permute-start | bytes 786440 | tf_op jit(solution)/shard_map/ppermute | solution.py:394
  41.4 0.0 collective-permute-done.5.refs_3_
  41.4 4.0 %own.6 = (f32[129,16,128]{2,1,0:T(8,128)S(1)}, bf16[32,16384]{1,0:T(8,128)(2,1)S(1)}, f32[16,256]{1,0:T(8,128)S(1)}) custom-call(s32[640]{0:T(1024)S(4)} %get-tuple-element.36.refs_0_, bf16[256,128,128]{2,1,0:T(8,128)(2,1)S(1)} %get-tuple-element.37.refs_1_, bf16[128,16,128]{2,1,0:T(8,128)(2,1)S(1)} %get-tuple-element.51.refs_2_, ...), custom_call_target="tpu_custom_call" | custom-call | flops 1000000000 | bytes 10000000 | tf_op jit(solution)/shard_map/own/pallas_call | solution.py:397
  45.5 0.0 collective-permute-done.4.refs_2_
  45.5 1.4 %far.6 = (f32[16,16384]{1,0:T(8,128)S(1)}, bf16[128,16,128]{2,1,0:T(8,128)(2,1)S(1)}, bf16[64,16,128]{2,1,0:T(8,128)(2,1)S(1)}, bf16[64,16,128]{2,1,0:T(8,128)(2,1)S(1)}, f32[129,16,128]{2,1,0:T(8,128)S(1)}) custom-call(s32[640]{0:T(1024)S(4)} %get-tuple-element.36.refs_0_, ...), custom_call_target="tpu_custom_call", output_to_operand_aliasing={{4}: (3, {})} | custom-call | tf_op jit(solution)/shard_map/far/pallas_call | solution.py:415
  46.9 0.1 collective-permute-start.7
  47.0 7.3 %collective-permute-start.6 = (bf16[64,16,128]{2,1,0:T(8,128)(2,1)S(1)}, bf16[64,16,128]{2,1,0:T(8,128)(2,1)S(1)}, u32[]{:S(2)}, u32[]{:S(2)}) collective-permute-start(bf16[64,16,128]{2,1,0:T(8,128)(2,1)S(1)} %get-tuple-element.57), channel_id=1, source_target_pairs={{0,127},{1,2},{2,1},{3,4},{4,3},{5,6},{6,5},{7,8},{8,7},{9,10},{10... | collective-permute-start | bytes 786440 | tf_op jit(solution)/shard_map/ppermute | solution.py:394
  54.2 0.0 collective-permute-done.7.refs_3_
  54.2 4.2 %own.7 = (f32[129,16,128]{2,1,0:T(8,128)S(1)}, bf16[32,16384]{1,0:T(8,128)(2,1)S(1)}, f32[16,256]{1,0:T(8,128)S(1)}) custom-call(s32[640]{0:T(1024)S(4)} %get-tuple-element.36.refs_0_, bf16[256,128,128]{2,1,0:T(8,128)(2,1)S(1)} %get-tuple-element.37.refs_1_, bf16[128,16,128]{2,1,0:T(8,128)(2,1)S(1)} %get-tuple-element.58.refs_2_, ...), custom_call_target="tpu_custom_call" | custom-call | flops 1000000000 | bytes 10000000 | tf_op jit(solution)/shard_map/own/pallas_call | solution.py:397
  58.5 0.0 collective-permute-done.6.refs_2_
  58.5 2.5 %far.7 = (bf16[32,16384]{1,0:T(8,128)(2,1)S(1)}, f32[16,256]{1,0:T(8,128)S(1)}, f32[129,16,128]{2,1,0:T(8,128)S(1)}) custom-call(s32[640]{0:T(1024)S(4)} %get-tuple-element.36.refs_0_, bf16[256,128,128]{2,1,0:T(8,128)(2,1)S(1)} %get-tuple-element.37.refs_1_, ...), custom_call_target="tpu_custom_call", output_to_operand_aliasing={{2}: (3, {})} | custom-call | tf_op jit(solution)/shard_map/far/pallas_call | solution.py:415
  61.0 0.1 collective-permute-start.8
  61.0 1.2 %collective-permute-done.8 = f32[16,256]{1,0:T(8,128)S(1)} collective-permute-done((f32[16,256]{1,0:T(8,128)S(1)}, f32[16,256]{1,0:T(8,128)S(1)}, u32[]{:S(2)}, u32[]{:S(2)}) %collective-permute-start.8) | collective-permute-done | bytes 16416 | tf_op jit(solution)/shard_map/ppermute | solution.py:439
  62.2 0.0 collective-permute-start.11
  62.2 0.1 collective-permute-start.10
  62.3 1.9 %collective-permute-start.9 = (f32[16,256]{1,0:T(8,128)S(1)}, f32[16,256]{1,0:T(8,128)S(1)}, u32[]{:S(2)}, u32[]{:S(2)}) collective-permute-start(f32[16,256]{1,0:T(8,128)S(1)} %add.30), channel_id=1, source_target_pairs={{0,2},{1,3},{2,4},{3,5},{4,6},{5,7},{6,0},{7,1},{8,10},{9,11},{10,... | collective-permute-start | bytes 49160 | tf_op jit(solution)/shard_map/ppermute | solution.py:439
  64.3 1.7 %collective-permute-done.11 = f32[16,256]{1,0:T(8,128)S(1)} collective-permute-done((f32[16,256]{1,0:T(8,128)S(1)}, f32[16,256]{1,0:T(8,128)S(1)}, u32[]{:S(2)}, u32[]{:S(2)}) %collective-permute-start.11) | collective-permute-done | bytes 16416 | tf_op jit(solution)/shard_map/ppermute | solution.py:439
  66.0 1.6 %collective-permute-done.10 = f32[16,256]{1,0:T(8,128)S(1)} collective-permute-done((f32[16,256]{1,0:T(8,128)S(1)}, f32[16,256]{1,0:T(8,128)S(1)}, u32[]{:S(2)}, u32[]{:S(2)}) %collective-permute-start.10) | collective-permute-done | bytes 16416 | tf_op jit(solution)/shard_map/ppermute | solution.py:439
  67.6 1.1 %collective-permute-done.9 = f32[16,256]{1,0:T(8,128)S(1)} collective-permute-done((f32[16,256]{1,0:T(8,128)S(1)}, f32[16,256]{1,0:T(8,128)S(1)}, u32[]{:S(2)}, u32[]{:S(2)}) %collective-permute-start.9) | collective-permute-done | bytes 16416 | tf_op jit(solution)/shard_map/ppermute | solution.py:439
  68.6 0.0 collective-permute-start.14
  68.7 0.1 collective-permute-start.13
  68.8 1.9 %collective-permute-start.12 = (f32[16,256]{1,0:T(8,128)S(1)}, f32[16,256]{1,0:T(8,128)S(1)}, u32[]{:S(2)}, u32[]{:S(2)}) collective-permute-start(f32[16,256]{1,0:T(8,128)S(1)} %add_add_fusion.2), channel_id=1, source_target_pairs={{0,8},{1,9},{2,10},{3,11},{4,12},{5,13},{6,14},{7,15},{8,16},{9,17... | collective-permute-start | bytes 49160 | tf_op jit(solution)/shard_map/ppermute | solution.py:439
  70.7 1.7 %collective-permute-done.14 = f32[16,256]{1,0:T(8,128)S(1)} collective-permute-done((f32[16,256]{1,0:T(8,128)S(1)}, f32[16,256]{1,0:T(8,128)S(1)}, u32[]{:S(2)}, u32[]{:S(2)}) %collective-permute-start.14) | collective-permute-done | bytes 16416 | tf_op jit(solution)/shard_map/ppermute | solution.py:439
  72.4 1.7 %collective-permute-done.13 = f32[16,256]{1,0:T(8,128)S(1)} collective-permute-done((f32[16,256]{1,0:T(8,128)S(1)}, f32[16,256]{1,0:T(8,128)S(1)}, u32[]{:S(2)}, u32[]{:S(2)}) %collective-permute-start.13) | collective-permute-done | bytes 16416 | tf_op jit(solution)/shard_map/ppermute | solution.py:439
  74.1 1.0 %collective-permute-done.12 = f32[16,256]{1,0:T(8,128)S(1)} collective-permute-done((f32[16,256]{1,0:T(8,128)S(1)}, f32[16,256]{1,0:T(8,128)S(1)}, u32[]{:S(2)}, u32[]{:S(2)}) %collective-permute-start.12) | collective-permute-done | bytes 16416 | tf_op jit(solution)/shard_map/ppermute | solution.py:439
  75.1 5.7 %collective-permute-start.17 = (f32[16,256]{1,0:T(8,128)S(1)}, f32[16,256]{1,0:T(8,128)S(1)}, u32[]{:S(2)}, u32[]{:S(2)}) collective-permute-start(f32[16,256]{1,0:T(8,128)S(1)} %add_add_fusion.1), channel_id=1, source_target_pairs={{0,96},{1,97},{2,98},{3,99},{4,100},{5,101},{6,102},{7,103},{8,104... | collective-permute-start | bytes 49160 | tf_op jit(solution)/shard_map/ppermute | solution.py:439
  80.8 0.0 collective-permute-start.16
  80.8 0.9 %collective-permute-start.15 = (f32[16,256]{1,0:T(8,128)S(1)}, f32[16,256]{1,0:T(8,128)S(1)}, u32[]{:S(2)}, u32[]{:S(2)}) collective-permute-start(f32[16,256]{1,0:T(8,128)S(1)} %add_add_fusion.1), channel_id=1, source_target_pairs={{0,32},{1,33},{2,34},{3,35},{4,36},{5,37},{6,38},{7,39},{8,40},{9,... | collective-permute-start | bytes 49160 | tf_op jit(solution)/shard_map/ppermute | solution.py:439
  81.7 0.5 collective-permute-done.17
  82.2 3.8 %collective-permute-done.16 = f32[16,256]{1,0:T(8,128)S(1)} collective-permute-done((f32[16,256]{1,0:T(8,128)S(1)}, f32[16,256]{1,0:T(8,128)S(1)}, u32[]{:S(2)}, u32[]{:S(2)}) %collective-permute-start.16) | collective-permute-done | bytes 16416 | tf_op jit(solution)/shard_map/ppermute | solution.py:439
  86.0 0.0 collective-permute-done.15
  86.1 6.3 %final.1 = (f32[80,16384]{1,0:T(8,128)}, f32[80,80]{1,0:T(8,128)}) custom-call(f32[16,256]{1,0:T(8,128)S(1)} %add_add_fusion.gram_in, bf16[32,16384]{1,0:T(8,128)(2,1)S(1)} %get-tuple-element.47.refs_5_.refs_6_.refs_0_, bf16[32,16384]{1,0:T(8,128)(2,1)S(1)} %get-tuple-element.54.refs_6_.refs_7_.refs_1_, ...), custom_call_target="tpu_custom_call" | custom-call | tf_op jit(solution)/shard_map/final/pallas_call | solution.py:452
  (4 shorter events, 0.0 us)
Async XLA Ops:
  1.3 14.6 %copy-start = (f32[16384,16]{0,1:T(8,128)S(1)}, f32[16384,16]{0,1:T(8,128)}, u32[]{:S(2)}) copy-start(f32[16384,16]{0,1:T(8,128)} %param.5) | copy-start | bytes 3145732
  7.0 8.9 %collective-permute-start.1 = (bf16[64,16,128]{2,1,0:T(8,128)(2,1)S(1)}, bf16[64,16,128]{2,1,0:T(8,128)(2,1)S(1)}, u32[]{:S(2)}, u32[]{:S(2)}) collective-permute-start(bf16[64,16,128]{2,1,0:T(8,128)(2,1)S(1)} %get-tuple-element.40), channel_id=1, source_target_pairs={{0,1},{1,0},{2,3},{3,2},{4,5},{5,4},{6,7},{7,6},{8,9},{9,8},{10,11... | collective-permute-start | bytes 786440 | tf_op jit(solution)/shard_map/ppermute | solution.py:395
  7.1 12.8 %collective-permute-start = (bf16[64,16,128]{2,1,0:T(8,128)(2,1)S(1)}, bf16[64,16,128]{2,1,0:T(8,128)(2,1)S(1)}, u32[]{:S(2)}, u32[]{:S(2)}) collective-permute-start(bf16[64,16,128]{2,1,0:T(8,128)(2,1)S(1)} %get-tuple-element.38), channel_id=1, source_target_pairs={{0,127},{1,2},{2,1},{3,4},{4,3},{5,6},{6,5},{7,8},{8,7},{9,10},{10... | collective-permute-start | bytes 786440 | tf_op jit(solution)/shard_map/ppermute | solution.py:394
  21.3 7.3 %collective-permute-start.3 = (bf16[64,16,128]{2,1,0:T(8,128)(2,1)S(1)}, bf16[64,16,128]{2,1,0:T(8,128)(2,1)S(1)}, u32[]{:S(2)}, u32[]{:S(2)}) collective-permute-start(bf16[64,16,128]{2,1,0:T(8,128)(2,1)S(1)} %get-tuple-element.45), channel_id=1, source_target_pairs={{0,1},{1,0},{2,3},{3,2},{4,5},{5,4},{6,7},{7,6},{8,9},{9,8},{10,11... | collective-permute-start | bytes 786440 | tf_op jit(solution)/shard_map/ppermute | solution.py:395
  21.4 11.3 %collective-permute-start.2 = (bf16[64,16,128]{2,1,0:T(8,128)(2,1)S(1)}, bf16[64,16,128]{2,1,0:T(8,128)(2,1)S(1)}, u32[]{:S(2)}, u32[]{:S(2)}) collective-permute-start(bf16[64,16,128]{2,1,0:T(8,128)(2,1)S(1)} %get-tuple-element.43), channel_id=1, source_target_pairs={{0,127},{1,2},{2,1},{3,4},{4,3},{5,6},{6,5},{7,8},{8,7},{9,10},{10... | collective-permute-start | bytes 786440 | tf_op jit(solution)/shard_map/ppermute | solution.py:394
  34.1 7.3 %collective-permute-start.5 = (bf16[64,16,128]{2,1,0:T(8,128)(2,1)S(1)}, bf16[64,16,128]{2,1,0:T(8,128)(2,1)S(1)}, u32[]{:S(2)}, u32[]{:S(2)}) collective-permute-start(bf16[64,16,128]{2,1,0:T(8,128)(2,1)S(1)} %get-tuple-element.52), channel_id=1, source_target_pairs={{0,1},{1,0},{2,3},{3,2},{4,5},{5,4},{6,7},{7,6},{8,9},{9,8},{10,11... | collective-permute-start | bytes 786440 | tf_op jit(solution)/shard_map/ppermute | solution.py:395
  34.2 11.3 %collective-permute-start.4 = (bf16[64,16,128]{2,1,0:T(8,128)(2,1)S(1)}, bf16[64,16,128]{2,1,0:T(8,128)(2,1)S(1)}, u32[]{:S(2)}, u32[]{:S(2)}) collective-permute-start(bf16[64,16,128]{2,1,0:T(8,128)(2,1)S(1)} %get-tuple-element.50), channel_id=1, source_target_pairs={{0,127},{1,2},{2,1},{3,4},{4,3},{5,6},{6,5},{7,8},{8,7},{9,10},{10... | collective-permute-start | bytes 786440 | tf_op jit(solution)/shard_map/ppermute | solution.py:394
  46.9 7.3 %collective-permute-start.7 = (bf16[64,16,128]{2,1,0:T(8,128)(2,1)S(1)}, bf16[64,16,128]{2,1,0:T(8,128)(2,1)S(1)}, u32[]{:S(2)}, u32[]{:S(2)}) collective-permute-start(bf16[64,16,128]{2,1,0:T(8,128)(2,1)S(1)} %get-tuple-element.59), channel_id=1, source_target_pairs={{0,1},{1,0},{2,3},{3,2},{4,5},{5,4},{6,7},{7,6},{8,9},{9,8},{10,11... | collective-permute-start | bytes 786440 | tf_op jit(solution)/shard_map/ppermute | solution.py:395
  47.0 11.5 %collective-permute-start.6 = (bf16[64,16,128]{2,1,0:T(8,128)(2,1)S(1)}, bf16[64,16,128]{2,1,0:T(8,128)(2,1)S(1)}, u32[]{:S(2)}, u32[]{:S(2)}) collective-permute-start(bf16[64,16,128]{2,1,0:T(8,128)(2,1)S(1)} %get-tuple-element.57), channel_id=1, source_target_pairs={{0,127},{1,2},{2,1},{3,4},{4,3},{5,6},{6,5},{7,8},{8,7},{9,10},{10... | collective-permute-start | bytes 786440 | tf_op jit(solution)/shard_map/ppermute | solution.py:394
  61.0 1.2 %collective-permute-start.8 = (f32[16,256]{1,0:T(8,128)S(1)}, f32[16,256]{1,0:T(8,128)S(1)}, u32[]{:S(2)}, u32[]{:S(2)}) collective-permute-start(f32[16,256]{1,0:T(8,128)S(1)} %get-tuple-element.66), channel_id=1, source_target_pairs={{0,1},{1,0},{2,3},{3,2},{4,5},{5,4},{6,7},{7,6},{8,9},{9,8},{10,11... | collective-permute-start | bytes 49160 | tf_op jit(solution)/shard_map/ppermute | solution.py:439
  62.2 3.7 %collective-permute-start.11 = (f32[16,256]{1,0:T(8,128)S(1)}, f32[16,256]{1,0:T(8,128)S(1)}, u32[]{:S(2)}, u32[]{:S(2)}) collective-permute-start(f32[16,256]{1,0:T(8,128)S(1)} %add.30), channel_id=1, source_target_pairs={{0,6},{1,7},{2,0},{3,1},{4,2},{5,3},{6,4},{7,5},{8,14},{9,15},{10,... | collective-permute-start | bytes 49160 | tf_op jit(solution)/shard_map/ppermute | solution.py:439
  62.2 5.3 %collective-permute-start.10 = (f32[16,256]{1,0:T(8,128)S(1)}, f32[16,256]{1,0:T(8,128)S(1)}, u32[]{:S(2)}, u32[]{:S(2)}) collective-permute-start(f32[16,256]{1,0:T(8,128)S(1)} %add.30), channel_id=1, source_target_pairs={{0,4},{1,5},{2,6},{3,7},{4,0},{5,1},{6,2},{7,3},{8,12},{9,13},{10,... | collective-permute-start | bytes 49160 | tf_op jit(solution)/shard_map/ppermute | solution.py:439
  62.3 6.3 %collective-permute-start.9 = (f32[16,256]{1,0:T(8,128)S(1)}, f32[16,256]{1,0:T(8,128)S(1)}, u32[]{:S(2)}, u32[]{:S(2)}) collective-permute-start(f32[16,256]{1,0:T(8,128)S(1)} %add.30), channel_id=1, source_target_pairs={{0,2},{1,3},{2,4},{3,5},{4,6},{5,7},{6,0},{7,1},{8,10},{9,11},{10,... | collective-permute-start | bytes 49160 | tf_op jit(solution)/shard_map/ppermute | solution.py:439
  68.6 3.7 %collective-permute-start.14 = (f32[16,256]{1,0:T(8,128)S(1)}, f32[16,256]{1,0:T(8,128)S(1)}, u32[]{:S(2)}, u32[]{:S(2)}) collective-permute-start(f32[16,256]{1,0:T(8,128)S(1)} %add_add_fusion.2), channel_id=1, source_target_pairs={{0,24},{1,25},{2,26},{3,27},{4,28},{5,29},{6,30},{7,31},{8,0},{9,1... | collective-permute-start | bytes 49160 | tf_op jit(solution)/shard_map/ppermute | solution.py:439
  68.7 5.5 %collective-permute-start.13 = (f32[16,256]{1,0:T(8,128)S(1)}, f32[16,256]{1,0:T(8,128)S(1)}, u32[]{:S(2)}, u32[]{:S(2)}) collective-permute-start(f32[16,256]{1,0:T(8,128)S(1)} %add_add_fusion.2), channel_id=1, source_target_pairs={{0,16},{1,17},{2,18},{3,19},{4,20},{5,21},{6,22},{7,23},{8,24},{9,... | collective-permute-start | bytes 49160 | tf_op jit(solution)/shard_map/ppermute | solution.py:439
  68.8 6.3 %collective-permute-start.12 = (f32[16,256]{1,0:T(8,128)S(1)}, f32[16,256]{1,0:T(8,128)S(1)}, u32[]{:S(2)}, u32[]{:S(2)}) collective-permute-start(f32[16,256]{1,0:T(8,128)S(1)} %add_add_fusion.2), channel_id=1, source_target_pairs={{0,8},{1,9},{2,10},{3,11},{4,12},{5,13},{6,14},{7,15},{8,16},{9,17... | collective-permute-start | bytes 49160 | tf_op jit(solution)/shard_map/ppermute | solution.py:439
  75.1 7.2 %collective-permute-start.17 = (f32[16,256]{1,0:T(8,128)S(1)}, f32[16,256]{1,0:T(8,128)S(1)}, u32[]{:S(2)}, u32[]{:S(2)}) collective-permute-start(f32[16,256]{1,0:T(8,128)S(1)} %add_add_fusion.1), channel_id=1, source_target_pairs={{0,96},{1,97},{2,98},{3,99},{4,100},{5,101},{6,102},{7,103},{8,104... | collective-permute-start | bytes 49160 | tf_op jit(solution)/shard_map/ppermute | solution.py:439
  80.8 5.2 %collective-permute-start.16 = (f32[16,256]{1,0:T(8,128)S(1)}, f32[16,256]{1,0:T(8,128)S(1)}, u32[]{:S(2)}, u32[]{:S(2)}) collective-permute-start(f32[16,256]{1,0:T(8,128)S(1)} %add_add_fusion.1), channel_id=1, source_target_pairs={{0,64},{1,65},{2,66},{3,67},{4,68},{5,69},{6,70},{7,71},{8,72},{9,... | collective-permute-start | bytes 49160 | tf_op jit(solution)/shard_map/ppermute | solution.py:439
  80.8 5.2 %collective-permute-start.15 = (f32[16,256]{1,0:T(8,128)S(1)}, f32[16,256]{1,0:T(8,128)S(1)}, u32[]{:S(2)}, u32[]{:S(2)}) collective-permute-start(f32[16,256]{1,0:T(8,128)S(1)} %add_add_fusion.1), channel_id=1, source_target_pairs={{0,32},{1,33},{2,34},{3,35},{4,36},{5,37},{6,38},{7,39},{8,40},{9,... | collective-permute-start | bytes 49160 | tf_op jit(solution)/shard_map/ppermute | solution.py:439

commit v6 on v5

--- a/solution.py
+++ b/solution.py
@@ -55,15 +55,15 @@
     half = send_a_ref.shape[0]
 
     def step(base, _):
-        for u in range(8):
-            g = base * 8 + u
+        for u in range(16):
+            g = base * 16 + u
             send_b_ref[g] = scaled_ref[plan_ref[SEND * LIST + half + g]]
-        for u in range(8):
-            g = base * 8 + u
+        for u in range(16):
+            g = base * 16 + u
             send_a_ref[g] = scaled_ref[plan_ref[SEND * LIST + g]]
         return 0
 
-    lax.fori_loop(0, half // 8, step, 0)
+    lax.fori_loop(0, half // 16, step, 0)
 
 
 def setup_kernel(index_in, ghost_in, values_ref, start_in, count_ref,
@@ -220,7 +220,7 @@
     half = got_ref.shape[0]
     side = tiles_ref.shape[1]
     blocks = scale_ref.shape[0]
-    spread_tiles(half, 32, acc_ref, lambda g: got_ref[g],
+    spread_tiles(half, 32 if last else 64, acc_ref, lambda g: got_ref[g],
                  lambda g: tiles_ref[plan_ref[SLOT * LIST + half + g]], lambda g: plan_ref[GROW * LIST + half + g])
 
     def close(b, where):
@@ -244,15 +244,15 @@
         return
 
     def close_step(base, _):
-        for u in range(8):
-            b = base * 8 + u
+        for u in range(16):
+            b = base * 16 + u
             where = pl.ds(pl.multiple_of(b * side, side), side)
             factor, value = close(b, where)
             vec_ref[:, where] = value
             scaled_ref[b] = (factor * value).astype(BF16)
         return 0
 
-    lax.fori_loop(0, blocks // 8, close_step, 0)
+    lax.fori_loop(0, blocks // 16, close_step, 0)
     pack(plan_ref, scaled_ref, send_a_ref, send_b_ref)
 
 

time: 92.7 us -> 92.3 us (level)
  Pallas kernels: 34.3 us -> 33.1 us
  transfers between devices with their start and end apart: 18 -> 18, of which waited for: 11 -> 12; matrix products, arithmetic and copies ran while one was open for 0% -> 0% of each run, Pallas kernels for 17% -> 16%
where the time goes in v6:
time: 92.3 us; the launch traced here: 92.2 us
  starting transfers between devices  42.1 us (46%)
  Pallas kernels  33.1 us (36%)
  waiting for transfers between devices  15.4 us (17%)
  between operations  1.56 us (2%)
    ppermute x4, starting transfers between devices, body(): got_b = lax.ppermute(send_b, AXIS, far)  30.8 us
    pallas_call x4, Pallas kernels, body(): pl.pallas_call(functools.partial(own_kernel, level - 1), out_shape=(acc_t...  15.2 us
    ppermute x10, waiting for transfers between devices, phase(): moved = moved + lax.ppermute(value, AXIS, perm)  14.2 us
    ppermute x10, starting transfers between devices, phase(): moved = moved + lax.ppermute(value, AXIS, perm)  11 us
    pallas_call x1, Pallas kernels, body(): pl.pallas_call(functools.partial(final_kernel, rows * n), out_shape=(shap...  6.35 us
    pallas_call x4, Pallas kernels, body(): pl.pallas_call(functools.partial(far_kernel, level, last), out_shape=outs...  6.03 us
    pallas_call x1, Pallas kernels, body(): pl.pallas_call(setup_kernel, out_shape=(shape((total, side, side), BF16),...  5.55 us
  transfers between devices with their start and end apart: 18, of which 12 were waited for; matrix products, arithmetic and copies ran while one was open for 0% of the time, Pallas kernels for 16%

profile of v6, /device:TPU:0, one launch (start us, length us, event | category | flops | bytes accessed | tf_op | source)
XLA Modules:
  0.0 92.2 jit_solution(1335365410501810951)
XLA Ops:
  1.3 0.0 copy-start
  1.3 5.6 %setup.1 = (bf16[256,128,128]{2,1,0:T(8,128)(2,1)S(1)}, s32[640]{0:T(1024)S(4)}, f32[128,8,128]{2,1,0:T(8,128)S(1)}, bf16[128,16,128]{2,1,0:T(8,128)(2,1)S(1)}, ...) custom-call(s32[2,256]{1,0:T(2,128)} %bitcast.7, s32[2,64]{1,0:T(2,128)} %bitcast.8, ...), custom_call_target="tpu_custom_call" | custom-call | tf_op jit(solution)/shard_map/setup/pallas_call | solution.py:376
  6.8 0.1 collective-permute-start.1
  6.9 9.0 %collective-permute-start = (bf16[64,16,128]{2,1,0:T(8,128)(2,1)S(1)}, bf16[64,16,128]{2,1,0:T(8,128)(2,1)S(1)}, u32[]{:S(2)}, u32[]{:S(2)}) collective-permute-start(bf16[64,16,128]{2,1,0:T(8,128)(2,1)S(1)} %get-tuple-element.38), channel_id=1, source_target_pairs={{0,127},{1,2},{2,1},{3,4},{4,3},{5,6},{6,5},{7,8},{8,7},{9,10},{10... | collective-permute-start | bytes 786440 | tf_op jit(solution)/shard_map/ppermute | solution.py:394
  16.0 0.0 collective-permute-done.1.refs_3_
  16.0 0.0 copy-done
  16.0 3.4 %own.4 = (f32[129,16,128]{2,1,0:T(8,128)S(1)}, bf16[32,16384]{1,0:T(8,128)(2,1)S(1)}, f32[16,256]{1,0:T(8,128)S(1)}) custom-call(s32[640]{0:T(1024)S(4)} %get-tuple-element.36.refs_0_, bf16[256,128,128]{2,1,0:T(8,128)(2,1)S(1)} %get-tuple-element.37.refs_1_, bf16[128,16,128]{2,1,0:T(8,128)(2,1)S(1)} %get-tuple-element.39.refs_2_, ...), custom_call_target="tpu_custom_call" | custom-call | flops 1000000000 | bytes 10000000 | tf_op jit(solution)/shard_map/own/pallas_call | solution.py:397
  19.4 0.6 collective-permute-done.refs_2_
  20.0 1.1 %far.4 = (f32[16,16384]{1,0:T(8,128)S(1)}, bf16[128,16,128]{2,1,0:T(8,128)(2,1)S(1)}, bf16[64,16,128]{2,1,0:T(8,128)(2,1)S(1)}, bf16[64,16,128]{2,1,0:T(8,128)(2,1)S(1)}, f32[129,16,128]{2,1,0:T(8,128)S(1)}) custom-call(s32[640]{0:T(1024)S(4)} %get-tuple-element.36.refs_0_, ...), custom_call_target="tpu_custom_call", output_to_operand_aliasing={{4}: (3, {})} | custom-call | tf_op jit(solution)/shard_map/far/pallas_call | solution.py:415
  21.1 0.1 collective-permute-start.3
  21.2 7.3 %collective-permute-start.2 = (bf16[64,16,128]{2,1,0:T(8,128)(2,1)S(1)}, bf16[64,16,128]{2,1,0:T(8,128)(2,1)S(1)}, u32[]{:S(2)}, u32[]{:S(2)}) collective-permute-start(bf16[64,16,128]{2,1,0:T(8,128)(2,1)S(1)} %get-tuple-element.43), channel_id=1, source_target_pairs={{0,127},{1,2},{2,1},{3,4},{4,3},{5,6},{6,5},{7,8},{8,7},{9,10},{10... | collective-permute-start | bytes 786440 | tf_op jit(solution)/shard_map/ppermute | solution.py:394
  28.5 0.0 collective-permute-done.3.refs_3_
  28.5 3.7 %own.5 = (f32[129,16,128]{2,1,0:T(8,128)S(1)}, bf16[32,16384]{1,0:T(8,128)(2,1)S(1)}, f32[16,256]{1,0:T(8,128)S(1)}) custom-call(s32[640]{0:T(1024)S(4)} %get-tuple-element.36.refs_0_, bf16[256,128,128]{2,1,0:T(8,128)(2,1)S(1)} %get-tuple-element.37.refs_1_, bf16[128,16,128]{2,1,0:T(8,128)(2,1)S(1)} %get-tuple-element.44.refs_2_, ...), custom_call_target="tpu_custom_call" | custom-call | flops 1000000000 | bytes 10000000 | tf_op jit(solution)/shard_map/own/pallas_call | solution.py:397
  32.2 0.4 collective-permute-done.2.refs_2_
  32.6 1.2 %far.5 = (f32[16,16384]{1,0:T(8,128)S(1)}, bf16[128,16,128]{2,1,0:T(8,128)(2,1)S(1)}, bf16[64,16,128]{2,1,0:T(8,128)(2,1)S(1)}, bf16[64,16,128]{2,1,0:T(8,128)(2,1)S(1)}, f32[129,16,128]{2,1,0:T(8,128)S(1)}) custom-call(s32[640]{0:T(1024)S(4)} %get-tuple-element.36.refs_0_, ...), custom_call_target="tpu_custom_call", output_to_operand_aliasing={{4}: (3, {})} | custom-call | tf_op jit(solution)/shard_map/far/pallas_call | solution.py:415
  33.8 0.1 collective-permute-start.5
  33.8 7.2 %collective-permute-start.4 = (bf16[64,16,128]{2,1,0:T(8,128)(2,1)S(1)}, bf16[64,16,128]{2,1,0:T(8,128)(2,1)S(1)}, u32[]{:S(2)}, u32[]{:S(2)}) collective-permute-start(bf16[64,16,128]{2,1,0:T(8,128)(2,1)S(1)} %get-tuple-element.50), channel_id=1, source_target_pairs={{0,127},{1,2},{2,1},{3,4},{4,3},{5,6},{6,5},{7,8},{8,7},{9,10},{10... | collective-permute-start | bytes 786440 | tf_op jit(solution)/shard_map/ppermute | solution.py:394
  41.1 0.0 collective-permute-done.5.refs_3_
  41.1 3.9 %own.6 = (f32[129,16,128]{2,1,0:T(8,128)S(1)}, bf16[32,16384]{1,0:T(8,128)(2,1)S(1)}, f32[16,256]{1,0:T(8,128)S(1)}) custom-call(s32[640]{0:T(1024)S(4)} %get-tuple-element.36.refs_0_, bf16[256,128,128]{2,1,0:T(8,128)(2,1)S(1)} %get-tuple-element.37.refs_1_, bf16[128,16,128]{2,1,0:T(8,128)(2,1)S(1)} %get-tuple-element.51.refs_2_, ...), custom_call_target="tpu_custom_call" | custom-call | flops 1000000000 | bytes 10000000 | tf_op jit(solution)/shard_map/own/pallas_call | solution.py:397
  45.0 0.1 collective-permute-done.4.refs_2_
  45.2 1.2 %far.6 = (f32[16,16384]{1,0:T(8,128)S(1)}, bf16[128,16,128]{2,1,0:T(8,128)(2,1)S(1)}, bf16[64,16,128]{2,1,0:T(8,128)(2,1)S(1)}, bf16[64,16,128]{2,1,0:T(8,128)(2,1)S(1)}, f32[129,16,128]{2,1,0:T(8,128)S(1)}) custom-call(s32[640]{0:T(1024)S(4)} %get-tuple-element.36.refs_0_, ...), custom_call_target="tpu_custom_call", output_to_operand_aliasing={{4}: (3, {})} | custom-call | tf_op jit(solution)/shard_map/far/pallas_call | solution.py:415
  46.4 0.1 collective-permute-start.7
  46.5 7.3 %collective-permute-start.6 = (bf16[64,16,128]{2,1,0:T(8,128)(2,1)S(1)}, bf16[64,16,128]{2,1,0:T(8,128)(2,1)S(1)}, u32[]{:S(2)}, u32[]{:S(2)}) collective-permute-start(bf16[64,16,128]{2,1,0:T(8,128)(2,1)S(1)} %get-tuple-element.57), channel_id=1, source_target_pairs={{0,127},{1,2},{2,1},{3,4},{4,3},{5,6},{6,5},{7,8},{8,7},{9,10},{10... | collective-permute-start | bytes 786440 | tf_op jit(solution)/shard_map/ppermute | solution.py:394
  53.7 0.0 collective-permute-done.7.refs_3_
  53.7 4.1 %own.7 = (f32[129,16,128]{2,1,0:T(8,128)S(1)}, bf16[32,16384]{1,0:T(8,128)(2,1)S(1)}, f32[16,256]{1,0:T(8,128)S(1)}) custom-call(s32[640]{0:T(1024)S(4)} %get-tuple-element.36.refs_0_, bf16[256,128,128]{2,1,0:T(8,128)(2,1)S(1)} %get-tuple-element.37.refs_1_, bf16[128,16,128]{2,1,0:T(8,128)(2,1)S(1)} %get-tuple-element.58.refs_2_, ...), custom_call_target="tpu_custom_call" | custom-call | flops 1000000000 | bytes 10000000 | tf_op jit(solution)/shard_map/own/pallas_call | solution.py:397
  57.9 0.0 collective-permute-done.6.refs_2_
  57.9 2.5 %far.7 = (bf16[32,16384]{1,0:T(8,128)(2,1)S(1)}, f32[16,256]{1,0:T(8,128)S(1)}, f32[129,16,128]{2,1,0:T(8,128)S(1)}) custom-call(s32[640]{0:T(1024)S(4)} %get-tuple-element.36.refs_0_, bf16[256,128,128]{2,1,0:T(8,128)(2,1)S(1)} %get-tuple-element.37.refs_1_, ...), custom_call_target="tpu_custom_call", output_to_operand_aliasing={{2}: (3, {})} | custom-call | tf_op jit(solution)/shard_map/far/pallas_call | solution.py:415
  60.4 0.2 collective-permute-start.8
  60.6 1.2 %collective-permute-done.8 = f32[16,256]{1,0:T(8,128)S(1)} collective-permute-done((f32[16,256]{1,0:T(8,128)S(1)}, f32[16,256]{1,0:T(8,128)S(1)}, u32[]{:S(2)}, u32[]{:S(2)}) %collective-permute-start.8) | collective-permute-done | bytes 16416 | tf_op jit(solution)/shard_map/ppermute | solution.py:439
  61.8 0.0 collective-permute-start.11
  61.8 0.1 collective-permute-start.10
  61.9 1.9 %collective-permute-start.9 = (f32[16,256]{1,0:T(8,128)S(1)}, f32[16,256]{1,0:T(8,128)S(1)}, u32[]{:S(2)}, u32[]{:S(2)}) collective-permute-start(f32[16,256]{1,0:T(8,128)S(1)} %add.30), channel_id=1, source_target_pairs={{0,2},{1,3},{2,4},{3,5},{4,6},{5,7},{6,0},{7,1},{8,10},{9,11},{10,... | collective-permute-start | bytes 49160 | tf_op jit(solution)/shard_map/ppermute | solution.py:439
  63.8 1.7 %collective-permute-done.11 = f32[16,256]{1,0:T(8,128)S(1)} collective-permute-done((f32[16,256]{1,0:T(8,128)S(1)}, f32[16,256]{1,0:T(8,128)S(1)}, u32[]{:S(2)}, u32[]{:S(2)}) %collective-permute-start.11) | collective-permute-done | bytes 16416 | tf_op jit(solution)/shard_map/ppermute | solution.py:439
  65.5 1.6 %collective-permute-done.10 = f32[16,256]{1,0:T(8,128)S(1)} collective-permute-done((f32[16,256]{1,0:T(8,128)S(1)}, f32[16,256]{1,0:T(8,128)S(1)}, u32[]{:S(2)}, u32[]{:S(2)}) %collective-permute-start.10) | collective-permute-done | bytes 16416 | tf_op jit(solution)/shard_map/ppermute | solution.py:439
  67.1 1.1 %collective-permute-done.9 = f32[16,256]{1,0:T(8,128)S(1)} collective-permute-done((f32[16,256]{1,0:T(8,128)S(1)}, f32[16,256]{1,0:T(8,128)S(1)}, u32[]{:S(2)}, u32[]{:S(2)}) %collective-permute-start.9) | collective-permute-done | bytes 16416 | tf_op jit(solution)/shard_map/ppermute | solution.py:439
  68.2 0.0 collective-permute-start.14
  68.2 0.1 collective-permute-start.13
  68.3 1.9 %collective-permute-start.12 = (f32[16,256]{1,0:T(8,128)S(1)}, f32[16,256]{1,0:T(8,128)S(1)}, u32[]{:S(2)}, u32[]{:S(2)}) collective-permute-start(f32[16,256]{1,0:T(8,128)S(1)} %add_add_fusion.2), channel_id=1, source_target_pairs={{0,8},{1,9},{2,10},{3,11},{4,12},{5,13},{6,14},{7,15},{8,16},{9,17... | collective-permute-start | bytes 49160 | tf_op jit(solution)/shard_map/ppermute | solution.py:439
  70.2 1.7 %collective-permute-done.14 = f32[16,256]{1,0:T(8,128)S(1)} collective-permute-done((f32[16,256]{1,0:T(8,128)S(1)}, f32[16,256]{1,0:T(8,128)S(1)}, u32[]{:S(2)}, u32[]{:S(2)}) %collective-permute-start.14) | collective-permute-done | bytes 16416 | tf_op jit(solution)/shard_map/ppermute | solution.py:439
  72.0 1.7 %collective-permute-done.13 = f32[16,256]{1,0:T(8,128)S(1)} collective-permute-done((f32[16,256]{1,0:T(8,128)S(1)}, f32[16,256]{1,0:T(8,128)S(1)}, u32[]{:S(2)}, u32[]{:S(2)}) %collective-permute-start.13) | collective-permute-done | bytes 16416 | tf_op jit(solution)/shard_map/ppermute | solution.py:439
  73.7 1.0 %collective-permute-done.12 = f32[16,256]{1,0:T(8,128)S(1)} collective-permute-done((f32[16,256]{1,0:T(8,128)S(1)}, f32[16,256]{1,0:T(8,128)S(1)}, u32[]{:S(2)}, u32[]{:S(2)}) %collective-permute-start.12) | collective-permute-done | bytes 16416 | tf_op jit(solution)/shard_map/ppermute | solution.py:439
  74.6 5.8 %collective-permute-start.17 = (f32[16,256]{1,0:T(8,128)S(1)}, f32[16,256]{1,0:T(8,128)S(1)}, u32[]{:S(2)}, u32[]{:S(2)}) collective-permute-start(f32[16,256]{1,0:T(8,128)S(1)} %add_add_fusion.1), channel_id=1, source_target_pairs={{0,96},{1,97},{2,98},{3,99},{4,100},{5,101},{6,102},{7,103},{8,104... | collective-permute-start | bytes 49160 | tf_op jit(solution)/shard_map/ppermute | solution.py:439
  80.5 0.0 collective-permute-start.16
  80.5 0.9 %collective-permute-start.15 = (f32[16,256]{1,0:T(8,128)S(1)}, f32[16,256]{1,0:T(8,128)S(1)}, u32[]{:S(2)}, u32[]{:S(2)}) collective-permute-start(f32[16,256]{1,0:T(8,128)S(1)} %add_add_fusion.1), channel_id=1, source_target_pairs={{0,32},{1,33},{2,34},{3,35},{4,36},{5,37},{6,38},{7,39},{8,40},{9,... | collective-permute-start | bytes 49160 | tf_op jit(solution)/shard_map/ppermute | solution.py:439
  81.4 0.5 collective-permute-done.17
  81.9 3.8 %collective-permute-done.16 = f32[16,256]{1,0:T(8,128)S(1)} collective-permute-done((f32[16,256]{1,0:T(8,128)S(1)}, f32[16,256]{1,0:T(8,128)S(1)}, u32[]{:S(2)}, u32[]{:S(2)}) %collective-permute-start.16) | collective-permute-done | bytes 16416 | tf_op jit(solution)/shard_map/ppermute | solution.py:439
  85.7 0.0 collective-permute-done.15
  85.7 6.3 %final.1 = (f32[80,16384]{1,0:T(8,128)}, f32[80,80]{1,0:T(8,128)}) custom-call(f32[16,256]{1,0:T(8,128)S(1)} %add_add_fusion.gram_in, bf16[32,16384]{1,0:T(8,128)(2,1)S(1)} %get-tuple-element.47.refs_5_.refs_6_.refs_0_, bf16[32,16384]{1,0:T(8,128)(2,1)S(1)} %get-tuple-element.54.refs_6_.refs_7_.refs_1_, ...), custom_call_target="tpu_custom_call" | custom-call | tf_op jit(solution)/shard_map/final/pallas_call | solution.py:452
  (4 shorter events, 0.0 us)
Async XLA Ops:
  1.3 14.7 %copy-start = (f32[16384,16]{0,1:T(8,128)S(1)}, f32[16384,16]{0,1:T(8,128)}, u32[]{:S(2)}) copy-start(f32[16384,16]{0,1:T(8,128)} %param.5) | copy-start | bytes 3145732
  6.8 9.1 %collective-permute-start.1 = (bf16[64,16,128]{2,1,0:T(8,128)(2,1)S(1)}, bf16[64,16,128]{2,1,0:T(8,128)(2,1)S(1)}, u32[]{:S(2)}, u32[]{:S(2)}) collective-permute-start(bf16[64,16,128]{2,1,0:T(8,128)(2,1)S(1)} %get-tuple-element.40), channel_id=1, source_target_pairs={{0,1},{1,0},{2,3},{3,2},{4,5},{5,4},{6,7},{7,6},{8,9},{9,8},{10,11... | collective-permute-start | bytes 786440 | tf_op jit(solution)/shard_map/ppermute | solution.py:395
  6.9 13.1 %collective-permute-start = (bf16[64,16,128]{2,1,0:T(8,128)(2,1)S(1)}, bf16[64,16,128]{2,1,0:T(8,128)(2,1)S(1)}, u32[]{:S(2)}, u32[]{:S(2)}) collective-permute-start(bf16[64,16,128]{2,1,0:T(8,128)(2,1)S(1)} %get-tuple-element.38), channel_id=1, source_target_pairs={{0,127},{1,2},{2,1},{3,4},{4,3},{5,6},{6,5},{7,8},{8,7},{9,10},{10... | collective-permute-start | bytes 786440 | tf_op jit(solution)/shard_map/ppermute | solution.py:394
  21.1 7.3 %collective-permute-start.3 = (bf16[64,16,128]{2,1,0:T(8,128)(2,1)S(1)}, bf16[64,16,128]{2,1,0:T(8,128)(2,1)S(1)}, u32[]{:S(2)}, u32[]{:S(2)}) collective-permute-start(bf16[64,16,128]{2,1,0:T(8,128)(2,1)S(1)} %get-tuple-element.45), channel_id=1, source_target_pairs={{0,1},{1,0},{2,3},{3,2},{4,5},{5,4},{6,7},{7,6},{8,9},{9,8},{10,11... | collective-permute-start | bytes 786440 | tf_op jit(solution)/shard_map/ppermute | solution.py:395
  21.2 11.3 %collective-permute-start.2 = (bf16[64,16,128]{2,1,0:T(8,128)(2,1)S(1)}, bf16[64,16,128]{2,1,0:T(8,128)(2,1)S(1)}, u32[]{:S(2)}, u32[]{:S(2)}) collective-permute-start(bf16[64,16,128]{2,1,0:T(8,128)(2,1)S(1)} %get-tuple-element.43), channel_id=1, source_target_pairs={{0,127},{1,2},{2,1},{3,4},{4,3},{5,6},{6,5},{7,8},{8,7},{9,10},{10... | collective-permute-start | bytes 786440 | tf_op jit(solution)/shard_map/ppermute | solution.py:394
  33.8 7.3 %collective-permute-start.5 = (bf16[64,16,128]{2,1,0:T(8,128)(2,1)S(1)}, bf16[64,16,128]{2,1,0:T(8,128)(2,1)S(1)}, u32[]{:S(2)}, u32[]{:S(2)}) collective-permute-start(bf16[64,16,128]{2,1,0:T(8,128)(2,1)S(1)} %get-tuple-element.52), channel_id=1, source_target_pairs={{0,1},{1,0},{2,3},{3,2},{4,5},{5,4},{6,7},{7,6},{8,9},{9,8},{10,11... | collective-permute-start | bytes 786440 | tf_op jit(solution)/shard_map/ppermute | solution.py:395
  33.8 11.3 %collective-permute-start.4 = (bf16[64,16,128]{2,1,0:T(8,128)(2,1)S(1)}, bf16[64,16,128]{2,1,0:T(8,128)(2,1)S(1)}, u32[]{:S(2)}, u32[]{:S(2)}) collective-permute-start(bf16[64,16,128]{2,1,0:T(8,128)(2,1)S(1)} %get-tuple-element.50), channel_id=1, source_target_pairs={{0,127},{1,2},{2,1},{3,4},{4,3},{5,6},{6,5},{7,8},{8,7},{9,10},{10... | collective-permute-start | bytes 786440 | tf_op jit(solution)/shard_map/ppermute | solution.py:394
  46.4 7.3 %collective-permute-start.7 = (bf16[64,16,128]{2,1,0:T(8,128)(2,1)S(1)}, bf16[64,16,128]{2,1,0:T(8,128)(2,1)S(1)}, u32[]{:S(2)}, u32[]{:S(2)}) collective-permute-start(bf16[64,16,128]{2,1,0:T(8,128)(2,1)S(1)} %get-tuple-element.59), channel_id=1, source_target_pairs={{0,1},{1,0},{2,3},{3,2},{4,5},{5,4},{6,7},{7,6},{8,9},{9,8},{10,11... | collective-permute-start | bytes 786440 | tf_op jit(solution)/shard_map/ppermute | solution.py:395
  46.5 11.4 %collective-permute-start.6 = (bf16[64,16,128]{2,1,0:T(8,128)(2,1)S(1)}, bf16[64,16,128]{2,1,0:T(8,128)(2,1)S(1)}, u32[]{:S(2)}, u32[]{:S(2)}) collective-permute-start(bf16[64,16,128]{2,1,0:T(8,128)(2,1)S(1)} %get-tuple-element.57), channel_id=1, source_target_pairs={{0,127},{1,2},{2,1},{3,4},{4,3},{5,6},{6,5},{7,8},{8,7},{9,10},{10... | collective-permute-start | bytes 786440 | tf_op jit(solution)/shard_map/ppermute | solution.py:394
  60.4 1.4 %collective-permute-start.8 = (f32[16,256]{1,0:T(8,128)S(1)}, f32[16,256]{1,0:T(8,128)S(1)}, u32[]{:S(2)}, u32[]{:S(2)}) collective-permute-start(f32[16,256]{1,0:T(8,128)S(1)} %get-tuple-element.66), channel_id=1, source_target_pairs={{0,1},{1,0},{2,3},{3,2},{4,5},{5,4},{6,7},{7,6},{8,9},{9,8},{10,11... | collective-permute-start | bytes 49160 | tf_op jit(solution)/shard_map/ppermute | solution.py:439
  61.8 3.7 %collective-permute-start.11 = (f32[16,256]{1,0:T(8,128)S(1)}, f32[16,256]{1,0:T(8,128)S(1)}, u32[]{:S(2)}, u32[]{:S(2)}) collective-permute-start(f32[16,256]{1,0:T(8,128)S(1)} %add.30), channel_id=1, source_target_pairs={{0,6},{1,7},{2,0},{3,1},{4,2},{5,3},{6,4},{7,5},{8,14},{9,15},{10,... | collective-permute-start | bytes 49160 | tf_op jit(solution)/shard_map/ppermute | solution.py:439
  61.8 5.3 %collective-permute-start.10 = (f32[16,256]{1,0:T(8,128)S(1)}, f32[16,256]{1,0:T(8,128)S(1)}, u32[]{:S(2)}, u32[]{:S(2)}) collective-permute-start(f32[16,256]{1,0:T(8,128)S(1)} %add.30), channel_id=1, source_target_pairs={{0,4},{1,5},{2,6},{3,7},{4,0},{5,1},{6,2},{7,3},{8,12},{9,13},{10,... | collective-permute-start | bytes 49160 | tf_op jit(solution)/shard_map/ppermute | solution.py:439
  61.9 6.3 %collective-permute-start.9 = (f32[16,256]{1,0:T(8,128)S(1)}, f32[16,256]{1,0:T(8,128)S(1)}, u32[]{:S(2)}, u32[]{:S(2)}) collective-permute-start(f32[16,256]{1,0:T(8,128)S(1)} %add.30), channel_id=1, source_target_pairs={{0,2},{1,3},{2,4},{3,5},{4,6},{5,7},{6,0},{7,1},{8,10},{9,11},{10,... | collective-permute-start | bytes 49160 | tf_op jit(solution)/shard_map/ppermute | solution.py:439
  68.2 3.7 %collective-permute-start.14 = (f32[16,256]{1,0:T(8,128)S(1)}, f32[16,256]{1,0:T(8,128)S(1)}, u32[]{:S(2)}, u32[]{:S(2)}) collective-permute-start(f32[16,256]{1,0:T(8,128)S(1)} %add_add_fusion.2), channel_id=1, source_target_pairs={{0,24},{1,25},{2,26},{3,27},{4,28},{5,29},{6,30},{7,31},{8,0},{9,1... | collective-permute-start | bytes 49160 | tf_op jit(solution)/shard_map/ppermute | solution.py:439
  68.2 5.5 %collective-permute-start.13 = (f32[16,256]{1,0:T(8,128)S(1)}, f32[16,256]{1,0:T(8,128)S(1)}, u32[]{:S(2)}, u32[]{:S(2)}) collective-permute-start(f32[16,256]{1,0:T(8,128)S(1)} %add_add_fusion.2), channel_id=1, source_target_pairs={{0,16},{1,17},{2,18},{3,19},{4,20},{5,21},{6,22},{7,23},{8,24},{9,... | collective-permute-start | bytes 49160 | tf_op jit(solution)/shard_map/ppermute | solution.py:439
  68.3 6.3 %collective-permute-start.12 = (f32[16,256]{1,0:T(8,128)S(1)}, f32[16,256]{1,0:T(8,128)S(1)}, u32[]{:S(2)}, u32[]{:S(2)}) collective-permute-start(f32[16,256]{1,0:T(8,128)S(1)} %add_add_fusion.2), channel_id=1, source_target_pairs={{0,8},{1,9},{2,10},{3,11},{4,12},{5,13},{6,14},{7,15},{8,16},{9,17... | collective-permute-start | bytes 49160 | tf_op jit(solution)/shard_map/ppermute | solution.py:439
  74.6 7.3 %collective-permute-start.17 = (f32[16,256]{1,0:T(8,128)S(1)}, f32[16,256]{1,0:T(8,128)S(1)}, u32[]{:S(2)}, u32[]{:S(2)}) collective-permute-start(f32[16,256]{1,0:T(8,128)S(1)} %add_add_fusion.1), channel_id=1, source_target_pairs={{0,96},{1,97},{2,98},{3,99},{4,100},{5,101},{6,102},{7,103},{8,104... | collective-permute-start | bytes 49160 | tf_op jit(solution)/shard_map/ppermute | solution.py:439
  80.5 5.2 %collective-permute-start.16 = (f32[16,256]{1,0:T(8,128)S(1)}, f32[16,256]{1,0:T(8,128)S(1)}, u32[]{:S(2)}, u32[]{:S(2)}) collective-permute-start(f32[16,256]{1,0:T(8,128)S(1)} %add_add_fusion.1), channel_id=1, source_target_pairs={{0,64},{1,65},{2,66},{3,67},{4,68},{5,69},{6,70},{7,71},{8,72},{9,... | collective-permute-start | bytes 49160 | tf_op jit(solution)/shard_map/ppermute | solution.py:439
  80.5 5.2 %collective-permute-start.15 = (f32[16,256]{1,0:T(8,128)S(1)}, f32[16,256]{1,0:T(8,128)S(1)}, u32[]{:S(2)}, u32[]{:S(2)}) collective-permute-start(f32[16,256]{1,0:T(8,128)S(1)} %add_add_fusion.1), channel_id=1, source_target_pairs={{0,32},{1,33},{2,34},{3,35},{4,36},{5,37},{6,38},{7,39},{8,40},{9,... | collective-permute-start | bytes 49160 | tf_op jit(solution)/shard_map/ppermute | solution.py:439

commit v7 on v6

--- a/solution.py
+++ b/solution.py
@@ -134,15 +134,15 @@
     small[2].wait()
 
     def scale_step(base, _):
-        for u in range(8):
-            b = base * 8 + u
+        for u in range(16):
+            b = base * 16 + u
             factor = lax.rsqrt(1.0 + acc_ref[b])
             scale_ref[b] = factor
             at = pl.ds(pl.multiple_of(b * side, side), side)
             scaled_ref[b] = (join([factor, factor], 0) * start_ref[:, at]).astype(BF16)
         return 0
 
-    lax.fori_loop(0, blocks // 8, scale_step, 0)
+    lax.fori_loop(0, blocks // 16, scale_step, 0)
     pack(plan_ref, scaled_ref, send_a_ref, send_b_ref)
 
 
@@ -391,8 +391,8 @@
     gram = None
     for level in range(1, STEPS + 1):
         last = level == STEPS
+        got_a = lax.ppermute(send_a, AXIS, near)
         got_b = lax.ppermute(send_b, AXIS, far)
-        got_a = lax.ppermute(send_a, AXIS, near)
         args = [plan, tiles, scaled, got_a, vectors[-1]] + parts + ([gram] if gram is not None else [])
         acc, part, gram = pl.pallas_call(
             functools.partial(own_kernel, level - 1),

time: 92.3 us -> 92.2 us (level)
  transfers between devices with their start and end apart: 18 -> 18, of which waited for: 12 -> 11; matrix products, arithmetic and copies ran while one was open for 0% -> 0% of each run, Pallas kernels for 16% -> 17%
where the time goes in v7:
time: 92.2 us; the launch traced here: 92.1 us
  starting transfers between devices  41.9 us (45%)
  Pallas kernels  33.5 us (36%)
  waiting for transfers between devices  15.1 us (16%)
  between operations  1.56 us (2%)
    ppermute x4, starting transfers between devices, body(): got_b = lax.ppermute(send_b, AXIS, far)  30.6 us
    pallas_call x4, Pallas kernels, body(): pl.pallas_call(functools.partial(own_kernel, level - 1), out_shape=(acc_t...  15.5 us
    ppermute x10, waiting for transfers between devices, phase(): moved = moved + lax.ppermute(value, AXIS, perm)  14.2 us
    ppermute x10, starting transfers between devices, phase(): moved = moved + lax.ppermute(value, AXIS, perm)  10.9 us
    pallas_call x1, Pallas kernels, body(): pl.pallas_call(functools.partial(final_kernel, rows * n), out_shape=(shap...  6.35 us
    pallas_call x4, Pallas kernels, body(): pl.pallas_call(functools.partial(far_kernel, level, last), out_shape=outs...  6.04 us
    pallas_call x1, Pallas kernels, body(): pl.pallas_call(setup_kernel, out_shape=(shape((total, side, side), BF16),...  5.59 us
  transfers between devices with their start and end apart: 18, of which 11 were waited for; matrix products, arithmetic and copies ran while one was open for 0% of the time, Pallas kernels for 17%

profile of v7, /device:TPU:0, one launch (start us, length us, event | category | flops | bytes accessed | tf_op | source)
XLA Modules:
  0.0 92.1 jit_solution(5679287863108895596)
XLA Ops:
  1.3 0.0 copy-start
  1.3 5.6 %setup.1 = (bf16[256,128,128]{2,1,0:T(8,128)(2,1)S(1)}, s32[640]{0:T(1024)S(4)}, f32[128,8,128]{2,1,0:T(8,128)S(1)}, bf16[128,16,128]{2,1,0:T(8,128)(2,1)S(1)}, ...) custom-call(s32[2,256]{1,0:T(2,128)} %bitcast.7, s32[2,64]{1,0:T(2,128)} %bitcast.8, ...), custom_call_target="tpu_custom_call" | custom-call | tf_op jit(solution)/shard_map/setup/pallas_call | solution.py:376
  6.9 0.1 collective-permute-start.1
  7.0 8.8 %collective-permute-start = (bf16[64,16,128]{2,1,0:T(8,128)(2,1)S(1)}, bf16[64,16,128]{2,1,0:T(8,128)(2,1)S(1)}, u32[]{:S(2)}, u32[]{:S(2)}) collective-permute-start(bf16[64,16,128]{2,1,0:T(8,128)(2,1)S(1)} %get-tuple-element.38), channel_id=1, source_target_pairs={{0,127},{1,2},{2,1},{3,4},{4,3},{5,6},{6,5},{7,8},{8,7},{9,10},{10... | collective-permute-start | bytes 786440 | tf_op jit(solution)/shard_map/ppermute | solution.py:395
  15.8 0.0 collective-permute-done.1.refs_3_
  15.8 0.0 copy-done
  15.8 3.5 %own.4 = (f32[129,16,128]{2,1,0:T(8,128)S(1)}, bf16[32,16384]{1,0:T(8,128)(2,1)S(1)}, f32[16,256]{1,0:T(8,128)S(1)}) custom-call(s32[640]{0:T(1024)S(4)} %get-tuple-element.36.refs_0_, bf16[256,128,128]{2,1,0:T(8,128)(2,1)S(1)} %get-tuple-element.37.refs_1_, bf16[128,16,128]{2,1,0:T(8,128)(2,1)S(1)} %get-tuple-element.39.refs_2_, ...), custom_call_target="tpu_custom_call" | custom-call | flops 1000000000 | bytes 10000000 | tf_op jit(solution)/shard_map/own/pallas_call | solution.py:397
  19.3 0.5 collective-permute-done.refs_2_
  19.9 1.1 %far.4 = (f32[16,16384]{1,0:T(8,128)S(1)}, bf16[128,16,128]{2,1,0:T(8,128)(2,1)S(1)}, bf16[64,16,128]{2,1,0:T(8,128)(2,1)S(1)}, bf16[64,16,128]{2,1,0:T(8,128)(2,1)S(1)}, f32[129,16,128]{2,1,0:T(8,128)S(1)}) custom-call(s32[640]{0:T(1024)S(4)} %get-tuple-element.36.refs_0_, ...), custom_call_target="tpu_custom_call", output_to_operand_aliasing={{4}: (3, {})} | custom-call | tf_op jit(solution)/shard_map/far/pallas_call | solution.py:415
  21.0 0.1 collective-permute-start.3
  21.1 7.3 %collective-permute-start.2 = (bf16[64,16,128]{2,1,0:T(8,128)(2,1)S(1)}, bf16[64,16,128]{2,1,0:T(8,128)(2,1)S(1)}, u32[]{:S(2)}, u32[]{:S(2)}) collective-permute-start(bf16[64,16,128]{2,1,0:T(8,128)(2,1)S(1)} %get-tuple-element.43), channel_id=1, source_target_pairs={{0,127},{1,2},{2,1},{3,4},{4,3},{5,6},{6,5},{7,8},{8,7},{9,10},{10... | collective-permute-start | bytes 786440 | tf_op jit(solution)/shard_map/ppermute | solution.py:395
  28.4 0.0 collective-permute-done.3.refs_3_
  28.4 3.8 %own.5 = (f32[129,16,128]{2,1,0:T(8,128)S(1)}, bf16[32,16384]{1,0:T(8,128)(2,1)S(1)}, f32[16,256]{1,0:T(8,128)S(1)}) custom-call(s32[640]{0:T(1024)S(4)} %get-tuple-element.36.refs_0_, bf16[256,128,128]{2,1,0:T(8,128)(2,1)S(1)} %get-tuple-element.37.refs_1_, bf16[128,16,128]{2,1,0:T(8,128)(2,1)S(1)} %get-tuple-element.44.refs_2_, ...), custom_call_target="tpu_custom_call" | custom-call | flops 1000000000 | bytes 10000000 | tf_op jit(solution)/shard_map/own/pallas_call | solution.py:397
  32.1 0.3 collective-permute-done.2.refs_2_
  32.4 1.2 %far.5 = (f32[16,16384]{1,0:T(8,128)S(1)}, bf16[128,16,128]{2,1,0:T(8,128)(2,1)S(1)}, bf16[64,16,128]{2,1,0:T(8,128)(2,1)S(1)}, bf16[64,16,128]{2,1,0:T(8,128)(2,1)S(1)}, f32[129,16,128]{2,1,0:T(8,128)S(1)}) custom-call(s32[640]{0:T(1024)S(4)} %get-tuple-element.36.refs_0_, ...), custom_call_target="tpu_custom_call", output_to_operand_aliasing={{4}: (3, {})} | custom-call | tf_op jit(solution)/shard_map/far/pallas_call | solution.py:415
  33.6 0.1 collective-permute-start.5
  33.7 7.2 %collective-permute-start.4 = (bf16[64,16,128]{2,1,0:T(8,128)(2,1)S(1)}, bf16[64,16,128]{2,1,0:T(8,128)(2,1)S(1)}, u32[]{:S(2)}, u32[]{:S(2)}) collective-permute-start(bf16[64,16,128]{2,1,0:T(8,128)(2,1)S(1)} %get-tuple-element.50), channel_id=1, source_target_pairs={{0,127},{1,2},{2,1},{3,4},{4,3},{5,6},{6,5},{7,8},{8,7},{9,10},{10... | collective-permute-start | bytes 786440 | tf_op jit(solution)/shard_map/ppermute | solution.py:395
  41.0 0.0 collective-permute-done.5.refs_3_
  41.0 4.0 %own.6 = (f32[129,16,128]{2,1,0:T(8,128)S(1)}, bf16[32,16384]{1,0:T(8,128)(2,1)S(1)}, f32[16,256]{1,0:T(8,128)S(1)}) custom-call(s32[640]{0:T(1024)S(4)} %get-tuple-element.36.refs_0_, bf16[256,128,128]{2,1,0:T(8,128)(2,1)S(1)} %get-tuple-element.37.refs_1_, bf16[128,16,128]{2,1,0:T(8,128)(2,1)S(1)} %get-tuple-element.51.refs_2_, ...), custom_call_target="tpu_custom_call" | custom-call | flops 1000000000 | bytes 10000000 | tf_op jit(solution)/shard_map/own/pallas_call | solution.py:397
  45.0 0.0 collective-permute-done.4.refs_2_
  45.0 1.2 %far.6 = (f32[16,16384]{1,0:T(8,128)S(1)}, bf16[128,16,128]{2,1,0:T(8,128)(2,1)S(1)}, bf16[64,16,128]{2,1,0:T(8,128)(2,1)S(1)}, bf16[64,16,128]{2,1,0:T(8,128)(2,1)S(1)}, f32[129,16,128]{2,1,0:T(8,128)S(1)}) custom-call(s32[640]{0:T(1024)S(4)} %get-tuple-element.36.refs_0_, ...), custom_call_target="tpu_custom_call", output_to_operand_aliasing={{4}: (3, {})} | custom-call | tf_op jit(solution)/shard_map/far/pallas_call | solution.py:415
  46.2 0.1 collective-permute-start.7
  46.3 7.2 %collective-permute-start.6 = (bf16[64,16,128]{2,1,0:T(8,128)(2,1)S(1)}, bf16[64,16,128]{2,1,0:T(8,128)(2,1)S(1)}, u32[]{:S(2)}, u32[]{:S(2)}) collective-permute-start(bf16[64,16,128]{2,1,0:T(8,128)(2,1)S(1)} %get-tuple-element.57), channel_id=1, source_target_pairs={{0,127},{1,2},{2,1},{3,4},{4,3},{5,6},{6,5},{7,8},{8,7},{9,10},{10... | collective-permute-start | bytes 786440 | tf_op jit(solution)/shard_map/ppermute | solution.py:395
  53.6 0.0 collective-permute-done.7.refs_3_
  53.6 4.2 %own.7 = (f32[129,16,128]{2,1,0:T(8,128)S(1)}, bf16[32,16384]{1,0:T(8,128)(2,1)S(1)}, f32[16,256]{1,0:T(8,128)S(1)}) custom-call(s32[640]{0:T(1024)S(4)} %get-tuple-element.36.refs_0_, bf16[256,128,128]{2,1,0:T(8,128)(2,1)S(1)} %get-tuple-element.37.refs_1_, bf16[128,16,128]{2,1,0:T(8,128)(2,1)S(1)} %get-tuple-element.58.refs_2_, ...), custom_call_target="tpu_custom_call" | custom-call | flops 1000000000 | bytes 10000000 | tf_op jit(solution)/shard_map/own/pallas_call | solution.py:397
  57.8 0.0 collective-permute-done.6.refs_2_
  57.8 2.5 %far.7 = (bf16[32,16384]{1,0:T(8,128)(2,1)S(1)}, f32[16,256]{1,0:T(8,128)S(1)}, f32[129,16,128]{2,1,0:T(8,128)S(1)}) custom-call(s32[640]{0:T(1024)S(4)} %get-tuple-element.36.refs_0_, bf16[256,128,128]{2,1,0:T(8,128)(2,1)S(1)} %get-tuple-element.37.refs_1_, ...), custom_call_target="tpu_custom_call", output_to_operand_aliasing={{2}: (3, {})} | custom-call | tf_op jit(solution)/shard_map/far/pallas_call | solution.py:415
  60.3 0.2 collective-permute-start.8
  60.6 1.2 %collective-permute-done.8 = f32[16,256]{1,0:T(8,128)S(1)} collective-permute-done((f32[16,256]{1,0:T(8,128)S(1)}, f32[16,256]{1,0:T(8,128)S(1)}, u32[]{:S(2)}, u32[]{:S(2)}) %collective-permute-start.8) | collective-permute-done | bytes 16416 | tf_op jit(solution)/shard_map/ppermute | solution.py:439
  61.7 0.0 collective-permute-start.11
  61.7 0.1 collective-permute-start.10
  61.8 1.9 %collective-permute-start.9 = (f32[16,256]{1,0:T(8,128)S(1)}, f32[16,256]{1,0:T(8,128)S(1)}, u32[]{:S(2)}, u32[]{:S(2)}) collective-permute-start(f32[16,256]{1,0:T(8,128)S(1)} %add.30), channel_id=1, source_target_pairs={{0,2},{1,3},{2,4},{3,5},{4,6},{5,7},{6,0},{7,1},{8,10},{9,11},{10,... | collective-permute-start | bytes 49160 | tf_op jit(solution)/shard_map/ppermute | solution.py:439
  63.8 1.7 %collective-permute-done.11 = f32[16,256]{1,0:T(8,128)S(1)} collective-permute-done((f32[16,256]{1,0:T(8,128)S(1)}, f32[16,256]{1,0:T(8,128)S(1)}, u32[]{:S(2)}, u32[]{:S(2)}) %collective-permute-start.11) | collective-permute-done | bytes 16416 | tf_op jit(solution)/shard_map/ppermute | solution.py:439
  65.5 1.6 %collective-permute-done.10 = f32[16,256]{1,0:T(8,128)S(1)} collective-permute-done((f32[16,256]{1,0:T(8,128)S(1)}, f32[16,256]{1,0:T(8,128)S(1)}, u32[]{:S(2)}, u32[]{:S(2)}) %collective-permute-start.10) | collective-permute-done | bytes 16416 | tf_op jit(solution)/shard_map/ppermute | solution.py:439
  67.1 1.1 %collective-permute-done.9 = f32[16,256]{1,0:T(8,128)S(1)} collective-permute-done((f32[16,256]{1,0:T(8,128)S(1)}, f32[16,256]{1,0:T(8,128)S(1)}, u32[]{:S(2)}, u32[]{:S(2)}) %collective-permute-start.9) | collective-permute-done | bytes 16416 | tf_op jit(solution)/shard_map/ppermute | solution.py:439
  68.2 0.0 collective-permute-start.14
  68.2 0.1 collective-permute-start.13
  68.3 1.9 %collective-permute-start.12 = (f32[16,256]{1,0:T(8,128)S(1)}, f32[16,256]{1,0:T(8,128)S(1)}, u32[]{:S(2)}, u32[]{:S(2)}) collective-permute-start(f32[16,256]{1,0:T(8,128)S(1)} %add_add_fusion.2), channel_id=1, source_target_pairs={{0,8},{1,9},{2,10},{3,11},{4,12},{5,13},{6,14},{7,15},{8,16},{9,17... | collective-permute-start | bytes 49160 | tf_op jit(solution)/shard_map/ppermute | solution.py:439
  70.2 1.7 %collective-permute-done.14 = f32[16,256]{1,0:T(8,128)S(1)} collective-permute-done((f32[16,256]{1,0:T(8,128)S(1)}, f32[16,256]{1,0:T(8,128)S(1)}, u32[]{:S(2)}, u32[]{:S(2)}) %collective-permute-start.14) | collective-permute-done | bytes 16416 | tf_op jit(solution)/shard_map/ppermute | solution.py:439
  71.9 1.7 %collective-permute-done.13 = f32[16,256]{1,0:T(8,128)S(1)} collective-permute-done((f32[16,256]{1,0:T(8,128)S(1)}, f32[16,256]{1,0:T(8,128)S(1)}, u32[]{:S(2)}, u32[]{:S(2)}) %collective-permute-start.13) | collective-permute-done | bytes 16416 | tf_op jit(solution)/shard_map/ppermute | solution.py:439
  73.6 1.0 %collective-permute-done.12 = f32[16,256]{1,0:T(8,128)S(1)} collective-permute-done((f32[16,256]{1,0:T(8,128)S(1)}, f32[16,256]{1,0:T(8,128)S(1)}, u32[]{:S(2)}, u32[]{:S(2)}) %collective-permute-start.12) | collective-permute-done | bytes 16416 | tf_op jit(solution)/shard_map/ppermute | solution.py:439
  74.6 5.7 %collective-permute-start.17 = (f32[16,256]{1,0:T(8,128)S(1)}, f32[16,256]{1,0:T(8,128)S(1)}, u32[]{:S(2)}, u32[]{:S(2)}) collective-permute-start(f32[16,256]{1,0:T(8,128)S(1)} %add_add_fusion.1), channel_id=1, source_target_pairs={{0,96},{1,97},{2,98},{3,99},{4,100},{5,101},{6,102},{7,103},{8,104... | collective-permute-start | bytes 49160 | tf_op jit(solution)/shard_map/ppermute | solution.py:439
  80.3 0.0 collective-permute-start.16
  80.3 0.9 %collective-permute-start.15 = (f32[16,256]{1,0:T(8,128)S(1)}, f32[16,256]{1,0:T(8,128)S(1)}, u32[]{:S(2)}, u32[]{:S(2)}) collective-permute-start(f32[16,256]{1,0:T(8,128)S(1)} %add_add_fusion.1), channel_id=1, source_target_pairs={{0,32},{1,33},{2,34},{3,35},{4,36},{5,37},{6,38},{7,39},{8,40},{9,... | collective-permute-start | bytes 49160 | tf_op jit(solution)/shard_map/ppermute | solution.py:439
  81.3 0.5 collective-permute-done.17
  81.8 3.8 %collective-permute-done.16 = f32[16,256]{1,0:T(8,128)S(1)} collective-permute-done((f32[16,256]{1,0:T(8,128)S(1)}, f32[16,256]{1,0:T(8,128)S(1)}, u32[]{:S(2)}, u32[]{:S(2)}) %collective-permute-start.16) | collective-permute-done | bytes 16416 | tf_op jit(solution)/shard_map/ppermute | solution.py:439
  85.6 0.0 collective-permute-done.15
  85.6 6.3 %final.1 = (f32[80,16384]{1,0:T(8,128)}, f32[80,80]{1,0:T(8,128)}) custom-call(f32[16,256]{1,0:T(8,128)S(1)} %add_add_fusion.gram_in, bf16[32,16384]{1,0:T(8,128)(2,1)S(1)} %get-tuple-element.47.refs_5_.refs_6_.refs_0_, bf16[32,16384]{1,0:T(8,128)(2,1)S(1)} %get-tuple-element.54.refs_6_.refs_7_.refs_1_, ...), custom_call_target="tpu_custom_call" | custom-call | tf_op jit(solution)/shard_map/final/pallas_call | solution.py:452
  (4 shorter events, 0.0 us)
Async XLA Ops:
  1.3 14.5 %copy-start = (f32[16384,16]{0,1:T(8,128)S(1)}, f32[16384,16]{0,1:T(8,128)}, u32[]{:S(2)}) copy-start(f32[16384,16]{0,1:T(8,128)} %param.5) | copy-start | bytes 3145732
  6.9 8.9 %collective-permute-start.1 = (bf16[64,16,128]{2,1,0:T(8,128)(2,1)S(1)}, bf16[64,16,128]{2,1,0:T(8,128)(2,1)S(1)}, u32[]{:S(2)}, u32[]{:S(2)}) collective-permute-start(bf16[64,16,128]{2,1,0:T(8,128)(2,1)S(1)} %get-tuple-element.40), channel_id=1, source_target_pairs={{0,1},{1,0},{2,3},{3,2},{4,5},{5,4},{6,7},{7,6},{8,9},{9,8},{10,11... | collective-permute-start | bytes 786440 | tf_op jit(solution)/shard_map/ppermute | solution.py:394
  7.0 12.9 %collective-permute-start = (bf16[64,16,128]{2,1,0:T(8,128)(2,1)S(1)}, bf16[64,16,128]{2,1,0:T(8,128)(2,1)S(1)}, u32[]{:S(2)}, u32[]{:S(2)}) collective-permute-start(bf16[64,16,128]{2,1,0:T(8,128)(2,1)S(1)} %get-tuple-element.38), channel_id=1, source_target_pairs={{0,127},{1,2},{2,1},{3,4},{4,3},{5,6},{6,5},{7,8},{8,7},{9,10},{10... | collective-permute-start | bytes 786440 | tf_op jit(solution)/shard_map/ppermute | solution.py:395
  21.0 7.4 %collective-permute-start.3 = (bf16[64,16,128]{2,1,0:T(8,128)(2,1)S(1)}, bf16[64,16,128]{2,1,0:T(8,128)(2,1)S(1)}, u32[]{:S(2)}, u32[]{:S(2)}) collective-permute-start(bf16[64,16,128]{2,1,0:T(8,128)(2,1)S(1)} %get-tuple-element.45), channel_id=1, source_target_pairs={{0,1},{1,0},{2,3},{3,2},{4,5},{5,4},{6,7},{7,6},{8,9},{9,8},{10,11... | collective-permute-start | bytes 786440 | tf_op jit(solution)/shard_map/ppermute | solution.py:394
  21.1 11.3 %collective-permute-start.2 = (bf16[64,16,128]{2,1,0:T(8,128)(2,1)S(1)}, bf16[64,16,128]{2,1,0:T(8,128)(2,1)S(1)}, u32[]{:S(2)}, u32[]{:S(2)}) collective-permute-start(bf16[64,16,128]{2,1,0:T(8,128)(2,1)S(1)} %get-tuple-element.43), channel_id=1, source_target_pairs={{0,127},{1,2},{2,1},{3,4},{4,3},{5,6},{6,5},{7,8},{8,7},{9,10},{10... | collective-permute-start | bytes 786440 | tf_op jit(solution)/shard_map/ppermute | solution.py:395
  33.6 7.3 %collective-permute-start.5 = (bf16[64,16,128]{2,1,0:T(8,128)(2,1)S(1)}, bf16[64,16,128]{2,1,0:T(8,128)(2,1)S(1)}, u32[]{:S(2)}, u32[]{:S(2)}) collective-permute-start(bf16[64,16,128]{2,1,0:T(8,128)(2,1)S(1)} %get-tuple-element.52), channel_id=1, source_target_pairs={{0,1},{1,0},{2,3},{3,2},{4,5},{5,4},{6,7},{7,6},{8,9},{9,8},{10,11... | collective-permute-start | bytes 786440 | tf_op jit(solution)/shard_map/ppermute | solution.py:394
  33.7 11.3 %collective-permute-start.4 = (bf16[64,16,128]{2,1,0:T(8,128)(2,1)S(1)}, bf16[64,16,128]{2,1,0:T(8,128)(2,1)S(1)}, u32[]{:S(2)}, u32[]{:S(2)}) collective-permute-start(bf16[64,16,128]{2,1,0:T(8,128)(2,1)S(1)} %get-tuple-element.50), channel_id=1, source_target_pairs={{0,127},{1,2},{2,1},{3,4},{4,3},{5,6},{6,5},{7,8},{8,7},{9,10},{10... | collective-permute-start | bytes 786440 | tf_op jit(solution)/shard_map/ppermute | solution.py:395
  46.2 7.3 %collective-permute-start.7 = (bf16[64,16,128]{2,1,0:T(8,128)(2,1)S(1)}, bf16[64,16,128]{2,1,0:T(8,128)(2,1)S(1)}, u32[]{:S(2)}, u32[]{:S(2)}) collective-permute-start(bf16[64,16,128]{2,1,0:T(8,128)(2,1)S(1)} %get-tuple-element.59), channel_id=1, source_target_pairs={{0,1},{1,0},{2,3},{3,2},{4,5},{5,4},{6,7},{7,6},{8,9},{9,8},{10,11... | collective-permute-start | bytes 786440 | tf_op jit(solution)/shard_map/ppermute | solution.py:394
  46.3 11.5 %collective-permute-start.6 = (bf16[64,16,128]{2,1,0:T(8,128)(2,1)S(1)}, bf16[64,16,128]{2,1,0:T(8,128)(2,1)S(1)}, u32[]{:S(2)}, u32[]{:S(2)}) collective-permute-start(bf16[64,16,128]{2,1,0:T(8,128)(2,1)S(1)} %get-tuple-element.57), channel_id=1, source_target_pairs={{0,127},{1,2},{2,1},{3,4},{4,3},{5,6},{6,5},{7,8},{8,7},{9,10},{10... | collective-permute-start | bytes 786440 | tf_op jit(solution)/shard_map/ppermute | solution.py:395
  60.3 1.4 %collective-permute-start.8 = (f32[16,256]{1,0:T(8,128)S(1)}, f32[16,256]{1,0:T(8,128)S(1)}, u32[]{:S(2)}, u32[]{:S(2)}) collective-permute-start(f32[16,256]{1,0:T(8,128)S(1)} %get-tuple-element.66), channel_id=1, source_target_pairs={{0,1},{1,0},{2,3},{3,2},{4,5},{5,4},{6,7},{7,6},{8,9},{9,8},{10,11... | collective-permute-start | bytes 49160 | tf_op jit(solution)/shard_map/ppermute | solution.py:439
  61.7 3.7 %collective-permute-start.11 = (f32[16,256]{1,0:T(8,128)S(1)}, f32[16,256]{1,0:T(8,128)S(1)}, u32[]{:S(2)}, u32[]{:S(2)}) collective-permute-start(f32[16,256]{1,0:T(8,128)S(1)} %add.30), channel_id=1, source_target_pairs={{0,6},{1,7},{2,0},{3,1},{4,2},{5,3},{6,4},{7,5},{8,14},{9,15},{10,... | collective-permute-start | bytes 49160 | tf_op jit(solution)/shard_map/ppermute | solution.py:439
  61.7 5.3 %collective-permute-start.10 = (f32[16,256]{1,0:T(8,128)S(1)}, f32[16,256]{1,0:T(8,128)S(1)}, u32[]{:S(2)}, u32[]{:S(2)}) collective-permute-start(f32[16,256]{1,0:T(8,128)S(1)} %add.30), channel_id=1, source_target_pairs={{0,4},{1,5},{2,6},{3,7},{4,0},{5,1},{6,2},{7,3},{8,12},{9,13},{10,... | collective-permute-start | bytes 49160 | tf_op jit(solution)/shard_map/ppermute | solution.py:439
  61.8 6.3 %collective-permute-start.9 = (f32[16,256]{1,0:T(8,128)S(1)}, f32[16,256]{1,0:T(8,128)S(1)}, u32[]{:S(2)}, u32[]{:S(2)}) collective-permute-start(f32[16,256]{1,0:T(8,128)S(1)} %add.30), channel_id=1, source_target_pairs={{0,2},{1,3},{2,4},{3,5},{4,6},{5,7},{6,0},{7,1},{8,10},{9,11},{10,... | collective-permute-start | bytes 49160 | tf_op jit(solution)/shard_map/ppermute | solution.py:439
  68.2 3.7 %collective-permute-start.14 = (f32[16,256]{1,0:T(8,128)S(1)}, f32[16,256]{1,0:T(8,128)S(1)}, u32[]{:S(2)}, u32[]{:S(2)}) collective-permute-start(f32[16,256]{1,0:T(8,128)S(1)} %add_add_fusion.2), channel_id=1, source_target_pairs={{0,24},{1,25},{2,26},{3,27},{4,28},{5,29},{6,30},{7,31},{8,0},{9,1... | collective-permute-start | bytes 49160 | tf_op jit(solution)/shard_map/ppermute | solution.py:439
  68.2 5.5 %collective-permute-start.13 = (f32[16,256]{1,0:T(8,128)S(1)}, f32[16,256]{1,0:T(8,128)S(1)}, u32[]{:S(2)}, u32[]{:S(2)}) collective-permute-start(f32[16,256]{1,0:T(8,128)S(1)} %add_add_fusion.2), channel_id=1, source_target_pairs={{0,16},{1,17},{2,18},{3,19},{4,20},{5,21},{6,22},{7,23},{8,24},{9,... | collective-permute-start | bytes 49160 | tf_op jit(solution)/shard_map/ppermute | solution.py:439
  68.3 6.3 %collective-permute-start.12 = (f32[16,256]{1,0:T(8,128)S(1)}, f32[16,256]{1,0:T(8,128)S(1)}, u32[]{:S(2)}, u32[]{:S(2)}) collective-permute-start(f32[16,256]{1,0:T(8,128)S(1)} %add_add_fusion.2), channel_id=1, source_target_pairs={{0,8},{1,9},{2,10},{3,11},{4,12},{5,13},{6,14},{7,15},{8,16},{9,17... | collective-permute-start | bytes 49160 | tf_op jit(solution)/shard_map/ppermute | solution.py:439
  74.6 7.2 %collective-permute-start.17 = (f32[16,256]{1,0:T(8,128)S(1)}, f32[16,256]{1,0:T(8,128)S(1)}, u32[]{:S(2)}, u32[]{:S(2)}) collective-permute-start(f32[16,256]{1,0:T(8,128)S(1)} %add_add_fusion.1), channel_id=1, source_target_pairs={{0,96},{1,97},{2,98},{3,99},{4,100},{5,101},{6,102},{7,103},{8,104... | collective-permute-start | bytes 49160 | tf_op jit(solution)/shard_map/ppermute | solution.py:439
  80.3 5.2 %collective-permute-start.16 = (f32[16,256]{1,0:T(8,128)S(1)}, f32[16,256]{1,0:T(8,128)S(1)}, u32[]{:S(2)}, u32[]{:S(2)}) collective-permute-start(f32[16,256]{1,0:T(8,128)S(1)} %add_add_fusion.1), channel_id=1, source_target_pairs={{0,64},{1,65},{2,66},{3,67},{4,68},{5,69},{6,70},{7,71},{8,72},{9,... | collective-permute-start | bytes 49160 | tf_op jit(solution)/shard_map/ppermute | solution.py:439
  80.3 5.2 %collective-permute-start.15 = (f32[16,256]{1,0:T(8,128)S(1)}, f32[16,256]{1,0:T(8,128)S(1)}, u32[]{:S(2)}, u32[]{:S(2)}) collective-permute-start(f32[16,256]{1,0:T(8,128)S(1)} %add_add_fusion.1), channel_id=1, source_target_pairs={{0,32},{1,33},{2,34},{3,35},{4,36},{5,37},{6,38},{7,39},{8,40},{9,... | collective-permute-start | bytes 49160 | tf_op jit(solution)/shard_map/ppermute | solution.py:439
